TPU v7x, 512 devices: a whole 4x4x16 slice. The times are simulated.
512 devices in a mesh: batch: 32 (over y, x, core), feat: 16 (over z).
Axes of the slice: x: 4, y: 4, z: 16, core: 2. Of those that a mesh axis runs over, the one named last changes fastest.
Arguments:
- embeds: bfloat16 [2048, 2, 8192], P('batch'), may hold values from -64 to 64
- weight: bfloat16 [8192, 8192], P('batch', 'feat'), may hold values from -0.0625 to 0.0625
Outputs:
- loss_value: float32 [], replicated
- grad_weight: float32 [8192, 8192], P('batch', 'feat')
All inputs are finite; a program needn't handle non-finite values.
Results may differ from a plain program's by a relative error of at most 0.00485.
Values may be sent and summed in bfloat16 or wider, within the bound.
No kernel may reach another device: no remote copies, remote signals or barrier semaphores. Data moves between devices by JAX's collectives and lax.ppermute only.
A program may use at most 64 MiB of HBM per device.

v0:
```python
import jax
import jax.numpy as jnp
from jax import lax
from jax.sharding import PartitionSpec as P

D_OUT = 8192


off_weight = 0.0051
loss_scale = 8.0
epsilon = 1e-05


def split_product(gram, view):
    high = gram.astype(jnp.bfloat16)
    low = (gram - high.astype(jnp.float32)).astype(jnp.bfloat16)
    return jnp.dot(high, view, preferred_element_type=jnp.float32) + jnp.dot(
        low, view, preferred_element_type=jnp.float32
    )


def body(embeds, weight):
    n_batch = lax.axis_size("batch")
    n_feat = lax.axis_size("feat")
    local_rows = embeds.shape[0]
    n_rows = local_rows * n_batch
    width_out = weight.shape[1]
    flattened = embeds.reshape(local_rows * 2, embeds.shape[2])
    exchanged = lax.all_to_all(flattened, "batch", split_axis=1, concat_axis=0, tiled=True)
    projected = jnp.dot(
        flattened,
        lax.all_gather(weight, "batch", axis=0, tiled=True),
        preferred_element_type=jnp.float32,
    )
    projected = projected.reshape(local_rows, 2, width_out)
    row_mean = lax.psum(jnp.sum(projected, axis=0), "batch") / n_rows
    centered = projected - row_mean
    variance = lax.psum(jnp.sum(centered * centered, axis=0), "batch") / n_rows
    spread = jnp.sqrt(variance + epsilon)
    standard = centered / spread
    normed = standard.astype(jnp.bfloat16)
    normed_all = lax.all_gather(normed, "batch", axis=0, tiled=True)
    partial_gram = jnp.einsum(
        "rvf,svf->vrs", normed, normed_all, preferred_element_type=jnp.float32
    )
    gram_both = lax.psum(partial_gram.astype(jnp.bfloat16), "feat").astype(jnp.float32)
    float_a = normed[:, 0].astype(jnp.float32)
    float_b = normed[:, 1].astype(jnp.float32)
    diagonal = lax.psum(jnp.sum(float_a * float_b, axis=0), "batch") / n_rows
    off_local = jnp.sum(gram_both[0] * gram_both[1]) / (n_rows * n_rows)
    diag_local = jnp.sum((1.0 - diagonal) ** 2 - off_weight * diagonal * diagonal)
    loss_value = (
        lax.psum(off_weight * off_local / n_feat + diag_local / n_batch, ("batch", "feat")) / D_OUT
    )
    weight_diag = 2.0 * ((1.0 - off_weight) * diagonal - 1.0)
    scale_off = 2.0 * off_weight / (n_rows * n_rows)
    grad_a = loss_scale * (
        scale_off * split_product(gram_both[1], normed_all[:, 0]) + weight_diag * float_b / n_rows
    )
    grad_b = loss_scale * (
        scale_off * split_product(gram_both[0], normed_all[:, 1]) + weight_diag * float_a / n_rows
    )
    grad_normed = jnp.stack([grad_a, grad_b], axis=1)
    grad_total, cross_total = lax.psum(
        (jnp.sum(grad_normed, axis=0), jnp.sum(grad_normed * standard, axis=0)), "batch"
    )
    grad_mean = grad_total / n_rows
    grad_cross = cross_total / n_rows
    grad_proj = ((grad_normed - grad_mean - standard * grad_cross) / spread).astype(jnp.bfloat16)
    grad_flat = grad_proj.reshape(local_rows * 2, width_out)
    grad_weight = lax.dot_general(
        exchanged,
        lax.all_gather(grad_flat, "batch", axis=0, tiled=True),
        (((0,), (0,)), ((), ())),
        preferred_element_type=jnp.float32,
    )
    return (loss_value, grad_weight)


def solution(mesh):
    return jax.shard_map(
        body,
        mesh=mesh,
        in_specs=(P("batch", None, None), P("batch", "feat")),
        out_specs=(P(), P("batch", "feat")),
        check_vma=False,
    )
```

profile of v0, /device:TPU:1, one launch (start us, length us, event | category | flops | bytes accessed | tf_op | source)
XLA Modules:
  0.0 634.7 jit_solution(1861705395341440390)
XLA Ops:
  7.2 0.0 all-gather.4.cloned.1.call-start
  7.2 0.7 all-gather.4.cloned.1.call-update
  7.9 0.0 all-gather.6.cloned.1.call-start
  7.9 77.2 %all-gather.4.cloned.1.call-done = bf16[8192,512]{1,0:T(8,128)(2,1)} async-done(((bf16[256,512]{1,0:T(8,128)(2,1)}), bf16[8192,512]{1,0:T(8,128)(2,1)}) %all-gather.4.cloned.1.call-update) | async-done | bytes 8388624 | tf_op jit(solution)/shard_map/all_gather | solution.py:32
  85.1 5.9 fusion.28
  91.0 62.3 %psum.49 = f32[2,512]{1,0:T(2,128)S(1)} all-reduce(f32[2,512]{1,0:T(2,128)S(1)} %get-tuple-element.16), channel_id=1, replica_groups=mesh['batch'=32,'feat'=16] {'batch'}, use_global_device_ids=true, to_apply=%region_1.0 | all-reduce | flops 1024 | bytes 8192 | tf_op jit(solution)/shard_map/psum | solution.py:36
  153.3 0.1 multiply_reduce_fusion.2
  153.4 65.5 %psum.50 = f32[2,512]{1,0:T(2,128)S(1)} all-reduce(f32[2,512]{1,0:T(2,128)S(1)} %multiply_reduce_fusion.2), channel_id=1, replica_groups=mesh['batch'=32,'feat'=16] {'batch'}, use_global_device_ids=true, to_apply=%region_3.0 | all-reduce | flops 1024 | bytes 8192 | tf_op jit(solution)/shard_map/psum | solution.py:38
  218.9 0.7 fusion.27
  219.6 0.0 copy-start.2
  219.6 0.0 all-gather.6.cloned.1.call-update
  219.6 0.0 all-reduce.3.cloned.1.call-start
  219.7 58.4 %all-gather.6.cloned.1.call-done = bf16[2048,2,512]{2,0,1:T(8,128)(2,1)} async-done(((bf16[64,2,512]{2,0,1:T(8,128)(2,1)}), bf16[2048,2,512]{2,0,1:T(8,128)(2,1)}) %all-gather.6.cloned.1.call-update) | async-done | bytes 4194320 | tf_op jit(solution)/shard_map/all_gather | solution.py:42
  278.0 4.4 convolution_convert_fusion
  282.5 0.0 all-reduce.3.cloned.1.call-update
  282.5 0.0 all-gather.8.cloned.1.call-start
  282.5 0.0 copy-done.2
  282.6 62.3 %psum.52 = f32[512]{0:T(512)S(1)} all-reduce(f32[512]{0:T(512)S(1)} %fusion.25), channel_id=1, replica_groups=mesh['batch'=32,'feat'=16] {'batch'}, use_global_device_ids=true, to_apply=%region_7.0 | all-reduce | flops 512 | bytes 4096 | tf_op jit(solution)/shard_map/psum | solution.py:49
  344.9 0.6 add_multiply_fusion
  345.5 63.5 %all-reduce.3.cloned.1.call-done = bf16[2,64,2048]{2,1,0:T(8,128)(2,1)} async-done(((bf16[2,64,2048]{2,1,0:T(8,128)(2,1)}), bf16[2,64,2048]{2,1,0:T(8,128)(2,1)}) %all-reduce.3.cloned.1.call-update) | async-done | bytes 524304 | tf_op jit(solution)/shard_map/psum | solution.py:46
  409.0 0.0 copy-start
  409.0 1.3 convert_element_type.60
  410.3 2.2 fusion.5
  412.4 0.0 copy-done
  412.5 0.5 fusion.3
  412.9 0.0 copy-start.1
  412.9 0.5 fusion.11
  413.4 0.0 copy-start.3
  413.4 0.5 fusion.16
  413.9 0.2 copy-done.3
  414.1 0.0 copy-start.4
  414.1 0.1 fusion.23
  414.2 0.5 copy-done.4
  414.7 73.1 %all-reduce = (f32[2,512]{1,0:T(2,128)S(1)}, f32[2,512]{1,0:T(2,128)S(1)}) all-reduce(f32[2,512]{1,0:T(2,128)S(1)} %get-tuple-element.11, f32[2,512]{1,0:T(2,128)S(1)} %get-tuple-element.10), channel_id=1, replica_groups=mesh['batch'=32,'feat'=16] {'batch'}, use_global_device_ids=true, to_apply=%region_13.0 | all-reduce | flops 2048 | bytes 16384 | tf_op jit(solution)/shard_map/psum | solution.py:64
  487.9 1.0 divide_convert_fusion
  488.9 0.1 copy.14
  489.1 0.7 reshape.29
  489.8 0.0 all-gather.8.cloned.1.call-update
  489.8 0.0 copy-done.1
  489.8 2.7 all_to_all.14
  492.5 4.1 copy.15
  496.6 4.3 all-to-all-start
  501.6 0.7 multiply_reduce_fusion
  503.0 118.8 %psum.53 = f32[]{:T(128)} all-reduce(f32[]{:T(128)S(6)} %add.38), channel_id=1, replica_groups=mesh['batch'=32,'feat'=16] {'batch','feat'}, use_global_device_ids=true, to_apply=%region_9.0 | all-reduce | flops 1 | bytes 8 | tf_op jit(solution)/shard_map/psum | solution.py:53
  622.5 0.0 all-to-all-done
  622.5 0.0 all-gather.8.cloned.1.call-done
  622.5 3.5 convolution_bitcast_fusion
  626.0 1.0 copy.16
  (4 shorter events, 0.1 us)
Async XLA Ops:
  7.2 77.9 %all-gather.4.cloned.1.call-start = ((), (), s32[]{:S(2)}) async-start(), calls=%async_computation.1 | async-start | bytes 8650752 | tf_op jit(solution)/shard_map/all_gather | solution.py:32
  7.9 270.1 %all-gather.6.cloned.1.call-start = ((), (), s32[]{:S(2)}) async-start(), calls=%async_computation.2 | async-start | bytes 4325376 | tf_op jit(solution)/shard_map/all_gather | solution.py:42
  219.6 62.9 %copy-start.2 = (bf16[64,2,512]{2,0,1:T(8,128)(2,1)S(1)}, bf16[64,2,512]{2,0,1:T(8,128)(2,1)}, u32[]{:S(2)}) copy-start(bf16[64,2,512]{2,0,1:T(8,128)(2,1)} %fusion.27) | copy-start | bytes 393220
  219.6 189.3 %all-reduce.3.cloned.1.call-start = ((), (), s32[]{:S(2)}) async-start(), calls=%async_computation.3 | async-start | bytes 1048576 | tf_op jit(solution)/shard_map/psum | solution.py:46
  282.5 340.0 %all-gather.8.cloned.1.call-start = ((), (), s32[]{:S(2)}) async-start(), calls=%async_computation.4 | async-start | bytes 4325376 | tf_op jit(solution)/shard_map/all_gather | solution.py:73
  409.0 3.5 copy-start
  412.9 76.9 %copy-start.1 = (bf16[64,2,8192]{2,1,0:T(2,128)(2,1)S(1)}, bf16[64,2,8192]{2,1,0:T(2,128)(2,1)}, u32[]{:S(2)}) copy-start(bf16[64,2,8192]{2,1,0:T(2,128)(2,1)} %param.2) | copy-start | bytes 6291460
  413.4 0.7 copy-start.3
  414.1 0.6 copy-start.4
  496.6 125.9 %all-to-all-start = ((bf16[128,32,256]{2,0,1:T(8,128)(2,1)}), bf16[128,32,256]{2,0,1:T(8,128)(2,1)S(1)}, u32[]{:S(2)}, u32[]{:S(2)}) async-start(bf16[128,32,256]{2,0,1:T(8,128)(2,1)} %copy.15), calls=%async_computation | async-start | bytes 4194304 | tf_op jit(solution)/shard_map/all_to_all | solution.py:29
Sparse Core Ops, SparseCore 0:
  11.1 73.9 all-gather.3
  219.7 58.2 all-gather.5
  282.6 126.3 all-reduce.2
  489.9 67.2 all-gather.7
where the time goes:
time: 635 us
  blocking collectives  382 us (60%)
  waiting for transfers between devices  200 us (31%)
  matrix products  17.5 us (3%)
  between operations  17 us (3%)
  local copies, waits for them, and re-layouts  9.33 us (1%)
    psum x1, blocking collectives, body(): lax.psum(off_weight * off_local / n_feat + diag_local / n_batch, ('batch'...  119 us
    all_gather x1, waiting for transfers between devices, body(): lax.all_gather(weight, 'batch', axis=0, tiled=True)  77.2 us
    psum x1, blocking collectives, body(): lax.psum((jnp.sum(grad_normed, axis=0), jnp.sum(grad_normed * standard, a...  73.1 us
    psum x1, blocking collectives, body(): variance = lax.psum(jnp.sum(centered * centered, axis=0), 'batch') / n_rows  65.5 us
    psum x1, waiting for transfers between devices, body(): lax.psum(partial_gram.astype(jnp.bfloat16), 'feat').astype(jnp.float32)  63.5 us
    psum x1, blocking collectives, body(): diagonal = lax.psum(jnp.sum(float_a * float_b, axis=0), 'batch') / n_rows  62.3 us
    psum x1, blocking collectives, body(): row_mean = lax.psum(jnp.sum(projected, axis=0), 'batch') / n_rows  62.3 us
    all_gather x1, waiting for transfers between devices, body(): normed_all = lax.all_gather(normed, 'batch', axis=0, tiled=True)  58.4 us
  transfers between devices with their start and end apart: 5, of which 3 were waited for; matrix products, arithmetic and copies ran while one was open for 1% of the time, Pallas kernels for 0%

commit v1 on v0

v1 whole, which is shorter than its diff:
```python
import jax
import jax.numpy as jnp
from jax import lax
from jax.sharding import Mesh, PartitionSpec as P

D_OUT = 8192

off_weight = 0.0051
loss_scale = 8.0
epsilon = 1e-05

F32 = jnp.float32
BF16 = jnp.bfloat16
PLANE = ("y", "x")
PAD = 16


def exchange(blocks, axes):
    return lax.all_to_all(blocks, axes, split_axis=0, concat_axis=0, tiled=True)


def gather(block, axes):
    n = lax.axis_size(axes)
    blocks = jnp.broadcast_to(block[None], (n,) + block.shape)
    return exchange(blocks, axes)


def pieces(value):
    high = lax.reduce_precision(value, 8, 7)
    rest = value - high
    middle = lax.reduce_precision(rest, 8, 7)
    low = rest - middle
    return [high.astype(BF16), middle.astype(BF16), low.astype(BF16)]


def pad_rows(rows, width):
    rows = [r.reshape(1, width) for r in rows]
    return jnp.concatenate(rows + [jnp.zeros((PAD - len(rows), width), BF16)], axis=0)


def scalar_rows(values, width):
    rows = []
    for value in values:
        rows += [jnp.broadcast_to(p, (width,)) for p in pieces(value)]
    return pad_rows(rows, width)


def split_product(gram_t, view):
    high = gram_t.astype(BF16)
    low = (gram_t - high.astype(F32)).astype(BF16)
    rows = (((0,), (0,)), ((), ()))
    return lax.dot_general(high, view, rows, preferred_element_type=F32) + lax.dot_general(
        low, view, rows, preferred_element_type=F32
    )


def body(embeds, weight):
    n_chip = lax.axis_size(PLANE)
    n_feat = lax.axis_size("feat")
    n_batch = 2 * n_chip
    local_rows, _, d_in = embeds.shape
    chip_rows = 2 * local_rows
    n_rows = local_rows * n_batch
    depth, width_out = weight.shape
    half = width_out // 2
    core = lax.axis_index("core")
    chip = lax.axis_index(PLANE)
    first = core == 0

    def in_core_order(own, other, axis):
        return jnp.concatenate([jnp.where(first, own, other), jnp.where(first, other, own)], axis=axis)

    def swap_core(a):
        return lax.ppermute(a, "core", [(0, 1), (1, 0)])

    with jax.named_scope("weight_gather"):
        halves = weight.reshape(depth, 2, half).transpose(1, 0, 2)
        chip_weight = exchange(halves, "core").reshape(2 * depth, half)
        all_weight = gather(chip_weight, PLANE).reshape(d_in, half)
    with jax.named_scope("embeds_order"):
        by_view = embeds.transpose(1, 0, 2).reshape(2 * local_rows, d_in)
        other_view = swap_core(by_view)
    with jax.named_scope("embeds_exchange"):
        exchanged = lax.all_to_all(
            by_view.reshape(2 * local_rows, n_batch, depth).transpose(1, 0, 2),
            ("y", "x", "core"), split_axis=0, concat_axis=0, tiled=True,
        ).reshape(n_batch, 2, local_rows, depth)
        embeds_a = exchanged[:, 0].reshape(n_rows, depth)
        embeds_b = exchanged[:, 1].reshape(n_rows, depth)

    with jax.named_scope("project"):
        own = jnp.dot(by_view, all_weight, preferred_element_type=F32)
        other = jnp.dot(other_view, all_weight, preferred_element_type=F32)
        own = jnp.concatenate([own[:local_rows], own[local_rows:]], axis=1)
        other = jnp.concatenate([other[:local_rows], other[local_rows:]], axis=1)
        projected = in_core_order(own, other, 0)
    with jax.named_scope("project_gather"):
        chip_mean = jnp.sum(projected, axis=0) / chip_rows
        block = jnp.concatenate(
            [(projected - chip_mean).astype(BF16), pad_rows(pieces(chip_mean), width_out)], axis=0
        )
        got = gather(block, PLANE)
    with jax.named_scope("standardize"):
        chip_means = jnp.sum(got[:, chip_rows : chip_rows + 3].astype(F32), axis=1)
        row_mean = jnp.sum(chip_means, axis=0) / n_chip
        centered = got[:, :chip_rows].astype(F32) + (chip_means - row_mean)[:, None, :]
        centered = centered.reshape(n_rows, width_out)
        variance = jnp.sum(centered * centered, axis=0) / n_rows
        spread = jnp.sqrt(variance + epsilon)
        standard = centered / spread
        normed = standard.astype(BF16)
        view_a, view_b = normed[:, :half], normed[:, half:]
        float_a, float_b = view_a.astype(F32), view_b.astype(F32)
        diagonal = jnp.sum(float_a * float_b, axis=0) / n_rows
        diag_local = jnp.sum((1.0 - diagonal) ** 2 - off_weight * diagonal * diagonal)

    with jax.named_scope("gram"):
        mine = lax.dynamic_slice_in_dim(normed, chip * chip_rows, chip_rows, axis=0)
        contract = (((1,), (1,)), ((), ()))
        part_a = lax.dot_general(view_a, mine[:, :half], contract, preferred_element_type=F32)
        part_b = lax.dot_general(view_b, mine[:, half:], contract, preferred_element_type=F32)
        parts = jnp.stack([part_a.astype(BF16), part_b.astype(BF16)])
    with jax.named_scope("gram_core"):
        parts = jnp.sum(exchange(parts, "core").astype(F32), axis=0)
    with jax.named_scope("gram_reduce"):
        parts = parts.astype(BF16).reshape(n_feat, n_rows // n_feat, chip_rows)
        extra = jnp.broadcast_to(scalar_rows([diag_local], chip_rows)[None], (n_feat, PAD, chip_rows))
        got_z = exchange(jnp.concatenate([parts, extra], axis=1), "feat")
        summed = jnp.sum(got_z.astype(F32), axis=0)
        gram_block = summed[: n_rows // n_feat].astype(BF16)
        diag_core = jnp.sum(summed[n_rows // n_feat : n_rows // n_feat + 3, 0])
    with jax.named_scope("gram_gather"):
        gram_t = gather(gram_block, "feat").reshape(n_rows, chip_rows)
        other_t, other_diag = swap_core(gram_t), swap_core(diag_core)
        gram_a = jnp.where(first, gram_t, other_t).astype(F32)
        gram_b = jnp.where(first, other_t, gram_t).astype(F32)
        diag_total = diag_core + other_diag
    with jax.named_scope("back"):
        off_local = jnp.sum(gram_a * gram_b)
        back_a = split_product(gram_b, view_a)
        back_b = split_product(gram_a, view_b)
        back = jnp.concatenate([back_a, back_b], axis=1).astype(BF16)
        block = jnp.concatenate([back, scalar_rows([off_local], width_out)], axis=0)
    with jax.named_scope("back_gather"):
        got = gather(block, PLANE)
    with jax.named_scope("grad"):
        off_total = jnp.sum(got[:, chip_rows : chip_rows + 3, 0].astype(F32)) / (n_rows * n_rows)
        loss_value = (off_weight * off_total + diag_total) / D_OUT
        back = got[:, :chip_rows].astype(F32).reshape(n_rows, width_out)
        weight_diag = 2.0 * ((1.0 - off_weight) * diagonal - 1.0)
        weight_diag = jnp.concatenate([weight_diag, weight_diag])
        scale_off = 2.0 * off_weight / (n_rows * n_rows)
        crossed = jnp.concatenate([float_b, float_a], axis=1)
        grad_normed = loss_scale * (scale_off * back + weight_diag * crossed / n_rows)
        grad_mean = jnp.sum(grad_normed, axis=0) / n_rows
        grad_cross = jnp.sum(grad_normed * standard, axis=0) / n_rows
        grad_proj = ((grad_normed - grad_mean - standard * grad_cross) / spread).astype(BF16)
    with jax.named_scope("grad_swap"):
        other_proj = swap_core(grad_proj)
    with jax.named_scope("weight_grad"):
        def half_grad(g):
            rows = (((0,), (0,)), ((), ()))
            return lax.dot_general(embeds_a, g[:, :half], rows, preferred_element_type=F32) + lax.dot_general(
                embeds_b, g[:, half:], rows, preferred_element_type=F32
            )
        grad_weight = in_core_order(half_grad(grad_proj), half_grad(other_proj), 1)
    return (loss_value, grad_weight)


def solution(mesh):
    n_batch, n_feat = mesh.devices.shape
    grid = Mesh(mesh.devices.reshape(4, n_batch // 8, 2, n_feat), ("y", "x", "core", "feat"))
    batch = ("y", "x", "core")
    return jax.shard_map(
        body,
        mesh=grid,
        in_specs=(P(batch, None, None), P(batch, "feat")),
        out_specs=(P(), P(batch, "feat")),
        check_vma=False,
    )
```

time: 635 us -> 338 us (0.53)
  blocking collectives: 382 us -> 81.9 us
  waiting for transfers between devices: 200 us -> 143 us
  starting transfers between devices: 4.51 us -> 43.5 us
  other arithmetic: 4.56 us -> 17.2 us
  local copies, waits for them, and re-layouts: 9.33 us -> 21.4 us
    psum x5 -> x0, blocking collectives: 382 us -> none  [the longest x1 119 us: body(): lax.psum(off_weight * off_local / n_feat + diag_local / n_batch, ('batch'...]
    all_to_all x1 -> x5, waiting for transfers between devices: 0.01 us -> 140 us  [the longest x4 122 us: exchange(): return lax.all_to_all(blocks, axes, split_axis=0, concat_axis=0, tiled=True)]
    all_gather x3 -> x0, waiting for transfers between devices: 136 us -> none  [the longest x1 77.2 us: body(): lax.all_gather(weight, 'batch', axis=0, tiled=True)]
    all_to_all x0 -> x3, blocking collectives: none -> 81.9 us  [exchange(): return lax.all_to_all(blocks, axes, split_axis=0, concat_axis=0, tiled=True)]
    psum x1 -> x0, waiting for transfers between devices: 63.5 us -> none  [body(): lax.psum(partial_gram.astype(jnp.bfloat16), 'feat').astype(jnp.float32)]
    all_to_all x1 -> x5, starting transfers between devices: 4.35 us -> 25.6 us  [the longest x4 20.1 us: exchange(): return lax.all_to_all(blocks, axes, split_axis=0, concat_axis=0, tiled=True)]
    ppermute x0 -> x4, starting transfers between devices: none -> 17.9 us  [swap_core(): return lax.ppermute(a, 'core', [(0, 1), (1, 0)])]
    unnamed x11 -> x17, local copies, waits for them, and re-layouts: 1.72 us -> 10 us
  transfers between devices with their start and end apart: 5 -> 9, of which waited for: 3 -> 7; matrix products, arithmetic and copies ran while one was open for 1% -> 8% of each run, Pallas kernels for 0% -> 0%
where the time goes in v1:
time: 338 us; the launch traced here: 336 us
  waiting for transfers between devices  143 us (42%)
  blocking collectives  81.9 us (24%)
  starting transfers between devices  43.5 us (13%)
  local copies, waits for them, and re-layouts  21.4 us (6%)
  other arithmetic  17.2 us (5%)
  matrix products  15.5 us (5%)
  between operations  14 us (4%)
    all_to_all x4, waiting for transfers between devices, exchange(): return lax.all_to_all(blocks, axes, split_axis=0, concat_axis=0, tiled=True)  122 us
    all_to_all x3, blocking collectives, exchange(): return lax.all_to_all(blocks, axes, split_axis=0, concat_axis=0, tiled=True)  81.9 us
    all_to_all x4, starting transfers between devices, exchange(): return lax.all_to_all(blocks, axes, split_axis=0, concat_axis=0, tiled=True)  20.1 us
    ppermute x4, starting transfers between devices, swap_core(): return lax.ppermute(a, 'core', [(0, 1), (1, 0)])  17.9 us
    all_to_all x1, waiting for transfers between devices, body(): lax.all_to_all(by_view.reshape(2 * local_rows, n_batch, depth).transpose(...  17.8 us
    unnamed x17, local copies, waits for them, and re-layouts  10 us
  transfers between devices with their start and end apart: 9, of which 7 were waited for; matrix products, arithmetic and copies ran while one was open for 8% of the time, Pallas kernels for 0%

profile of v1, /device:TPU:1, one launch (start us, length us, event | category | flops | bytes accessed | tf_op | source)
XLA Modules:
  0.0 336.3 jit_solution(18332631262562773361)
XLA Ops:
  0.6 1.1 copy.59
  1.7 10.5 %all_to_all.40 = bf16[2,256,256]{1,2,0:T(8,128)(2,1)S(1)} all-to-all(bf16[2,256,256]{1,2,0:T(8,128)(2,1)S(1)} %bitcast.69), channel_id=1, replica_groups=mesh['y'=4,'x'=4,'core'=2,'feat'=16] {'core'}, dimensions={0} | all-to-all | bytes 524288 | tf_op jit(solution)/shard_map/weight_gather/all_to_all | solution.py:19
  12.3 2.4 broadcast_in_dim.15
  14.7 4.5 %all-to-all-start.1 = ((bf16[16,512,256]{2,1,0:T(8,128)(2,1)}), bf16[16,512,256]{2,1,0:T(8,128)(2,1)}, u32[]{:S(2)}, u32[]{:S(2)}) async-start(bf16[16,512,256]{2,1,0:T(8,128)(2,1)} %broadcast_in_dim.15), calls=%async_computation.1 | async-start | bytes 8388608 | tf_op jit(solution)/shard_map/weight_gather/all_to_all | solution.py:19
  19.2 2.8 copy.58
  22.0 2.3 collective-permute-start
  24.3 58.2 %all-to-all-done.1 = bf16[16,512,256]{2,1,0:T(8,128)(2,1)} async-done(((bf16[16,512,256]{2,1,0:T(8,128)(2,1)}), bf16[16,512,256]{2,1,0:T(8,128)(2,1)}, u32[]{:S(2)}, u32[]{:S(2)}) %all-to-all-start.1) | async-done | bytes 4194336 | tf_op jit(solution)/shard_map/weight_gather/all_to_all | solution.py:19
  82.5 2.9 fusion.51
  85.4 3.5 %fusion.52 = f32[128,256]{1,0:T(8,128)S(1)} fusion(bf16[128,8192]{1,0:T(8,128)(2,1)} %collective-permute-done, bf16[8192,256]{1,0:T(8,128)(2,1)} %bitcast.5), kind=kOutput, calls=%fused_computation.96 | convolution fusion | flops 536870912 | bytes 6422528 | tf_op jit(solution)/shard_map/project/dot_general | solution.py:93
  89.3 1.6 broadcast_in_dim.16
  90.9 4.7 %all-to-all-start.2 = ((bf16[16,144,512]{2,1,0:T(8,128)(2,1)}), bf16[16,144,512]{2,1,0:T(8,128)(2,1)S(1)}, u32[]{:S(2)}, u32[]{:S(2)}) async-start(bf16[16,144,512]{2,1,0:T(8,128)(2,1)} %broadcast_in_dim.16), calls=%async_computation.2 | async-start | bytes 4718592 | tf_op jit(solution)/shard_map/project_gather/all_to_all | solution.py:19
  95.7 32.9 %all-to-all-done.2 = bf16[16,144,512]{2,1,0:T(8,128)(2,1)S(1)} async-done(((bf16[16,144,512]{2,1,0:T(8,128)(2,1)}), bf16[16,144,512]{2,1,0:T(8,128)(2,1)S(1)}, u32[]{:S(2)}, u32[]{:S(2)}) %all-to-all-start.2) | async-done | bytes 2359328 | tf_op jit(solution)/shard_map/project_gather/all_to_all | solution.py:19
  128.7 0.7 convert_add_fusion
  129.4 0.7 copy-done.5
  130.7 1.3 copy-done
  132.3 0.6 add_multiply_fusion.1
  138.7 1.1 pad_maximum_fusion
  139.8 6.2 %all-to-all-start.3 = ((bf16[2,2048,128]{2,1,0:T(8,128)(2,1)}), bf16[2,2048,128]{2,1,0:T(8,128)(2,1)S(1)}, u32[]{:S(2)}, u32[]{:S(2)}) async-start(bf16[2,2048,128]{2,1,0:T(8,128)(2,1)} %pad_maximum_fusion), calls=%async_computation.3 | async-start | bytes 2097152 | tf_op jit(solution)/shard_map/gram_core/all_to_all | solution.py:19
  146.1 1.7 all-to-all-done.3
  147.8 1.1 reduce_sum.153
  148.9 1.2 pad_maximum_fusion.1
  150.1 44.2 %all_to_all.41 = bf16[16,144,128]{2,1,0:T(8,128)(2,1)S(1)} all-to-all(bf16[16,144,128]{2,1,0:T(8,128)(2,1)S(1)} %pad_maximum_fusion.1), channel_id=1, replica_groups=mesh['y'=4,'x'=4,'core'=2,'feat'=16] {'feat'}, dimensions={0} | all-to-all | bytes 1179648 | tf_op jit(solution)/shard_map/gram_reduce/all_to_all | solution.py:19
  194.5 27.2 %all_to_all.42 = bf16[16,128,128]{2,1,0:T(8,128)(2,1)S(1)} all-to-all(bf16[16,128,128]{2,1,0:T(8,128)(2,1)S(1)} %broadcast_in_dim.19), channel_id=1, replica_groups=mesh['y'=4,'x'=4,'core'=2,'feat'=16] {'feat'}, dimensions={0} | all-to-all | bytes 1048576 | tf_op jit(solution)/shard_map/gram_gather/all_to_all | solution.py:19
  221.7 9.0 %collective-permute-start.1 = (bf16[2048,128]{1,0:T(8,128)(2,1)S(1)}, bf16[2048,128]{1,0:T(8,128)(2,1)S(1)}, u32[]{:S(2)}, u32[]{:S(2)}) collective-permute-start(bf16[2048,128]{1,0:T(8,128)(2,1)S(1)} %bitcast.67), channel_id=1, source_target_pairs={{0,16},{16,0},{1,17},{17,1},{2,18},{18,2},{3,19},{19,3},{4,20},{20... | collective-permute-start | bytes 1572872 | tf_op jit(solution)/shard_map/gram_gather/ppermute | solution.py:74
  230.7 1.5 collective-permute-done.1
  232.3 0.9 fusion.17
  239.8 1.7 broadcast_in_dim.20
  241.5 4.6 %all-to-all-start.6 = ((bf16[16,144,512]{2,1,0:T(8,128)(2,1)}), bf16[16,144,512]{2,1,0:T(8,128)(2,1)}, u32[]{:S(2)}, u32[]{:S(2)}) async-start(bf16[16,144,512]{2,1,0:T(8,128)(2,1)} %broadcast_in_dim.20), calls=%async_computation.6 | async-start | bytes 4718592 | tf_op jit(solution)/shard_map/back_gather/all_to_all | solution.py:19
  246.1 2.2 copy.69
  248.3 2.6 copy.64
  250.9 2.2 slice_convert_fusion
  253.1 29.6 %all-to-all-done.6 = bf16[16,144,512]{2,1,0:T(8,128)(2,1)} async-done(((bf16[16,144,512]{2,1,0:T(8,128)(2,1)}), bf16[16,144,512]{2,1,0:T(8,128)(2,1)}, u32[]{:S(2)}, u32[]{:S(2)}) %all-to-all-start.6) | async-done | bytes 2359328 | tf_op jit(solution)/shard_map/back_gather/all_to_all | solution.py:19
  282.7 5.5 %all-to-all-start.7 = ((bf16[32,128,256]{2,1,0:T(8,128)(2,1)}), bf16[32,128,256]{2,1,0:T(8,128)(2,1)}, u32[]{:S(2)}, u32[]{:S(2)}) async-start(bf16[32,128,256]{2,1,0:T(8,128)(2,1)} %copy.64), calls=%async_computation.7 | async-start | bytes 4194304 | tf_op jit(solution)/shard_map/embeds_exchange/all_to_all | solution.py:84
  288.3 3.8 %fusion.32 = (f32[512]{0:T(512)S(1)}, f32[512]{0:T(512)S(1)}, f32[16,128,512]{2,1,0:T(8,128)S(1)}) fusion(f32[16,128,256]{2,1,0:T(8,128)} %bitcast.60, f32[16,128,256]{2,1,0:T(8,128)S(1)} %bitcast.59, f32[512]{0:T(512)S(1)} %pad_maximum_fusion.6, bf16[16,144,512]{2,1,0:T(8,128)(2,1)} %all-to-all-done.6, f32[512]{0:T(512)S(1)} %add_sqrt_fusion, ...), kind=kLoop, calls=%fused_computation.54 | loop fusion | flops 13630464 | bytes 12623872 | tf_op jit(solution)/shard_map/grad/reduce_sum | solution.py:155
  292.4 0.7 copy-done.4
  293.0 3.1 fusion.9
  296.1 2.3 collective-permute-start.3
  298.5 17.8 %all-to-all-done.7 = bf16[32,128,256]{2,1,0:T(8,128)(2,1)} async-done(((bf16[32,128,256]{2,1,0:T(8,128)(2,1)}), bf16[32,128,256]{2,1,0:T(8,128)(2,1)}, u32[]{:S(2)}, u32[]{:S(2)}) %all-to-all-start.7) | async-done | bytes 2097184 | tf_op jit(solution)/shard_map/embeds_exchange/all_to_all | solution.py:84
  316.3 1.7 fusion.46
  318.6 4.3 %collective-permute-start.2 = (f32[]{:T(128)}, f32[]{:T(128)}, u32[]{:S(2)}, u32[]{:S(2)}) collective-permute-start(f32[]{:T(128)} %slice_reduce_fusion), channel_id=1, source_target_pairs={{0,16},{16,0},{1,17},{17,1},{2,18},{18,2},{3,19},{19,3},{4,20},{20... | collective-permute-start | bytes 20 | tf_op jit(solution)/shard_map/gram_gather/ppermute | solution.py:74
  322.9 1.1 collective-permute-done.2
  325.2 0.8 slice.90
  326.1 0.6 convert_reduce_fusion.3
  327.3 1.7 fusion.22
  329.0 1.7 convolution_add_fusion.1
  330.7 1.7 fusion.18
  332.4 1.7 select_bitcast_fusion.1
  334.2 1.0 copy.65
  (49 shorter events, 5.2 us)
Async XLA Ops:
  14.7 67.8 %all-to-all-start.1 = ((bf16[16,512,256]{2,1,0:T(8,128)(2,1)}), bf16[16,512,256]{2,1,0:T(8,128)(2,1)}, u32[]{:S(2)}, u32[]{:S(2)}) async-start(bf16[16,512,256]{2,1,0:T(8,128)(2,1)} %broadcast_in_dim.15), calls=%async_computation.1 | async-start | bytes 8388608 | tf_op jit(solution)/shard_map/weight_gather/all_to_all | solution.py:19
  22.0 63.4 %copy-start.2 = (bf16[64,2,8192]{2,0,1:T(8,128)(2,1)}, bf16[64,2,8192]{2,0,1:T(8,128)(2,1)S(1)}, u32[]{:S(2)}) copy-start(bf16[64,2,8192]{2,0,1:T(8,128)(2,1)S(1)} %copy.58) | copy-start | bytes 6291460
  22.0 63.4 %collective-permute-start = (bf16[128,8192]{1,0:T(8,128)(2,1)S(1)}, bf16[128,8192]{1,0:T(8,128)(2,1)}, u32[]{:S(2)}, u32[]{:S(2)}) collective-permute-start(bf16[128,8192]{1,0:T(8,128)(2,1)S(1)} %bitcast.56), channel_id=1, source_target_pairs={{0,16},{16,0},{1,17},{17,1},{2,18},{18,2},{3,19},{19,3},{4,20},{20... | collective-permute-start | bytes 6291464 | tf_op jit(solution)/shard_map/embeds_order/ppermute | solution.py:74
  90.9 37.6 %all-to-all-start.2 = ((bf16[16,144,512]{2,1,0:T(8,128)(2,1)}), bf16[16,144,512]{2,1,0:T(8,128)(2,1)S(1)}, u32[]{:S(2)}, u32[]{:S(2)}) async-start(bf16[16,144,512]{2,1,0:T(8,128)(2,1)} %broadcast_in_dim.16), calls=%async_computation.2 | async-start | bytes 4718592 | tf_op jit(solution)/shard_map/project_gather/all_to_all | solution.py:19
  128.6 1.5 copy-start.5
  130.1 1.9 copy-start
  139.8 8.0 %all-to-all-start.3 = ((bf16[2,2048,128]{2,1,0:T(8,128)(2,1)}), bf16[2,2048,128]{2,1,0:T(8,128)(2,1)S(1)}, u32[]{:S(2)}, u32[]{:S(2)}) async-start(bf16[2,2048,128]{2,1,0:T(8,128)(2,1)} %pad_maximum_fusion), calls=%async_computation.3 | async-start | bytes 2097152 | tf_op jit(solution)/shard_map/gram_core/all_to_all | solution.py:19
  221.7 10.5 %collective-permute-start.1 = (bf16[2048,128]{1,0:T(8,128)(2,1)S(1)}, bf16[2048,128]{1,0:T(8,128)(2,1)S(1)}, u32[]{:S(2)}, u32[]{:S(2)}) collective-permute-start(bf16[2048,128]{1,0:T(8,128)(2,1)S(1)} %bitcast.67), channel_id=1, source_target_pairs={{0,16},{16,0},{1,17},{17,1},{2,18},{18,2},{3,19},{19,3},{4,20},{20... | collective-permute-start | bytes 1572872 | tf_op jit(solution)/shard_map/gram_gather/ppermute | solution.py:74
  241.5 41.3 %all-to-all-start.6 = ((bf16[16,144,512]{2,1,0:T(8,128)(2,1)}), bf16[16,144,512]{2,1,0:T(8,128)(2,1)}, u32[]{:S(2)}, u32[]{:S(2)}) async-start(bf16[16,144,512]{2,1,0:T(8,128)(2,1)} %broadcast_in_dim.20), calls=%async_computation.6 | async-start | bytes 4718592 | tf_op jit(solution)/shard_map/back_gather/all_to_all | solution.py:19
  253.1 35.2 %copy-start.3 = (f32[2048,256]{1,0:T(8,128)S(1)}, f32[2048,256]{1,0:T(8,128)}, u32[]{:S(2)}) copy-start(f32[2048,256]{1,0:T(8,128)} %get-tuple-element.36) | copy-start | bytes 6291460
  282.7 33.5 %all-to-all-start.7 = ((bf16[32,128,256]{2,1,0:T(8,128)(2,1)}), bf16[32,128,256]{2,1,0:T(8,128)(2,1)}, u32[]{:S(2)}, u32[]{:S(2)}) async-start(bf16[32,128,256]{2,1,0:T(8,128)(2,1)} %copy.64), calls=%async_computation.7 | async-start | bytes 4194304 | tf_op jit(solution)/shard_map/embeds_exchange/all_to_all | solution.py:84
  288.3 4.1 %copy-start.1 = (f32[16,128,512]{2,1,0:T(8,128)S(1)}, f32[16,128,512]{2,1,0:T(8,128)}, u32[]{:S(2)}) copy-start(f32[16,128,512]{2,1,0:T(8,128)} %copy-done) | copy-start | bytes 12582916
  288.3 4.7 %copy-start.4 = (f32[2048,256]{1,0:T(8,128)S(1)}, f32[2048,256]{1,0:T(8,128)}, u32[]{:S(2)}) copy-start(f32[2048,256]{1,0:T(8,128)} %get-tuple-element.37) | copy-start | bytes 6291460
  296.1 34.6 %collective-permute-start.3 = (bf16[2048,512]{1,0:T(8,128)(2,1)}, bf16[2048,512]{1,0:T(8,128)(2,1)}, u32[]{:S(2)}, u32[]{:S(2)}) collective-permute-start(bf16[2048,512]{1,0:T(8,128)(2,1)} %fusion.9), channel_id=1, source_target_pairs={{0,16},{16,0},{1,17},{17,1},{2,18},{18,2},{3,19},{19,3},{4,20},{20... | collective-permute-start | bytes 6291464 | tf_op jit(solution)/shard_map/grad_swap/ppermute | solution.py:74
  318.6 5.4 %collective-permute-start.2 = (f32[]{:T(128)}, f32[]{:T(128)}, u32[]{:S(2)}, u32[]{:S(2)}) collective-permute-start(f32[]{:T(128)} %slice_reduce_fusion), channel_id=1, source_target_pairs={{0,16},{16,0},{1,17},{17,1},{2,18},{18,2},{3,19},{19,3},{4,20},{20... | collective-permute-start | bytes 20 | tf_op jit(solution)/shard_map/gram_gather/ppermute | solution.py:74

commit v2 on v1

--- a/solution.py
+++ b/solution.py
@@ -38,13 +38,6 @@
     return jnp.concatenate(rows + [jnp.zeros((PAD - len(rows), width), BF16)], axis=0)
 
 
-def scalar_rows(values, width):
-    rows = []
-    for value in values:
-        rows += [jnp.broadcast_to(p, (width,)) for p in pieces(value)]
-    return pad_rows(rows, width)
-
-
 def split_product(gram_t, view):
     high = gram_t.astype(BF16)
     low = (gram_t - high.astype(F32)).astype(BF16)
@@ -73,22 +66,20 @@
     def swap_core(a):
         return lax.ppermute(a, "core", [(0, 1), (1, 0)])
 
+    with jax.named_scope("embeds_order"):
+        by_view = embeds.transpose(1, 0, 2).reshape(2 * local_rows, d_in)
+        share = 2 * local_rows // n_feat
+        z_rows = lax.dynamic_slice_in_dim(by_view, lax.axis_index("feat") * share, share, axis=0)
+        z_rows = z_rows.reshape(share, n_chip, 2 * depth).transpose(1, 0, 2)
     with jax.named_scope("weight_gather"):
         halves = weight.reshape(depth, 2, half).transpose(1, 0, 2)
         chip_weight = exchange(halves, "core").reshape(2 * depth, half)
-        all_weight = gather(chip_weight, PLANE).reshape(d_in, half)
-    with jax.named_scope("embeds_order"):
-        by_view = embeds.transpose(1, 0, 2).reshape(2 * local_rows, d_in)
+        blocks = jnp.broadcast_to(chip_weight[None], (n_chip,) + chip_weight.shape)
+        blocks, by_view, z_rows = lax.optimization_barrier((blocks, by_view, z_rows))
         other_view = swap_core(by_view)
-    with jax.named_scope("embeds_exchange"):
-        exchanged = lax.all_to_all(
-            by_view.reshape(2 * local_rows, n_batch, depth).transpose(1, 0, 2),
-            ("y", "x", "core"), split_axis=0, concat_axis=0, tiled=True,
-        ).reshape(n_batch, 2, local_rows, depth)
-        embeds_a = exchanged[:, 0].reshape(n_rows, depth)
-        embeds_b = exchanged[:, 1].reshape(n_rows, depth)
-
+        all_weight = exchange(blocks, PLANE).reshape(d_in, half)
     with jax.named_scope("project"):
+        all_weight, by_view = lax.optimization_barrier((all_weight, by_view))
         own = jnp.dot(by_view, all_weight, preferred_element_type=F32)
         other = jnp.dot(other_view, all_weight, preferred_element_type=F32)
         own = jnp.concatenate([own[:local_rows], own[local_rows:]], axis=1)
@@ -97,9 +88,24 @@
     with jax.named_scope("project_gather"):
         chip_mean = jnp.sum(projected, axis=0) / chip_rows
         block = jnp.concatenate(
-            [(projected - chip_mean).astype(BF16), pad_rows(pieces(chip_mean), width_out)], axis=0
+            [
+                (projected - chip_mean).astype(BF16),
+                jnp.stack(pieces(chip_mean)),
+                jnp.zeros((PAD - share - 3, width_out), BF16),
+            ],
+            axis=0,
         )
-        got = gather(block, PLANE)
+        blocks = jnp.broadcast_to(block[None], (n_chip,) + block.shape)
+        got = exchange(jnp.concatenate([blocks, z_rows], axis=1), PLANE)
+    with jax.named_scope("embeds_gather"):
+        z_got = got[:, chip_rows + PAD - share :].reshape(n_chip, share, 2, depth)
+        kept = jnp.where(first, z_got[:, :, 0], z_got[:, :, 1])
+        sent = swap_core(jnp.where(first, z_got[:, :, 1], z_got[:, :, 0]))
+        rows = jnp.stack([jnp.where(first, kept, sent), jnp.where(first, sent, kept)], axis=1)
+        exchanged = lax.all_gather(rows, "feat", axis=0, tiled=False)
+        exchanged = exchanged.reshape(2, n_feat // 2, n_batch, share, depth).transpose(0, 2, 1, 3, 4)
+        embeds_a = exchanged[0].reshape(n_rows, depth)
+        embeds_b = exchanged[1].reshape(n_rows, depth)
     with jax.named_scope("standardize"):
         chip_means = jnp.sum(got[:, chip_rows : chip_rows + 3].astype(F32), axis=1)
         row_mean = jnp.sum(chip_means, axis=0) / n_chip
@@ -112,7 +118,8 @@
         view_a, view_b = normed[:, :half], normed[:, half:]
         float_a, float_b = view_a.astype(F32), view_b.astype(F32)
         diagonal = jnp.sum(float_a * float_b, axis=0) / n_rows
-        diag_local = jnp.sum((1.0 - diagonal) ** 2 - off_weight * diagonal * diagonal)
+        diag_terms = (1.0 - diagonal) ** 2 - off_weight * diagonal * diagonal
+        diag_local = diag_terms[:chip_rows] + diag_terms[chip_rows:]
 
     with jax.named_scope("gram"):
         mine = lax.dynamic_slice_in_dim(normed, chip * chip_rows, chip_rows, axis=0)
@@ -120,31 +127,36 @@
         part_a = lax.dot_general(view_a, mine[:, :half], contract, preferred_element_type=F32)
         part_b = lax.dot_general(view_b, mine[:, half:], contract, preferred_element_type=F32)
         parts = jnp.stack([part_a.astype(BF16), part_b.astype(BF16)])
+        extra = pad_rows(pieces(diag_local), chip_rows)
+        parts, extra, diagonal, spread = lax.optimization_barrier((parts, extra, diagonal, spread))
     with jax.named_scope("gram_core"):
         parts = jnp.sum(exchange(parts, "core").astype(F32), axis=0)
     with jax.named_scope("gram_reduce"):
         parts = parts.astype(BF16).reshape(n_feat, n_rows // n_feat, chip_rows)
-        extra = jnp.broadcast_to(scalar_rows([diag_local], chip_rows)[None], (n_feat, PAD, chip_rows))
+        extra = jnp.broadcast_to(extra[None], (n_feat, PAD, chip_rows))
         got_z = exchange(jnp.concatenate([parts, extra], axis=1), "feat")
         summed = jnp.sum(got_z.astype(F32), axis=0)
         gram_block = summed[: n_rows // n_feat].astype(BF16)
-        diag_core = jnp.sum(summed[n_rows // n_feat : n_rows // n_feat + 3, 0])
+        diag_core = jnp.sum(summed[n_rows // n_feat : n_rows // n_feat + 3], axis=0)
+        gram_block, diag_core = lax.optimization_barrier((gram_block, diag_core))
     with jax.named_scope("gram_gather"):
         gram_t = gather(gram_block, "feat").reshape(n_rows, chip_rows)
-        other_t, other_diag = swap_core(gram_t), swap_core(diag_core)
+        other_t = swap_core(gram_t)
         gram_a = jnp.where(first, gram_t, other_t).astype(F32)
         gram_b = jnp.where(first, other_t, gram_t).astype(F32)
-        diag_total = diag_core + other_diag
     with jax.named_scope("back"):
-        off_local = jnp.sum(gram_a * gram_b)
+        off_local = jnp.sum(gram_a * gram_b, axis=0)
         back_a = split_product(gram_b, view_a)
         back_b = split_product(gram_a, view_b)
         back = jnp.concatenate([back_a, back_b], axis=1).astype(BF16)
-        block = jnp.concatenate([back, scalar_rows([off_local], width_out)], axis=0)
+        terms = jnp.concatenate([off_local, jnp.zeros((width_out - chip_rows,), F32)])
+        block = jnp.concatenate([back, pad_rows(pieces(terms), width_out)], axis=0)
+        other_diag = swap_core(diag_core)
     with jax.named_scope("back_gather"):
         got = gather(block, PLANE)
     with jax.named_scope("grad"):
-        off_total = jnp.sum(got[:, chip_rows : chip_rows + 3, 0].astype(F32)) / (n_rows * n_rows)
+        off_total = jnp.sum(got[:, chip_rows : chip_rows + 3, :chip_rows].astype(F32)) / (n_rows * n_rows)
+        diag_total = jnp.sum(diag_core + other_diag)
         loss_value = (off_weight * off_total + diag_total) / D_OUT
         back = got[:, :chip_rows].astype(F32).reshape(n_rows, width_out)
         weight_diag = 2.0 * ((1.0 - off_weight) * diagonal - 1.0)

time: 338 us -> 338 us (level)
  the two profiles are of different devices: /device:TPU:1 before, /device:TPU:8 now
where the time goes in v2:
time: 338 us; the launch traced here: 337 us
  waiting for transfers between devices  152 us (45%)
  blocking collectives  82.7 us (24%)
  starting transfers between devices  36 us (11%)
  other arithmetic  18.1 us (5%)
  local copies, waits for them, and re-layouts  17.7 us (5%)
  between operations  16.9 us (5%)
  matrix products  13.3 us (4%)
    all_to_all x4, waiting for transfers between devices, exchange(): return lax.all_to_all(blocks, axes, split_axis=0, concat_axis=0, tiled=True)  125 us
    all_to_all x3, blocking collectives, exchange(): return lax.all_to_all(blocks, axes, split_axis=0, concat_axis=0, tiled=True)  82.7 us
    all_to_all x4, starting transfers between devices, exchange(): return lax.all_to_all(blocks, axes, split_axis=0, concat_axis=0, tiled=True)  25.5 us
    all_gather x1, waiting for transfers between devices, body(): exchanged = lax.all_gather(rows, 'feat', axis=0, tiled=False)  22.4 us
    ppermute x5, starting transfers between devices, swap_core(): return lax.ppermute(a, 'core', [(0, 1), (1, 0)])  10.4 us
    unnamed x16, local copies, waits for them, and re-layouts  9.76 us
  transfers between devices with their start and end apart: 10, of which 7 were waited for; matrix products, arithmetic and copies ran while one was open for 6% of the time, Pallas kernels for 0%

profile of v2, /device:TPU:8, one launch (start us, length us, event | category | flops | bytes accessed | tf_op | source)
XLA Modules:
  0.0 336.7 jit_solution(16670037325086252948)
XLA Ops:
  7.2 1.8 copy.39
  9.0 3.4 %all-to-all-start = ((bf16[2,256,256]{1,2,0:T(8,128)(2,1)}), bf16[2,256,256]{1,2,0:T(8,128)(2,1)S(1)}, u32[]{:S(2)}, u32[]{:S(2)}) async-start(bf16[2,256,256]{1,2,0:T(8,128)(2,1)} %bitcast.1), calls=%async_computation | async-start | bytes 524288 | tf_op jit(solution)/shard_map/weight_gather/all_to_all | solution.py:19
  12.4 2.8 copy.41
  15.3 2.4 broadcast_in_dim.19
  17.7 10.1 %all-to-all-start.1 = ((bf16[16,512,256]{2,1,0:T(8,128)(2,1)}), bf16[16,512,256]{2,1,0:T(8,128)(2,1)}, u32[]{:S(2)}, u32[]{:S(2)}) async-start(bf16[16,512,256]{2,1,0:T(8,128)(2,1)} %broadcast_in_dim.19), calls=%async_computation.1 | async-start | bytes 8388608 | tf_op jit(solution)/shard_map/weight_gather/all_to_all | solution.py:19
  27.8 2.1 collective-permute-start
  29.9 61.7 %all-to-all-done.1 = bf16[16,512,256]{2,1,0:T(8,128)(2,1)} async-done(((bf16[16,512,256]{2,1,0:T(8,128)(2,1)}), bf16[16,512,256]{2,1,0:T(8,128)(2,1)}, u32[]{:S(2)}, u32[]{:S(2)}) %all-to-all-start.1) | async-done | bytes 4194336 | tf_op jit(solution)/shard_map/weight_gather/all_to_all | solution.py:19
  91.7 2.9 fusion.56
  94.6 3.5 %fusion.57 = f32[128,256]{1,0:T(8,128)S(1)} fusion(bf16[128,8192]{1,0:T(8,128)(2,1)} %collective-permute-done, bf16[8192,256]{1,0:T(8,128)(2,1)} %bitcast.8), kind=kOutput, calls=%fused_computation.122 | convolution fusion | flops 536870912 | bytes 6422528 | tf_op jit(solution)/shard_map/project/dot_general | solution.py:84
  98.5 1.6 pad_maximum_fusion
  100.1 6.0 %all-to-all-start.2 = ((bf16[16,144,512]{2,1,0:T(8,128)(2,1)}), bf16[16,144,512]{2,1,0:T(8,128)(2,1)S(1)}, u32[]{:S(2)}, u32[]{:S(2)}) async-start(bf16[16,144,512]{2,1,0:T(8,128)(2,1)} %pad_maximum_fusion), calls=%async_computation.2 | async-start | bytes 4718592 | tf_op jit(solution)/shard_map/project_gather/all_to_all | solution.py:19
  106.2 33.6 %all-to-all-done.2 = bf16[16,144,512]{2,1,0:T(8,128)(2,1)S(1)} async-done(((bf16[16,144,512]{2,1,0:T(8,128)(2,1)}), bf16[16,144,512]{2,1,0:T(8,128)(2,1)S(1)}, u32[]{:S(2)}, u32[]{:S(2)}) %all-to-all-start.2) | async-done | bytes 2359328 | tf_op jit(solution)/shard_map/project_gather/all_to_all | solution.py:19
  139.8 0.7 convert_add_fusion
  140.6 0.6 copy-done.2
  141.2 0.6 fusion.12
  141.8 1.3 copy-done
  144.5 4.6 %all_to_all.35 = bf16[2,2048,128]{2,1,0:T(8,128)(2,1)S(1)} all-to-all(bf16[2,2048,128]{2,1,0:T(8,128)(2,1)S(1)} %pad_maximum_fusion.1), channel_id=1, replica_groups=mesh['y'=4,'x'=4,'core'=2,'feat'=16] {'core'}, dimensions={0} | all-to-all | bytes 2097152 | tf_op jit(solution)/shard_map/gram_core/all_to_all | solution.py:19
  149.1 1.1 reduce_sum.154
  150.2 1.1 pad_maximum_fusion.2
  151.3 46.0 %all_to_all.36 = bf16[16,144,128]{2,1,0:T(8,128)(2,1)S(1)} all-to-all(bf16[16,144,128]{2,1,0:T(8,128)(2,1)S(1)} %pad_maximum_fusion.2), channel_id=1, replica_groups=mesh['y'=4,'x'=4,'core'=2,'feat'=16] {'feat'}, dimensions={0} | all-to-all | bytes 1179648 | tf_op jit(solution)/shard_map/gram_reduce/all_to_all | solution.py:19
  197.5 32.1 %all_to_all.37 = bf16[16,128,128]{2,1,0:T(8,128)(2,1)S(1)} all-to-all(bf16[16,128,128]{2,1,0:T(8,128)(2,1)S(1)} %broadcast_in_dim.24), channel_id=1, replica_groups=mesh['y'=4,'x'=4,'core'=2,'feat'=16] {'feat'}, dimensions={0} | all-to-all | bytes 1048576 | tf_op jit(solution)/shard_map/gram_gather/all_to_all | solution.py:19
  229.7 1.9 collective-permute-start.1
  231.6 1.9 collective-permute-done.1
  235.5 1.7 broadcast_in_dim.26
  237.2 6.0 %all-to-all-start.6 = ((bf16[16,144,512]{2,1,0:T(8,128)(2,1)}), bf16[16,144,512]{2,1,0:T(8,128)(2,1)}, u32[]{:S(2)}, u32[]{:S(2)}) async-start(bf16[16,144,512]{2,1,0:T(8,128)(2,1)} %broadcast_in_dim.26), calls=%async_computation.6 | async-start | bytes 4718592 | tf_op jit(solution)/shard_map/back_gather/all_to_all | solution.py:19
  243.6 2.1 collective-permute-start.3
  245.8 1.0 collective-permute-done.3
  246.8 0.7 pad_maximum_fusion.7
  247.5 2.2 slice_convert_fusion
  249.7 29.7 %all-to-all-done.6 = bf16[16,144,512]{2,1,0:T(8,128)(2,1)} async-done(((bf16[16,144,512]{2,1,0:T(8,128)(2,1)}), bf16[16,144,512]{2,1,0:T(8,128)(2,1)}, u32[]{:S(2)}, u32[]{:S(2)}) %all-to-all-start.6) | async-done | bytes 2359328 | tf_op jit(solution)/shard_map/back_gather/all_to_all | solution.py:19
  279.4 4.4 %fusion.32 = (f32[512]{0:T(512)S(1)}, f32[512]{0:T(512)S(1)}, f32[16,128,512]{2,1,0:T(8,128)S(1)}) fusion(f32[16,128,256]{2,1,0:T(8,128)} %bitcast.70, f32[16,128,256]{2,1,0:T(8,128)} %bitcast.69, f32[512]{0:T(512)S(1)} %pad_maximum_fusion.8, bf16[16,144,512]{2,1,0:T(8,128)(2,1)} %all-to-all-done.6, f32[512]{0:T(512)S(1)} %add_sqrt_fusion, ...), kind=kLoop, calls=%fused_computation.55 | loop fusion | flops 13630464 | bytes 12623872 | tf_op jit(solution)/shard_map/grad/reduce_sum | solution.py:167
  284.1 0.7 copy-done.3
  284.8 0.6 copy-done.4
  285.4 2.1 fusion.9
  287.5 1.9 collective-permute-start.4
  289.5 2.4 collective-permute-start.2
  291.9 1.7 collective-permute-done.2
  293.6 0.6 add_reduce_fusion
  294.2 22.4 %all-gather.3.cloned.1.call-done = bf16[256,2,8,256]{3,2,0,1:T(8,128)(2,1)} async-done(((bf16[16,2,8,256]{3,2,0,1:T(8,128)(2,1)}), bf16[256,2,8,256]{3,2,0,1:T(8,128)(2,1)}) %all-gather.3.cloned.1.call-update) | async-done | bytes 2097168 | tf_op jit(solution)/shard_map/embeds_gather/all_gather | solution.py:105
  316.5 1.7 copy.42
  318.5 1.1 copy.44
  319.7 1.4 convert_reduce_fusion.3
  322.4 0.5 fusion.22
  322.9 0.7 copy-done.5
  323.6 0.5 convolution_add_fusion.1
  324.1 1.7 fusion.18
  325.9 1.8 broadcast_select_fusion.5
  327.7 1.0 copy.45
  (66 shorter events, 5.3 us)
Async XLA Ops:
  9.0 6.2 %all-to-all-start = ((bf16[2,256,256]{1,2,0:T(8,128)(2,1)}), bf16[2,256,256]{1,2,0:T(8,128)(2,1)S(1)}, u32[]{:S(2)}, u32[]{:S(2)}) async-start(bf16[2,256,256]{1,2,0:T(8,128)(2,1)} %bitcast.1), calls=%async_computation | async-start | bytes 524288 | tf_op jit(solution)/shard_map/weight_gather/all_to_all | solution.py:19
  17.7 73.9 %all-to-all-start.1 = ((bf16[16,512,256]{2,1,0:T(8,128)(2,1)}), bf16[16,512,256]{2,1,0:T(8,128)(2,1)}, u32[]{:S(2)}, u32[]{:S(2)}) async-start(bf16[16,512,256]{2,1,0:T(8,128)(2,1)} %broadcast_in_dim.19), calls=%async_computation.1 | async-start | bytes 8388608 | tf_op jit(solution)/shard_map/weight_gather/all_to_all | solution.py:19
  27.8 66.8 %collective-permute-start = (bf16[128,8192]{1,0:T(8,128)(2,1)S(1)}, bf16[128,8192]{1,0:T(8,128)(2,1)}, u32[]{:S(2)}, u32[]{:S(2)}) collective-permute-start(bf16[128,8192]{1,0:T(8,128)(2,1)S(1)} %bitcast.72), channel_id=1, source_target_pairs={{0,16},{16,0},{1,17},{17,1},{2,18},{18,2},{3,19},{19,3},{4,20},{20... | collective-permute-start | bytes 6291464 | tf_op jit(solution)/shard_map/weight_gather/ppermute | solution.py:67
  100.1 39.6 %all-to-all-start.2 = ((bf16[16,144,512]{2,1,0:T(8,128)(2,1)}), bf16[16,144,512]{2,1,0:T(8,128)(2,1)S(1)}, u32[]{:S(2)}, u32[]{:S(2)}) async-start(bf16[16,144,512]{2,1,0:T(8,128)(2,1)} %pad_maximum_fusion), calls=%async_computation.2 | async-start | bytes 4718592 | tf_op jit(solution)/shard_map/project_gather/all_to_all | solution.py:19
  139.7 1.5 copy-start.2
  141.2 1.9 copy-start
  229.7 3.8 %collective-permute-start.1 = (bf16[2048,128]{1,0:T(8,128)(2,1)S(1)}, bf16[2048,128]{1,0:T(8,128)(2,1)S(1)}, u32[]{:S(2)}, u32[]{:S(2)}) collective-permute-start(bf16[2048,128]{1,0:T(8,128)(2,1)S(1)} %bitcast.76), channel_id=1, source_target_pairs={{0,16},{16,0},{1,17},{17,1},{2,18},{18,2},{3,19},{19,3},{4,20},{20... | collective-permute-start | bytes 1572872 | tf_op jit(solution)/shard_map/gram_gather/ppermute | solution.py:67
  237.2 6.1 %slice-start = ((bf16[16,144,512]{2,1,0:T(8,128)(2,1)}), bf16[16,8,512]{2,1,0:T(8,128)(2,1)S(1)}, s32[]{:S(2)}) async-start(bf16[16,144,512]{2,1,0:T(8,128)(2,1)} %copy-done.2), calls=%async_computation.8 | async-start | bytes 262144 | tf_op jit(solution)/shard_map/embeds_gather/slice | solution.py:101
  237.2 42.2 %all-to-all-start.6 = ((bf16[16,144,512]{2,1,0:T(8,128)(2,1)}), bf16[16,144,512]{2,1,0:T(8,128)(2,1)}, u32[]{:S(2)}, u32[]{:S(2)}) async-start(bf16[16,144,512]{2,1,0:T(8,128)(2,1)} %broadcast_in_dim.26), calls=%async_computation.6 | async-start | bytes 4718592 | tf_op jit(solution)/shard_map/back_gather/all_to_all | solution.py:19
  243.2 73.3 %all-gather.3.cloned.1.call-start = ((), (), s32[]{:S(2)}) async-start(), calls=%async_computation.7 | async-start | bytes 2228224 | tf_op jit(solution)/shard_map/embeds_gather/all_gather | solution.py:105
  243.6 3.1 collective-permute-start.3
  279.4 4.7 %copy-start.1 = (f32[16,128,512]{2,1,0:T(8,128)S(1)}, f32[16,128,512]{2,1,0:T(8,128)}, u32[]{:S(2)}) copy-start(f32[16,128,512]{2,1,0:T(8,128)} %copy-done) | copy-start | bytes 12582916
  279.4 5.4 %copy-start.3 = (f32[2048,256]{1,0:T(8,128)S(1)}, f32[2048,256]{1,0:T(8,128)}, u32[]{:S(2)}) copy-start(f32[2048,256]{1,0:T(8,128)} %get-tuple-element.54) | copy-start | bytes 6291460
  279.4 6.0 %copy-start.4 = (f32[2048,256]{1,0:T(8,128)S(1)}, f32[2048,256]{1,0:T(8,128)}, u32[]{:S(2)}) copy-start(f32[2048,256]{1,0:T(8,128)} %get-tuple-element.55) | copy-start | bytes 6291460
  287.5 36.6 %collective-permute-start.4 = (bf16[2048,512]{1,0:T(8,128)(2,1)S(1)}, bf16[2048,512]{1,0:T(8,128)(2,1)}, u32[]{:S(2)}, u32[]{:S(2)}) collective-permute-start(bf16[2048,512]{1,0:T(8,128)(2,1)S(1)} %fusion.9), channel_id=1, source_target_pairs={{0,16},{16,0},{1,17},{17,1},{2,18},{18,2},{3,19},{19,3},{4,20},{20... | collective-permute-start | bytes 6291464 | tf_op jit(solution)/shard_map/grad_swap/ppermute | solution.py:67
  289.5 4.1 %collective-permute-start.2 = (f32[128]{0:T(128)S(1)}, f32[128]{0:T(128)S(1)}, u32[]{:S(2)}, u32[]{:S(2)}) collective-permute-start(f32[128]{0:T(128)S(1)} %slice_reduce_fusion), channel_id=1, source_target_pairs={{0,16},{16,0},{1,17},{17,1},{2,18},{18,2},{3,19},{19,3},{4,20},{20... | collective-permute-start | bytes 1544 | tf_op jit(solution)/shard_map/back/ppermute | solution.py:67
  322.4 1.2 copy-start.5
Sparse Core Ops, SparseCore 0:
  247.6 68.8 all-gather.2

commit v3 on v2

--- a/solution.py
+++ b/solution.py
@@ -12,6 +12,7 @@
 F32 = jnp.float32
 BF16 = jnp.bfloat16
 PLANE = ("y", "x")
+BATCH = ("y", "x", "core")
 PAD = 16
 
 
@@ -66,46 +67,45 @@
     def swap_core(a):
         return lax.ppermute(a, "core", [(0, 1), (1, 0)])
 
+    with jax.named_scope("embeds_exchange"):
+        share = 2 * local_rows // n_feat
+        per_view = n_feat // 2
+        z = lax.axis_index("feat")
+        z_rows = lax.dynamic_slice(embeds, ((z % per_view) * share, z // per_view, 0), (share, 1, d_in))
+        z_rows = z_rows.reshape(share, n_batch, depth).transpose(1, 0, 2)
+        z_rows = exchange(z_rows, BATCH)
+        weight, z_rows = lax.optimization_barrier((weight, z_rows))
+        embeds_k = lax.all_gather(z_rows, "feat", axis=0, tiled=False)
+        embeds_k = embeds_k.reshape(2, per_view, n_batch, share, depth).transpose(0, 2, 1, 3, 4)
+        embeds_k = embeds_k.reshape(2, n_rows, depth)
+    with jax.named_scope("weight_gather"):
+        core_weight = gather(weight, PLANE).reshape(n_chip * depth, width_out)
     with jax.named_scope("embeds_order"):
-        by_view = embeds.transpose(1, 0, 2).reshape(2 * local_rows, d_in)
-        share = 2 * local_rows // n_feat
-        z_rows = lax.dynamic_slice_in_dim(by_view, lax.axis_index("feat") * share, share, axis=0)
-        z_rows = z_rows.reshape(share, n_chip, 2 * depth).transpose(1, 0, 2)
-    with jax.named_scope("weight_gather"):
-        halves = weight.reshape(depth, 2, half).transpose(1, 0, 2)
-        chip_weight = exchange(halves, "core").reshape(2 * depth, half)
-        blocks = jnp.broadcast_to(chip_weight[None], (n_chip,) + chip_weight.shape)
-        blocks, by_view, z_rows = lax.optimization_barrier((blocks, by_view, z_rows))
-        other_view = swap_core(by_view)
-        all_weight = exchange(blocks, PLANE).reshape(d_in, half)
+        by_core = embeds.reshape(local_rows, 2, n_chip, 2, depth).transpose(3, 1, 0, 2, 4)
+        by_core = by_core.reshape(2, 2 * local_rows, n_chip * depth)
+        own_rows = lax.dynamic_index_in_dim(by_core, core, 0, keepdims=False)
+        other_rows = swap_core(lax.dynamic_index_in_dim(by_core, 1 - core, 0, keepdims=False))
     with jax.named_scope("project"):
-        all_weight, by_view = lax.optimization_barrier((all_weight, by_view))
-        own = jnp.dot(by_view, all_weight, preferred_element_type=F32)
-        other = jnp.dot(other_view, all_weight, preferred_element_type=F32)
-        own = jnp.concatenate([own[:local_rows], own[local_rows:]], axis=1)
-        other = jnp.concatenate([other[:local_rows], other[local_rows:]], axis=1)
-        projected = in_core_order(own, other, 0)
+        own = jnp.dot(own_rows, core_weight, preferred_element_type=F32)
+        other = jnp.dot(other_rows, core_weight, preferred_element_type=F32)
+        def by_half(p):
+            a, b = p[:local_rows], p[local_rows:]
+            low = jnp.concatenate([a[:, :half], b[:, :half]], axis=1)
+            high = jnp.concatenate([a[:, half:], b[:, half:]], axis=1)
+            return jnp.where(first, low, high), jnp.where(first, high, low)
+
+        own_kept, own_sent = by_half(own)
+        other_kept, other_sent = by_half(other)
+        got_other, got_own = jnp.split(swap_core(jnp.concatenate([own_sent, other_sent])), 2)
+        projected = in_core_order(own_kept + got_own, other_kept + got_other, 0)
     with jax.named_scope("project_gather"):
         chip_mean = jnp.sum(projected, axis=0) / chip_rows
         block = jnp.concatenate(
-            [
-                (projected - chip_mean).astype(BF16),
-                jnp.stack(pieces(chip_mean)),
-                jnp.zeros((PAD - share - 3, width_out), BF16),
-            ],
-            axis=0,
+            [(projected - chip_mean).astype(BF16), pad_rows(pieces(chip_mean), width_out)], axis=0
         )
-        blocks = jnp.broadcast_to(block[None], (n_chip,) + block.shape)
-        got = exchange(jnp.concatenate([blocks, z_rows], axis=1), PLANE)
-    with jax.named_scope("embeds_gather"):
-        z_got = got[:, chip_rows + PAD - share :].reshape(n_chip, share, 2, depth)
-        kept = jnp.where(first, z_got[:, :, 0], z_got[:, :, 1])
-        sent = swap_core(jnp.where(first, z_got[:, :, 1], z_got[:, :, 0]))
-        rows = jnp.stack([jnp.where(first, kept, sent), jnp.where(first, sent, kept)], axis=1)
-        exchanged = lax.all_gather(rows, "feat", axis=0, tiled=False)
-        exchanged = exchanged.reshape(2, n_feat // 2, n_batch, share, depth).transpose(0, 2, 1, 3, 4)
-        embeds_a = exchanged[0].reshape(n_rows, depth)
-        embeds_b = exchanged[1].reshape(n_rows, depth)
+        block, embeds_k = lax.optimization_barrier((block, embeds_k))
+        got = gather(block, PLANE)
+        embeds_a, embeds_b = embeds_k[0], embeds_k[1]
     with jax.named_scope("standardize"):
         chip_means = jnp.sum(got[:, chip_rows : chip_rows + 3].astype(F32), axis=1)
         row_mean = jnp.sum(chip_means, axis=0) / n_chip
@@ -182,11 +182,10 @@
 def solution(mesh):
     n_batch, n_feat = mesh.devices.shape
     grid = Mesh(mesh.devices.reshape(4, n_batch // 8, 2, n_feat), ("y", "x", "core", "feat"))
-    batch = ("y", "x", "core")
     return jax.shard_map(
         body,
         mesh=grid,
-        in_specs=(P(batch, None, None), P(batch, "feat")),
-        out_specs=(P(), P(batch, "feat")),
+        in_specs=(P(BATCH, None, None), P(BATCH, "feat")),
+        out_specs=(P(), P(BATCH, "feat")),
         check_vma=False,
     )

time: 338 us -> 327 us (0.967)
  the two profiles are of different devices: /device:TPU:8 before, /device:TPU:1 now
where the time goes in v3:
time: 327 us; the launch traced here: 326 us
  waiting for transfers between devices  115 us (35%)
  blocking collectives  105 us (32%)
  starting transfers between devices  33.5 us (10%)
  local copies, waits for them, and re-layouts  25.6 us (8%)
  between operations  17 us (5%)
  other arithmetic  14.7 us (4%)
  matrix products  14.4 us (4%)
    all_to_all x3, waiting for transfers between devices, exchange(): return lax.all_to_all(blocks, axes, split_axis=0, concat_axis=0, tiled=True)  111 us
    all_to_all x4, blocking collectives, exchange(): return lax.all_to_all(blocks, axes, split_axis=0, concat_axis=0, tiled=True)  105 us
    ppermute x5, starting transfers between devices, swap_core(): return lax.ppermute(a, 'core', [(0, 1), (1, 0)])  19.5 us
    all_to_all x3, starting transfers between devices, exchange(): return lax.all_to_all(blocks, axes, split_axis=0, concat_axis=0, tiled=True)  13.9 us
    broadcast_in_dim x4, local copies, waits for them, and re-layouts, gather(): blocks = jnp.broadcast_to(block[None], (n,) + block.shape)  6.74 us
  transfers between devices with their start and end apart: 9, of which 5 were waited for; matrix products, arithmetic and copies ran while one was open for 7% of the time, Pallas kernels for 0%

profile of v3, /device:TPU:1, one launch (start us, length us, event | category | flops | bytes accessed | tf_op | source)
XLA Modules:
  0.0 325.6 jit_solution(12376174837081906650)
XLA Ops:
  7.2 1.7 dynamic-slice_reduce_fusion
  9.0 17.9 %all_to_all.35 = bf16[32,8,256]{2,1,0:T(8,128)(2,1)} all-to-all(bf16[32,8,256]{2,1,0:T(8,128)(2,1)S(1)} %copy.45), channel_id=1, replica_groups=mesh['y'=4,'x'=4,'core'=2,'feat'=16] {'y','x','core'}, dimensions={0} | all-to-all | bytes 262144 | tf_op jit(solution)/shard_map/embeds_exchange/all_to_all | solution.py:20
  27.0 3.3 %broadcast_in_dim.12 = bf16[16,256,512]{2,1,0:T(8,128)(2,1)} broadcast(bf16[256,512]{1,0:T(8,128)(2,1)} %param.3), dimensions={1,2} | broadcast | bytes 4456448 | tf_op jit(solution)/shard_map/weight_gather/broadcast_in_dim | solution.py:25
  30.3 4.5 %all-to-all-start.1 = ((bf16[16,256,512]{2,1,0:T(8,128)(2,1)}), bf16[16,256,512]{2,1,0:T(8,128)(2,1)}, u32[]{:S(2)}, u32[]{:S(2)}) async-start(bf16[16,256,512]{2,1,0:T(8,128)(2,1)} %broadcast_in_dim.12), calls=%async_computation.1 | async-start | bytes 8388608 | tf_op jit(solution)/shard_map/weight_gather/all_to_all | solution.py:20
  34.9 0.7 all-gather.3.cloned.1.call-update
  35.6 3.3 %reshape.165 = bf16[64,2,16,2,256]{4,3,2,1,0:T(2,128)(2,1)S(1)} reshape(bf16[64,2,8192]{2,1,0:T(2,128)(2,1)} %param.2) | data formatting | bytes 4194304 | tf_op jit(solution)/shard_map/embeds_order/reshape | solution.py:84
  38.9 1.6 copy.58
  40.6 2.9 reshape.166
  43.6 2.3 collective-permute-start
  45.9 52.1 %all-to-all-done.1 = bf16[16,256,512]{2,1,0:T(8,128)(2,1)} async-done(((bf16[16,256,512]{2,1,0:T(8,128)(2,1)}), bf16[16,256,512]{2,1,0:T(8,128)(2,1)}, u32[]{:S(2)}, u32[]{:S(2)}) %all-to-all-start.1) | async-done | bytes 4194336 | tf_op jit(solution)/shard_map/weight_gather/all_to_all | solution.py:20
  98.0 2.9 fusion.28
  100.9 3.2 fusion.63
  104.3 3.2 collective-permute-start.1
  107.4 3.3 %copy.46 = bf16[2,32,8,8,256]{4,3,2,1,0:T(8,128)(2,1)} copy(bf16[2,32,8,8,256]{4,3,1,2,0:T(8,128)(2,1)} %bitcast.75) | data formatting | bytes 4194304 | tf_op jit(solution)/shard_map/embeds_exchange/transpose | solution.py:79
  111.1 1.6 broadcast_in_dim.13
  112.7 4.7 %all-to-all-start.2 = ((bf16[16,144,512]{2,1,0:T(8,128)(2,1)}), bf16[16,144,512]{2,1,0:T(8,128)(2,1)S(1)}, u32[]{:S(2)}, u32[]{:S(2)}) async-start(bf16[16,144,512]{2,1,0:T(8,128)(2,1)} %broadcast_in_dim.13), calls=%async_computation.2 | async-start | bytes 4718592 | tf_op jit(solution)/shard_map/project_gather/all_to_all | solution.py:20
  117.6 24.5 %all-to-all-done.2 = bf16[16,144,512]{2,1,0:T(8,128)(2,1)S(1)} async-done(((bf16[16,144,512]{2,1,0:T(8,128)(2,1)}), bf16[16,144,512]{2,1,0:T(8,128)(2,1)S(1)}, u32[]{:S(2)}, u32[]{:S(2)}) %all-to-all-start.2) | async-done | bytes 2359328 | tf_op jit(solution)/shard_map/project_gather/all_to_all | solution.py:20
  142.2 0.7 convert_add_fusion
  142.9 0.7 copy-done.4
  143.6 0.6 fusion.12
  144.2 1.3 copy-done
  145.9 0.4 fusion.10
  146.9 14.6 %all_to_all.36 = bf16[2,2048,128]{2,1,0:T(8,128)(2,1)S(1)} all-to-all(bf16[2,2048,128]{2,1,0:T(8,128)(2,1)S(1)} %pad_maximum_fusion), channel_id=1, replica_groups=mesh['y'=4,'x'=4,'core'=2,'feat'=16] {'core'}, dimensions={0} | all-to-all | bytes 2097152 | tf_op jit(solution)/shard_map/gram_core/all_to_all | solution.py:20
  161.5 1.1 reduce_sum.154
  162.6 1.1 pad_maximum_fusion.1
  163.7 45.8 %all_to_all.37 = bf16[16,144,128]{2,1,0:T(8,128)(2,1)S(1)} all-to-all(bf16[16,144,128]{2,1,0:T(8,128)(2,1)S(1)} %pad_maximum_fusion.1), channel_id=1, replica_groups=mesh['y'=4,'x'=4,'core'=2,'feat'=16] {'feat'}, dimensions={0} | all-to-all | bytes 1179648 | tf_op jit(solution)/shard_map/gram_reduce/all_to_all | solution.py:20
  209.7 27.2 %all_to_all.38 = bf16[16,128,128]{2,1,0:T(8,128)(2,1)S(1)} all-to-all(bf16[16,128,128]{2,1,0:T(8,128)(2,1)S(1)} %broadcast_in_dim.16), channel_id=1, replica_groups=mesh['y'=4,'x'=4,'core'=2,'feat'=16] {'feat'}, dimensions={0} | all-to-all | bytes 1048576 | tf_op jit(solution)/shard_map/gram_gather/all_to_all | solution.py:20
  236.9 9.0 %collective-permute-start.2 = (bf16[2048,128]{1,0:T(8,128)(2,1)S(1)}, bf16[2048,128]{1,0:T(8,128)(2,1)S(1)}, u32[]{:S(2)}, u32[]{:S(2)}) collective-permute-start(bf16[2048,128]{1,0:T(8,128)(2,1)S(1)} %bitcast.77), channel_id=1, source_target_pairs={{0,16},{16,0},{1,17},{17,1},{2,18},{18,2},{3,19},{19,3},{4,20},{20... | collective-permute-start | bytes 1572872 | tf_op jit(solution)/shard_map/gram_gather/ppermute | solution.py:68
  246.0 1.5 collective-permute-done.2
  249.5 1.7 broadcast_in_dim.17
  251.2 4.6 %all-to-all-start.6 = ((bf16[16,144,512]{2,1,0:T(8,128)(2,1)}), bf16[16,144,512]{2,1,0:T(8,128)(2,1)}, u32[]{:S(2)}, u32[]{:S(2)}) async-start(bf16[16,144,512]{2,1,0:T(8,128)(2,1)} %broadcast_in_dim.17), calls=%async_computation.6 | async-start | bytes 4718592 | tf_op jit(solution)/shard_map/back_gather/all_to_all | solution.py:20
  255.8 2.2 slice_convert_fusion
  258.0 34.4 %all-to-all-done.6 = bf16[16,144,512]{2,1,0:T(8,128)(2,1)} async-done(((bf16[16,144,512]{2,1,0:T(8,128)(2,1)}), bf16[16,144,512]{2,1,0:T(8,128)(2,1)}, u32[]{:S(2)}, u32[]{:S(2)}) %all-to-all-start.6) | async-done | bytes 2359328 | tf_op jit(solution)/shard_map/back_gather/all_to_all | solution.py:20
  292.4 4.4 %fusion.43 = (f32[512]{0:T(512)S(1)}, f32[512]{0:T(512)S(1)}, f32[16,128,512]{2,1,0:T(8,128)S(1)}) fusion(f32[16,128,256]{2,1,0:T(8,128)} %bitcast.69, f32[16,128,256]{2,1,0:T(8,128)} %bitcast.68, f32[512]{0:T(512)S(1)} %pad_maximum_fusion.9, bf16[16,144,512]{2,1,0:T(8,128)(2,1)} %all-to-all-done.6, f32[512]{0:T(512)S(1)} %add_sqrt_fusion, ...), kind=kLoop, calls=%fused_computation.67 | loop fusion | flops 13630464 | bytes 12623872 | tf_op jit(solution)/shard_map/grad/reduce_sum | solution.py:167
  297.1 0.7 copy-done.2
  297.8 0.6 copy-done.3
  298.4 2.1 fusion.9
  300.5 3.1 collective-permute-start.4
  303.6 1.9 collective-permute-start.3
  305.5 1.8 collective-permute-done.3
  307.4 0.6 add_reduce_fusion
  308.0 0.8 slice.131
  308.7 0.6 convert_reduce_fusion.3
  310.6 1.9 fusion.22
  312.6 0.5 convolution_add_fusion.1
  313.1 1.7 fusion.18
  314.9 1.8 broadcast_select_fusion.3
  316.7 1.0 copy.49
  (62 shorter events, 4.3 us)
Async XLA Ops:
  30.3 67.7 %all-to-all-start.1 = ((bf16[16,256,512]{2,1,0:T(8,128)(2,1)}), bf16[16,256,512]{2,1,0:T(8,128)(2,1)}, u32[]{:S(2)}, u32[]{:S(2)}) async-start(bf16[16,256,512]{2,1,0:T(8,128)(2,1)} %broadcast_in_dim.12), calls=%async_computation.1 | async-start | bytes 8388608 | tf_op jit(solution)/shard_map/weight_gather/all_to_all | solution.py:20
  34.8 72.6 %all-gather.3.cloned.1.call-start = ((), (), s32[]{:S(2)}) async-start(), calls=%async_computation.7 | async-start | bytes 2228224 | tf_op jit(solution)/shard_map/embeds_exchange/all_gather | solution.py:78
  43.6 57.4 %collective-permute-start = (bf16[128,4096]{1,0:T(8,128)(2,1)S(1)}, bf16[128,4096]{1,0:T(8,128)(2,1)}, u32[]{:S(2)}, u32[]{:S(2)}) collective-permute-start(bf16[128,4096]{1,0:T(8,128)(2,1)S(1)} %dynamic-slice_bitcast_fusion), channel_id=1, source_target_pairs={{0,16},{16,0},{1,17},{17,1},{2,18},{18,2},{3,19},{19,3},{4,20},{20... | collective-permute-start | bytes 3145736 | tf_op jit(solution)/shard_map/embeds_order/ppermute | solution.py:68
  104.3 6.5 %collective-permute-start.1 = (f32[128,512]{1,0:T(8,128)S(1)}, f32[128,512]{1,0:T(8,128)S(1)}, u32[]{:S(2)}, u32[]{:S(2)}) collective-permute-start(f32[128,512]{1,0:T(8,128)S(1)} %pad_maximum_fusion.3), channel_id=1, source_target_pairs={{0,16},{16,0},{1,17},{17,1},{2,18},{18,2},{3,19},{19,3},{4,20},{20... | collective-permute-start | bytes 786440 | tf_op jit(solution)/shard_map/project/ppermute | solution.py:68
  112.7 29.4 %all-to-all-start.2 = ((bf16[16,144,512]{2,1,0:T(8,128)(2,1)}), bf16[16,144,512]{2,1,0:T(8,128)(2,1)S(1)}, u32[]{:S(2)}, u32[]{:S(2)}) async-start(bf16[16,144,512]{2,1,0:T(8,128)(2,1)} %broadcast_in_dim.13), calls=%async_computation.2 | async-start | bytes 4718592 | tf_op jit(solution)/shard_map/project_gather/all_to_all | solution.py:20
  142.1 1.5 copy-start.4
  143.6 1.9 copy-start
  236.9 10.5 %collective-permute-start.2 = (bf16[2048,128]{1,0:T(8,128)(2,1)S(1)}, bf16[2048,128]{1,0:T(8,128)(2,1)S(1)}, u32[]{:S(2)}, u32[]{:S(2)}) collective-permute-start(bf16[2048,128]{1,0:T(8,128)(2,1)S(1)} %bitcast.77), channel_id=1, source_target_pairs={{0,16},{16,0},{1,17},{17,1},{2,18},{18,2},{3,19},{19,3},{4,20},{20... | collective-permute-start | bytes 1572872 | tf_op jit(solution)/shard_map/gram_gather/ppermute | solution.py:68
  251.2 41.3 %all-to-all-start.6 = ((bf16[16,144,512]{2,1,0:T(8,128)(2,1)}), bf16[16,144,512]{2,1,0:T(8,128)(2,1)}, u32[]{:S(2)}, u32[]{:S(2)}) async-start(bf16[16,144,512]{2,1,0:T(8,128)(2,1)} %broadcast_in_dim.17), calls=%async_computation.6 | async-start | bytes 4718592 | tf_op jit(solution)/shard_map/back_gather/all_to_all | solution.py:20
  292.4 4.7 %copy-start.1 = (f32[16,128,512]{2,1,0:T(8,128)S(1)}, f32[16,128,512]{2,1,0:T(8,128)}, u32[]{:S(2)}) copy-start(f32[16,128,512]{2,1,0:T(8,128)} %copy-done) | copy-start | bytes 12582916
  292.4 5.3 %copy-start.2 = (f32[2048,256]{1,0:T(8,128)S(1)}, f32[2048,256]{1,0:T(8,128)}, u32[]{:S(2)}) copy-start(f32[2048,256]{1,0:T(8,128)} %get-tuple-element.56) | copy-start | bytes 6291460
  292.4 5.9 %copy-start.3 = (f32[2048,256]{1,0:T(8,128)S(1)}, f32[2048,256]{1,0:T(8,128)}, u32[]{:S(2)}) copy-start(f32[2048,256]{1,0:T(8,128)} %get-tuple-element.57) | copy-start | bytes 6291460
  300.5 12.6 %collective-permute-start.4 = (bf16[2048,512]{1,0:T(8,128)(2,1)S(1)}, bf16[2048,512]{1,0:T(8,128)(2,1)}, u32[]{:S(2)}, u32[]{:S(2)}) collective-permute-start(bf16[2048,512]{1,0:T(8,128)(2,1)S(1)} %fusion.9), channel_id=1, source_target_pairs={{0,16},{16,0},{1,17},{17,1},{2,18},{18,2},{3,19},{19,3},{4,20},{20... | collective-permute-start | bytes 6291464 | tf_op jit(solution)/shard_map/grad_swap/ppermute | solution.py:68
  303.6 3.8 %collective-permute-start.3 = (f32[128]{0:T(128)S(1)}, f32[128]{0:T(128)S(1)}, u32[]{:S(2)}, u32[]{:S(2)}) collective-permute-start(f32[128]{0:T(128)S(1)} %slice_reduce_fusion), channel_id=1, source_target_pairs={{0,16},{16,0},{1,17},{17,1},{2,18},{18,2},{3,19},{19,3},{4,20},{20... | collective-permute-start | bytes 1544 | tf_op jit(solution)/shard_map/back/ppermute | solution.py:68
  310.6 1.9 copy-start.5
Sparse Core Ops, SparseCore 0:
  37.8 67.5 all-gather.2

commit v4 on v3

--- a/solution.py
+++ b/solution.py
@@ -1,6 +1,10 @@
+import functools
+
 import jax
 import jax.numpy as jnp
 from jax import lax
+from jax.experimental import pallas as pl
+from jax.experimental.pallas import tpu as pltpu
 from jax.sharding import Mesh, PartitionSpec as P
 
 D_OUT = 8192
@@ -46,6 +50,50 @@
     return lax.dot_general(high, view, rows, preferred_element_type=F32) + lax.dot_general(
         low, view, rows, preferred_element_type=F32
     )
+
+
+def ring_groups():
+    index = lambda y, x, c: (y * 4 + x) * 2 + c
+    along_x = lambda c: [[index(y, x, c) for x in range(4)] for y in range(4)]
+    along_y = lambda c: [[index(y, x, c) for y in range(4)] for x in range(4)]
+    return along_x(0) + along_y(1), along_y(0) + along_x(1)
+
+
+def ring_gather(block, groups):
+    blocks = jnp.broadcast_to(block[None], (4,) + block.shape)
+    return lax.all_to_all(blocks, BATCH, split_axis=0, concat_axis=0, tiled=True, axis_index_groups=groups)
+
+
+def grad_kernel(n_rows, chip_rows, scale, back_ref, got_ref, shift_ref, inv_ref, cross_ref, out_ref, grad_ref, std_ref):
+    n_chip, _, width = got_ref.shape
+    half = width // 2
+    inv, factor = inv_ref[...], cross_ref[...]
+
+    def fold(a):
+        return jnp.sum(a.reshape(chip_rows // 8, 8, width), axis=0)
+
+    def first(p, sums):
+        centered = got_ref[p, :chip_rows].astype(F32) + shift_ref[pl.ds(p, 1), :]
+        standard = centered * inv
+        normed = standard.astype(BF16).astype(F32)
+        crossed = jnp.concatenate([normed[:, half:], normed[:, :half]], axis=1)
+        grad = scale * back_ref[p, :chip_rows].astype(F32) + factor * crossed
+        rows = pl.ds(pl.multiple_of(p * chip_rows, chip_rows), chip_rows)
+        grad_ref[rows, :] = grad
+        std_ref[rows, :] = standard
+        return sums[0] + fold(grad), sums[1] + fold(grad * standard)
+
+    zero = jnp.zeros((8, width), F32)
+    total, cross = lax.fori_loop(0, n_chip, first, (zero, zero))
+    grad_mean = jnp.sum(total, axis=0, keepdims=True) / n_rows
+    grad_cross = jnp.sum(cross, axis=0, keepdims=True) / n_rows
+
+    def second(p, carry):
+        rows = pl.ds(pl.multiple_of(p * chip_rows, chip_rows), chip_rows)
+        out_ref[rows, :] = ((grad_ref[rows, :] - grad_mean - std_ref[rows, :] * grad_cross) * inv).astype(BF16)
+        return carry
+
+    lax.fori_loop(0, n_chip, second, 0)
 
 
 def body(embeds, weight):
@@ -76,15 +124,16 @@
         z_rows = exchange(z_rows, BATCH)
         weight, z_rows = lax.optimization_barrier((weight, z_rows))
         embeds_k = lax.all_gather(z_rows, "feat", axis=0, tiled=False)
-        embeds_k = embeds_k.reshape(2, per_view, n_batch, share, depth).transpose(0, 2, 1, 3, 4)
-        embeds_k = embeds_k.reshape(2, n_rows, depth)
     with jax.named_scope("weight_gather"):
-        core_weight = gather(weight, PLANE).reshape(n_chip * depth, width_out)
+        first_groups, second_groups = ring_groups()
+        row_weight = ring_gather(weight, first_groups)
+        core_weight = ring_gather(row_weight, second_groups).reshape(n_chip * depth, width_out)
     with jax.named_scope("embeds_order"):
-        by_core = embeds.reshape(local_rows, 2, n_chip, 2, depth).transpose(3, 1, 0, 2, 4)
-        by_core = by_core.reshape(2, 2 * local_rows, n_chip * depth)
-        own_rows = lax.dynamic_index_in_dim(by_core, core, 0, keepdims=False)
-        other_rows = swap_core(lax.dynamic_index_in_dim(by_core, 1 - core, 0, keepdims=False))
+        by_core = embeds.reshape(local_rows, 2, 4, n_chip // 4, 2, depth)
+        rows_zero = by_core[:, :, :, :, 0].transpose(1, 0, 2, 3, 4).reshape(2 * local_rows, n_chip * depth)
+        rows_one = by_core[:, :, :, :, 1].transpose(1, 0, 3, 2, 4).reshape(2 * local_rows, n_chip * depth)
+        own_rows = jnp.where(first, rows_zero, rows_one)
+        other_rows = swap_core(jnp.where(first, rows_one, rows_zero))
     with jax.named_scope("project"):
         own = jnp.dot(own_rows, core_weight, preferred_element_type=F32)
         other = jnp.dot(other_rows, core_weight, preferred_element_type=F32)
@@ -105,16 +154,19 @@
         )
         block, embeds_k = lax.optimization_barrier((block, embeds_k))
         got = gather(block, PLANE)
+        embeds_k = embeds_k.reshape(2, per_view, n_batch, share, depth).transpose(0, 2, 1, 3, 4)
+        embeds_k = embeds_k.reshape(2, n_rows, depth)
         embeds_a, embeds_b = embeds_k[0], embeds_k[1]
     with jax.named_scope("standardize"):
         chip_means = jnp.sum(got[:, chip_rows : chip_rows + 3].astype(F32), axis=1)
         row_mean = jnp.sum(chip_means, axis=0) / n_chip
-        centered = got[:, :chip_rows].astype(F32) + (chip_means - row_mean)[:, None, :]
+        shift = chip_means - row_mean
+        centered = got[:, :chip_rows].astype(F32) + shift[:, None, :]
         centered = centered.reshape(n_rows, width_out)
         variance = jnp.sum(centered * centered, axis=0) / n_rows
         spread = jnp.sqrt(variance + epsilon)
-        standard = centered / spread
-        normed = standard.astype(BF16)
+        inverse = 1.0 / spread
+        normed = (centered * inverse).astype(BF16)
         view_a, view_b = normed[:, :half], normed[:, half:]
         float_a, float_b = view_a.astype(F32), view_b.astype(F32)
         diagonal = jnp.sum(float_a * float_b, axis=0) / n_rows
@@ -128,7 +180,9 @@
         part_b = lax.dot_general(view_b, mine[:, half:], contract, preferred_element_type=F32)
         parts = jnp.stack([part_a.astype(BF16), part_b.astype(BF16)])
         extra = pad_rows(pieces(diag_local), chip_rows)
-        parts, extra, diagonal, spread = lax.optimization_barrier((parts, extra, diagonal, spread))
+        weight_diag = 2.0 * ((1.0 - off_weight) * diagonal - 1.0)
+        factor = loss_scale / n_rows * jnp.concatenate([weight_diag, weight_diag])
+        parts, extra, factor, inverse = lax.optimization_barrier((parts, extra, factor, inverse))
     with jax.named_scope("gram_core"):
         parts = jnp.sum(exchange(parts, "core").astype(F32), axis=0)
     with jax.named_scope("gram_reduce"):
@@ -151,22 +205,25 @@
         back = jnp.concatenate([back_a, back_b], axis=1).astype(BF16)
         terms = jnp.concatenate([off_local, jnp.zeros((width_out - chip_rows,), F32)])
         block = jnp.concatenate([back, pad_rows(pieces(terms), width_out)], axis=0)
-        other_diag = swap_core(diag_core)
+        block, diag_terms = lax.optimization_barrier((block, diag_core + swap_core(diag_core)))
     with jax.named_scope("back_gather"):
-        got = gather(block, PLANE)
+        got_back = gather(block, PLANE)
     with jax.named_scope("grad"):
-        off_total = jnp.sum(got[:, chip_rows : chip_rows + 3, :chip_rows].astype(F32)) / (n_rows * n_rows)
-        diag_total = jnp.sum(diag_core + other_diag)
+        off_total = jnp.sum(got_back[:, chip_rows : chip_rows + 3, :chip_rows].astype(F32)) / (n_rows * n_rows)
+        diag_total = jnp.sum(diag_terms)
         loss_value = (off_weight * off_total + diag_total) / D_OUT
-        back = got[:, :chip_rows].astype(F32).reshape(n_rows, width_out)
-        weight_diag = 2.0 * ((1.0 - off_weight) * diagonal - 1.0)
-        weight_diag = jnp.concatenate([weight_diag, weight_diag])
         scale_off = 2.0 * off_weight / (n_rows * n_rows)
-        crossed = jnp.concatenate([float_b, float_a], axis=1)
-        grad_normed = loss_scale * (scale_off * back + weight_diag * crossed / n_rows)
-        grad_mean = jnp.sum(grad_normed, axis=0) / n_rows
-        grad_cross = jnp.sum(grad_normed * standard, axis=0) / n_rows
-        grad_proj = ((grad_normed - grad_mean - standard * grad_cross) / spread).astype(BF16)
+        vmem = pl.BlockSpec(memory_space=pltpu.VMEM)
+        grad_proj = pl.pallas_call(
+            functools.partial(grad_kernel, n_rows, chip_rows, loss_scale * scale_off),
+            out_shape=jax.ShapeDtypeStruct((n_rows, width_out), BF16),
+            in_specs=[vmem] * 5,
+            out_specs=vmem,
+            scratch_shapes=[pltpu.VMEM((n_rows, width_out), F32)] * 2,
+            compiler_params=pltpu.CompilerParams(vmem_limit_bytes=32 * 1024 * 1024),
+            cost_estimate=pl.CostEstimate(flops=20 * n_rows * width_out, bytes_accessed=8 * n_rows * width_out, transcendentals=0),
+            name="grad",
+        )(got_back, got, shift, inverse[None], factor[None])
     with jax.named_scope("grad_swap"):
         other_proj = swap_core(grad_proj)
     with jax.named_scope("weight_grad"):

time: 327 us -> 322 us (0.985)
  waiting for transfers between devices: 115 us -> 69.6 us
  blocking collectives: 105 us -> 149 us
  local copies, waits for them, and re-layouts: 25.6 us -> 21.8 us
  Pallas kernels: 0 us -> 3.69 us
  other arithmetic: 14.7 us -> 11.3 us
    all_to_all x3 -> x1, waiting for transfers between devices: 111 us -> 24.4 us  [exchange(): return lax.all_to_all(blocks, axes, split_axis=0, concat_axis=0, tiled=True)]
    all_gather x1, waiting for transfers between devices: 0.02 us -> 36.4 us  [body(): embeds_k = lax.all_gather(z_rows, 'feat', axis=0, tiled=False)]
    all_to_all x4 -> x5, blocking collectives: 105 us -> 136 us  [exchange(): return lax.all_to_all(blocks, axes, split_axis=0, concat_axis=0, tiled=True)]
    all_to_all x0 -> x1, blocking collectives: none -> 12.5 us  [ring_gather(): lax.all_to_all(blocks, BATCH, split_axis=0, concat_axis=0, tiled=True, ax...]
    all_to_all x3 -> x1, starting transfers between devices: 13.9 us -> 6.77 us  [exchange(): return lax.all_to_all(blocks, axes, split_axis=0, concat_axis=0, tiled=True)]
    all_to_all x0 -> x1, waiting for transfers between devices: none -> 5.78 us  [ring_gather(): lax.all_to_all(blocks, BATCH, split_axis=0, concat_axis=0, tiled=True, ax...]
    slice x2 -> x4, local copies, waits for them, and re-layouts: 0.79 us -> 6.46 us  [the longest x1 6.08 us: body(): by_core[:, :, :, :, 1].transpose(1, 0, 3, 2, 4)]
    all_to_all x0 -> x1, starting transfers between devices: none -> 4.86 us  [ring_gather(): lax.all_to_all(blocks, BATCH, split_axis=0, concat_axis=0, tiled=True, ax...]
  transfers between devices with their start and end apart: 9 -> 8, of which waited for: 5 -> 6; matrix products, arithmetic and copies ran while one was open for 7% -> 9% of each run, Pallas kernels for 0% -> 0%
where the time goes in v4:
time: 322 us; the launch traced here: 321 us
  blocking collectives  149 us (46%)
  waiting for transfers between devices  69.6 us (22%)
  starting transfers between devices  33 us (10%)
  local copies, waits for them, and re-layouts  21.8 us (7%)
  between operations  16.9 us (5%)
  matrix products  15.5 us (5%)
  other arithmetic  11.3 us (4%)
  Pallas kernels  3.69 us (1%)
    all_to_all x5, blocking collectives, exchange(): return lax.all_to_all(blocks, axes, split_axis=0, concat_axis=0, tiled=True)  136 us
    all_gather x1, waiting for transfers between devices, body(): embeds_k = lax.all_gather(z_rows, 'feat', axis=0, tiled=False)  36.4 us
    all_to_all x1, waiting for transfers between devices, exchange(): return lax.all_to_all(blocks, axes, split_axis=0, concat_axis=0, tiled=True)  24.4 us
    ppermute x5, starting transfers between devices, swap_core(): return lax.ppermute(a, 'core', [(0, 1), (1, 0)])  21.3 us
    all_to_all x1, blocking collectives, ring_gather(): lax.all_to_all(blocks, BATCH, split_axis=0, concat_axis=0, tiled=True, ax...  12.5 us
    all_to_all x1, starting transfers between devices, exchange(): return lax.all_to_all(blocks, axes, split_axis=0, concat_axis=0, tiled=True)  6.77 us
  transfers between devices with their start and end apart: 8, of which 6 were waited for; matrix products, arithmetic and copies ran while one was open for 9% of the time, Pallas kernels for 0%

profile of v4, /device:TPU:1, one launch (start us, length us, event | category | flops | bytes accessed | tf_op | source)
XLA Modules:
  0.0 320.8 jit_solution(5620726656082266204)
XLA Ops:
  7.2 1.7 dynamic-slice_reduce_fusion
  9.0 17.9 %all_to_all.40 = bf16[32,8,256]{2,1,0:T(8,128)(2,1)} all-to-all(bf16[32,8,256]{2,1,0:T(8,128)(2,1)S(1)} %copy.52), channel_id=1, replica_groups=mesh['y'=4,'x'=4,'core'=2,'feat'=16] {'y','x','core'}, dimensions={0} | all-to-all | bytes 262144 | tf_op jit(solution)/shard_map/embeds_exchange/all_to_all | solution.py:24
  27.0 1.0 broadcast_in_dim.18
  28.0 12.5 %all_to_all.41 = bf16[4,256,512]{2,1,0:T(8,128)(2,1)S(1)} all-to-all(bf16[4,256,512]{2,1,0:T(8,128)(2,1)S(1)} %broadcast_in_dim.18), channel_id=1, replica_groups={{0,32,64,96},{128,160,192,224},{256,288,320,352},{384,416,448,480},{16,..., dimensions={0} | all-to-all | bytes 2097152 | tf_op jit(solution)/shard_map/weight_gather/all_to_all | solution.py:64
  40.5 2.4 broadcast_in_dim.19
  42.8 4.9 %all-to-all-start.2 = ((bf16[4,4,256,512]{3,2,1,0:T(8,128)(2,1)}), bf16[4,4,256,512]{3,2,1,0:T(8,128)(2,1)}, u32[]{:S(2)}, u32[]{:S(2)}) async-start(bf16[4,4,256,512]{3,2,1,0:T(8,128)(2,1)} %broadcast_in_dim.19), calls=%async_computation.2 | async-start | bytes 8388608 | tf_op jit(solution)/shard_map/weight_gather/all_to_all | solution.py:64
  47.8 3.3 %reshape.158 = bf16[64,2,4,4,2,256]{5,4,3,2,1,0:T(2,128)(2,1)S(1)} reshape(bf16[64,2,8192]{2,1,0:T(2,128)(2,1)} %param.2) | data formatting | bytes 4194304 | tf_op jit(solution)/shard_map/embeds_order/reshape | solution.py:132
  51.1 6.1 %fusion.39 = (bf16[64,2,4,4,1,256]{5,4,3,2,1,0:T(2,128)(2,1)}, bf16[64,2,4,4,1,256]{5,4,3,2,1,0:T(2,128)(2,1)}) fusion(bf16[64,2,4,4,2,256]{5,4,3,2,1,0:T(2,128)(2,1)S(1)} %reshape.158), kind=kLoop, calls=%fused_computation.101 | loop fusion | bytes 4194304 | tf_op jit(solution)/shard_map/embeds_order/slice | solution.py:134
  57.2 4.5 %broadcast_select_fusion.1 = (bf16[2,64,4,4,256]{4,1,3,2,0:T(8,128)(2,1)S(1)}, bf16[2,64,4,4,256]{4,1,3,2,0:T(8,128)(2,1)S(1)}) fusion(pred[]{:T(512)S(6)} %eq.5, bf16[64,2,4,4,1,256]{5,4,3,2,1,0:T(2,128)(2,1)} %get-tuple-element.58, bf16[64,2,4,4,1,256]{5,4,3,2,1,0:T(2,128)(2,1)} %get-tuple-element.57), kind=kLoop, calls=%fused_computation.32 | loop fusion | flops 1048576 | bytes 4194305 | tf_op jit(solution)/shard_map/embeds_order/jit(_where)/select_n | solution.py:135
  61.7 0.8 copy.53
  62.5 0.8 select_n.102
  63.3 3.2 collective-permute-start
  66.5 0.8 copy.51
  67.3 0.8 select_n.94
  68.1 0.8 collective-permute-done
  68.9 5.8 %all-to-all-done.2 = bf16[4,4,256,512]{3,2,1,0:T(8,128)(2,1)} async-done(((bf16[4,4,256,512]{3,2,1,0:T(8,128)(2,1)}), bf16[4,4,256,512]{3,2,1,0:T(8,128)(2,1)}, u32[]{:S(2)}, u32[]{:S(2)}) %all-to-all-start.2) | async-done | bytes 4194336 | tf_op jit(solution)/shard_map/weight_gather/all_to_all | solution.py:64
  74.7 3.3 %fusion.43 = f32[128,512]{1,0:T(8,128)S(1)} fusion(bf16[128,4096]{1,0:T(8,128)(2,1)} %collective-permute-done, bf16[4096,512]{1,0:T(8,128)(2,1)} %bitcast.6), kind=kOutput, calls=%fused_computation.105 | convolution fusion | flops 536870912 | bytes 5505024 | tf_op jit(solution)/shard_map/project/dot_general | solution.py:139
  78.0 2.9 fusion.42
  81.0 4.0 %collective-permute-start.1 = (f32[128,512]{1,0:T(8,128)S(1)}, f32[128,512]{1,0:T(8,128)S(1)}, u32[]{:S(2)}, u32[]{:S(2)}) collective-permute-start(f32[128,512]{1,0:T(8,128)S(1)} %pad_maximum_fusion.3), channel_id=1, source_target_pairs={{0,16},{16,0},{1,17},{17,1},{2,18},{18,2},{3,19},{19,3},{4,20},{20... | collective-permute-start | bytes 786440 | tf_op jit(solution)/shard_map/project/ppermute | solution.py:116
  85.0 1.1 collective-permute-done.1
  86.5 36.4 %all-gather.3.cloned.1.call-done = bf16[512,8,256]{2,1,0:T(8,128)(2,1)} async-done(((bf16[32,8,256]{2,1,0:T(8,128)(2,1)}), bf16[512,8,256]{2,1,0:T(8,128)(2,1)}) %all-gather.3.cloned.1.call-update) | async-done | bytes 2097168 | tf_op jit(solution)/shard_map/embeds_exchange/all_gather | solution.py:126
  122.9 1.6 broadcast_in_dim.20
  124.6 6.8 %all-to-all-start.3 = ((bf16[16,144,512]{2,1,0:T(8,128)(2,1)}), bf16[16,144,512]{2,1,0:T(8,128)(2,1)S(1)}, u32[]{:S(2)}, u32[]{:S(2)}) async-start(bf16[16,144,512]{2,1,0:T(8,128)(2,1)} %broadcast_in_dim.20), calls=%async_computation.3 | async-start | bytes 4718592 | tf_op jit(solution)/shard_map/project_gather/all_to_all | solution.py:24
  131.4 24.4 %all-to-all-done.3.got_ref = bf16[16,144,512]{2,1,0:T(8,128)(2,1)S(1)} async-done(((bf16[16,144,512]{2,1,0:T(8,128)(2,1)}), bf16[16,144,512]{2,1,0:T(8,128)(2,1)S(1)}, u32[]{:S(2)}, u32[]{:S(2)}) %all-to-all-start.3) | async-done | bytes 2359328 | tf_op jit(solution)/shard_map/project_gather/all_to_all | solution.py:24
  156.0 0.7 multiply_reduce_fusion
  156.7 0.6 fusion
  157.7 0.4 fusion.1
  158.1 0.4 fusion.2
  158.8 14.7 %all_to_all.42 = bf16[2,2048,128]{2,1,0:T(8,128)(2,1)S(1)} all-to-all(bf16[2,2048,128]{2,1,0:T(8,128)(2,1)S(1)} %pad_maximum_fusion), channel_id=1, replica_groups=mesh['y'=4,'x'=4,'core'=2,'feat'=16] {'core'}, dimensions={0} | all-to-all | bytes 2097152 | tf_op jit(solution)/shard_map/gram_core/all_to_all | solution.py:24
  173.5 1.1 reduce_sum.136
  174.7 1.1 pad_maximum_fusion.1
  175.7 40.6 %all_to_all.43 = bf16[16,144,128]{2,1,0:T(8,128)(2,1)S(1)} all-to-all(bf16[16,144,128]{2,1,0:T(8,128)(2,1)S(1)} %pad_maximum_fusion.1), channel_id=1, replica_groups=mesh['y'=4,'x'=4,'core'=2,'feat'=16] {'feat'}, dimensions={0} | all-to-all | bytes 1179648 | tf_op jit(solution)/shard_map/gram_reduce/all_to_all | solution.py:24
  216.6 27.4 %all_to_all.44 = bf16[16,128,128]{2,1,0:T(8,128)(2,1)S(1)} all-to-all(bf16[16,128,128]{2,1,0:T(8,128)(2,1)S(1)} %broadcast_in_dim.23), channel_id=1, replica_groups=mesh['y'=4,'x'=4,'core'=2,'feat'=16] {'feat'}, dimensions={0} | all-to-all | bytes 1048576 | tf_op jit(solution)/shard_map/gram_gather/all_to_all | solution.py:24
  243.9 9.0 %collective-permute-start.2 = (bf16[2048,128]{1,0:T(8,128)(2,1)S(1)}, bf16[2048,128]{1,0:T(8,128)(2,1)S(1)}, u32[]{:S(2)}, u32[]{:S(2)}) collective-permute-start(bf16[2048,128]{1,0:T(8,128)(2,1)S(1)} %bitcast.68), channel_id=1, source_target_pairs={{0,16},{16,0},{1,17},{17,1},{2,18},{18,2},{3,19},{19,3},{4,20},{20... | collective-permute-start | bytes 1572872 | tf_op jit(solution)/shard_map/gram_gather/ppermute | solution.py:116
  253.0 1.9 collective-permute-start.3
  254.9 1.1 collective-permute-done.3
  256.7 0.4 fusion.3
  257.4 0.4 fusion.4
  258.2 35.9 %all_to_all.45.back_ref = bf16[16,144,512]{2,1,0:T(8,128)(2,1)S(1)} all-to-all(bf16[16,144,512]{2,1,0:T(8,128)(2,1)S(1)} %broadcast_in_dim.24), channel_id=1, replica_groups=mesh['y'=4,'x'=4,'core'=2,'feat'=16] {'y','x'}, dimensions={0} | all-to-all | bytes 4718592 | tf_op jit(solution)/shard_map/back_gather/all_to_all | solution.py:24
  294.1 3.7 %grad.1 = bf16[2048,512]{1,0:T(8,128)(2,1)} custom-call(bf16[16,144,512]{2,1,0:T(8,128)(2,1)S(1)} %all_to_all.45.back_ref, bf16[16,144,512]{2,1,0:T(8,128)(2,1)S(1)} %all-to-all-done.3.got_ref, f32[16,512]{1,0:T(8,128)S(1)} %broadcast_subtract_fusion.shift_ref, f32[1,512]{1,0:T(1,128)S(1)} %bitcast.64, f32[1,512]{1,0:T(1,128)S(1)} %bitcast.65), custom_call_target="tpu_custom_call" | custom-call | flops 20971520 | bytes 8388608 | tf_op jit(solution)/shard_map/grad/grad/pallas_call | solution.py:217
  297.8 3.2 %collective-permute-start.4 = (bf16[2048,512]{1,0:T(8,128)(2,1)}, bf16[2048,512]{1,0:T(8,128)(2,1)}, u32[]{:S(2)}, u32[]{:S(2)}) collective-permute-start(bf16[2048,512]{1,0:T(8,128)(2,1)} %grad.1), channel_id=1, source_target_pairs={{0,16},{16,0},{1,17},{17,1},{2,18},{18,2},{3,19},{19,3},{4,20},{20... | collective-permute-start | bytes 6291464 | tf_op jit(solution)/shard_map/grad_swap/ppermute | solution.py:116
  301.5 0.6 reduce_sum.141
  302.1 1.4 convert_reduce_fusion.3
  304.8 1.7 fusion.12
  306.5 1.7 convolution_add_fusion.1
  308.3 1.7 fusion.8
  310.0 1.8 broadcast_select_fusion.5
  311.8 1.0 copy.56
  (58 shorter events, 3.5 us)
Async XLA Ops:
  42.8 31.8 %all-to-all-start.2 = ((bf16[4,4,256,512]{3,2,1,0:T(8,128)(2,1)}), bf16[4,4,256,512]{3,2,1,0:T(8,128)(2,1)}, u32[]{:S(2)}, u32[]{:S(2)}) async-start(bf16[4,4,256,512]{3,2,1,0:T(8,128)(2,1)} %broadcast_in_dim.19), calls=%async_computation.2 | async-start | bytes 8388608 | tf_op jit(solution)/shard_map/weight_gather/all_to_all | solution.py:64
  47.7 75.2 %all-gather.3.cloned.1.call-start = ((), (), s32[]{:S(2)}) async-start(), calls=%async_computation.8 | async-start | bytes 2228224 | tf_op jit(solution)/shard_map/embeds_exchange/all_gather | solution.py:126
  63.3 5.6 %collective-permute-start = (bf16[128,4096]{1,0:T(8,128)(2,1)S(1)}, bf16[128,4096]{1,0:T(8,128)(2,1)}, u32[]{:S(2)}, u32[]{:S(2)}) collective-permute-start(bf16[128,4096]{1,0:T(8,128)(2,1)S(1)} %select_n.102), channel_id=1, source_target_pairs={{0,16},{16,0},{1,17},{17,1},{2,18},{18,2},{3,19},{19,3},{4,20},{20... | collective-permute-start | bytes 3145736 | tf_op jit(solution)/shard_map/embeds_order/ppermute | solution.py:116
  81.0 5.1 %collective-permute-start.1 = (f32[128,512]{1,0:T(8,128)S(1)}, f32[128,512]{1,0:T(8,128)S(1)}, u32[]{:S(2)}, u32[]{:S(2)}) collective-permute-start(f32[128,512]{1,0:T(8,128)S(1)} %pad_maximum_fusion.3), channel_id=1, source_target_pairs={{0,16},{16,0},{1,17},{17,1},{2,18},{18,2},{3,19},{19,3},{4,20},{20... | collective-permute-start | bytes 786440 | tf_op jit(solution)/shard_map/project/ppermute | solution.py:116
  124.6 31.3 %all-to-all-start.3 = ((bf16[16,144,512]{2,1,0:T(8,128)(2,1)}), bf16[16,144,512]{2,1,0:T(8,128)(2,1)S(1)}, u32[]{:S(2)}, u32[]{:S(2)}) async-start(bf16[16,144,512]{2,1,0:T(8,128)(2,1)} %broadcast_in_dim.20), calls=%async_computation.3 | async-start | bytes 4718592 | tf_op jit(solution)/shard_map/project_gather/all_to_all | solution.py:24
  157.3 1.4 copy-start.1
  216.4 39.9 %copy-start.2 = (bf16[2048,512]{1,0:T(8,128)(2,1)S(1)}, bf16[2048,512]{1,0:T(8,128)(2,1)}, u32[]{:S(2)}) copy-start(bf16[2048,512]{1,0:T(8,128)(2,1)} %copy-done.1) | copy-start | bytes 6291460
  243.9 12.1 %collective-permute-start.2 = (bf16[2048,128]{1,0:T(8,128)(2,1)S(1)}, bf16[2048,128]{1,0:T(8,128)(2,1)S(1)}, u32[]{:S(2)}, u32[]{:S(2)}) collective-permute-start(bf16[2048,128]{1,0:T(8,128)(2,1)S(1)} %bitcast.68), channel_id=1, source_target_pairs={{0,16},{16,0},{1,17},{17,1},{2,18},{18,2},{3,19},{19,3},{4,20},{20... | collective-permute-start | bytes 1572872 | tf_op jit(solution)/shard_map/gram_gather/ppermute | solution.py:116
  253.0 3.0 collective-permute-start.3
  294.1 3.7 %copy-start = (bf16[16,144,512]{2,1,0:T(8,128)(2,1)}, bf16[16,144,512]{2,1,0:T(8,128)(2,1)S(1)}, u32[]{:S(2)}) copy-start(bf16[16,144,512]{2,1,0:T(8,128)(2,1)S(1)} %all_to_all.45.back_ref) | copy-start | bytes 7077892
  294.1 6.9 %copy-start.3 = (bf16[512,8,256]{2,1,0:T(8,128)(2,1)S(1)}, bf16[512,8,256]{2,1,0:T(8,128)(2,1)}, u32[]{:S(2)}) copy-start(bf16[512,8,256]{2,1,0:T(8,128)(2,1)} %all-gather.3.cloned.1.call-done) | copy-start | bytes 6291460
  297.8 10.4 %collective-permute-start.4 = (bf16[2048,512]{1,0:T(8,128)(2,1)}, bf16[2048,512]{1,0:T(8,128)(2,1)}, u32[]{:S(2)}, u32[]{:S(2)}) collective-permute-start(bf16[2048,512]{1,0:T(8,128)(2,1)} %grad.1), channel_id=1, source_target_pairs={{0,16},{16,0},{1,17},{17,1},{2,18},{18,2},{3,19},{19,3},{4,20},{20... | collective-permute-start | bytes 6291464 | tf_op jit(solution)/shard_map/grad_swap/ppermute | solution.py:116
Sparse Core Ops, SparseCore 0:
  57.3 65.5 all-gather.2

commit v5 on v4

--- a/solution.py
+++ b/solution.py
@@ -17,6 +17,7 @@
 BF16 = jnp.bfloat16
 PLANE = ("y", "x")
 BATCH = ("y", "x", "core")
+FEAT = ("z1", "z0")
 PAD = 16
 
 
@@ -98,7 +99,8 @@
 
 def body(embeds, weight):
     n_chip = lax.axis_size(PLANE)
-    n_feat = lax.axis_size("feat")
+    n_near, n_far = lax.axis_size("z0"), lax.axis_size("z1")
+    n_feat = n_near * n_far
     n_batch = 2 * n_chip
     local_rows, _, d_in = embeds.shape
     chip_rows = 2 * local_rows
@@ -116,14 +118,12 @@
         return lax.ppermute(a, "core", [(0, 1), (1, 0)])
 
     with jax.named_scope("embeds_exchange"):
-        share = 2 * local_rows // n_feat
-        per_view = n_feat // 2
-        z = lax.axis_index("feat")
-        z_rows = lax.dynamic_slice(embeds, ((z % per_view) * share, z // per_view, 0), (share, 1, d_in))
-        z_rows = z_rows.reshape(share, n_batch, depth).transpose(1, 0, 2)
-        z_rows = exchange(z_rows, BATCH)
-        weight, z_rows = lax.optimization_barrier((weight, z_rows))
-        embeds_k = lax.all_gather(z_rows, "feat", axis=0, tiled=False)
+        odd = lax.axis_index("z0") % 2
+        one_view = lax.dynamic_index_in_dim(embeds, odd, 1, keepdims=False)
+        one_view = one_view.reshape(local_rows, n_batch, depth).transpose(1, 0, 2)
+        one_view = exchange(one_view, BATCH).reshape(n_rows, depth)
+        weight, one_view = lax.optimization_barrier((weight, one_view))
+        other_one = lax.ppermute(one_view, "z0", [(0, 1), (1, 0), (2, 3), (3, 2)])
     with jax.named_scope("weight_gather"):
         first_groups, second_groups = ring_groups()
         row_weight = ring_gather(weight, first_groups)
@@ -152,11 +152,7 @@
         block = jnp.concatenate(
             [(projected - chip_mean).astype(BF16), pad_rows(pieces(chip_mean), width_out)], axis=0
         )
-        block, embeds_k = lax.optimization_barrier((block, embeds_k))
         got = gather(block, PLANE)
-        embeds_k = embeds_k.reshape(2, per_view, n_batch, share, depth).transpose(0, 2, 1, 3, 4)
-        embeds_k = embeds_k.reshape(2, n_rows, depth)
-        embeds_a, embeds_b = embeds_k[0], embeds_k[1]
     with jax.named_scope("standardize"):
         chip_means = jnp.sum(got[:, chip_rows : chip_rows + 3].astype(F32), axis=1)
         row_mean = jnp.sum(chip_means, axis=0) / n_chip
@@ -182,19 +178,24 @@
         extra = pad_rows(pieces(diag_local), chip_rows)
         weight_diag = 2.0 * ((1.0 - off_weight) * diagonal - 1.0)
         factor = loss_scale / n_rows * jnp.concatenate([weight_diag, weight_diag])
-        parts, extra, factor, inverse = lax.optimization_barrier((parts, extra, factor, inverse))
+        parts, extra, factor, inverse, other_one = lax.optimization_barrier((parts, extra, factor, inverse, other_one))
     with jax.named_scope("gram_core"):
         parts = jnp.sum(exchange(parts, "core").astype(F32), axis=0)
     with jax.named_scope("gram_reduce"):
-        parts = parts.astype(BF16).reshape(n_feat, n_rows // n_feat, chip_rows)
-        extra = jnp.broadcast_to(extra[None], (n_feat, PAD, chip_rows))
-        got_z = exchange(jnp.concatenate([parts, extra], axis=1), "feat")
+        parts = parts.astype(BF16).reshape(n_near, n_rows // n_near, chip_rows)
+        extra = jnp.broadcast_to(extra[None], (n_near, PAD, chip_rows))
+        got_z = exchange(jnp.concatenate([parts, extra], axis=1), "z0")
+        summed = jnp.sum(got_z.astype(F32), axis=0)
+        extra = pad_rows(pieces(jnp.sum(summed[n_rows // n_near :], axis=0)), chip_rows)
+        parts = summed[: n_rows // n_near].astype(BF16).reshape(n_far, n_rows // n_feat, chip_rows)
+        extra = jnp.broadcast_to(extra[None], (n_far, PAD, chip_rows))
+        got_z = exchange(jnp.concatenate([parts, extra], axis=1), "z1")
         summed = jnp.sum(got_z.astype(F32), axis=0)
         gram_block = summed[: n_rows // n_feat].astype(BF16)
-        diag_core = jnp.sum(summed[n_rows // n_feat : n_rows // n_feat + 3], axis=0)
+        diag_core = jnp.sum(summed[n_rows // n_feat :], axis=0)
         gram_block, diag_core = lax.optimization_barrier((gram_block, diag_core))
     with jax.named_scope("gram_gather"):
-        gram_t = gather(gram_block, "feat").reshape(n_rows, chip_rows)
+        gram_t = gather(gather(gram_block, "z1"), "z0").reshape(n_rows, chip_rows)
         other_t = swap_core(gram_t)
         gram_a = jnp.where(first, gram_t, other_t).astype(F32)
         gram_b = jnp.where(first, other_t, gram_t).astype(F32)
@@ -227,6 +228,8 @@
     with jax.named_scope("grad_swap"):
         other_proj = swap_core(grad_proj)
     with jax.named_scope("weight_grad"):
+        embeds_a = jnp.where(odd == 0, one_view, other_one)
+        embeds_b = jnp.where(odd == 0, other_one, one_view)
         def half_grad(g):
             rows = (((0,), (0,)), ((), ()))
             return lax.dot_general(embeds_a, g[:, :half], rows, preferred_element_type=F32) + lax.dot_general(
@@ -238,11 +241,11 @@
 
 def solution(mesh):
     n_batch, n_feat = mesh.devices.shape
-    grid = Mesh(mesh.devices.reshape(4, n_batch // 8, 2, n_feat), ("y", "x", "core", "feat"))
+    grid = Mesh(mesh.devices.reshape(4, n_batch // 8, 2, n_feat // 4, 4), BATCH + FEAT)
     return jax.shard_map(
         body,
         mesh=grid,
-        in_specs=(P(BATCH, None, None), P(BATCH, "feat")),
-        out_specs=(P(), P(BATCH, "feat")),
+        in_specs=(P(BATCH, None, None), P(BATCH, FEAT)),
+        out_specs=(P(), P(BATCH, FEAT)),
         check_vma=False,
     )

time: 322 us -> 287 us (0.89)
  waiting for transfers between devices: 69.6 us -> 45.8 us
  between operations: 16.9 us -> 3.59 us
  local copies, waits for them, and re-layouts: 21.8 us -> 27 us
    all_gather x1 -> x0, waiting for transfers between devices: 36.4 us -> none  [body(): embeds_k = lax.all_gather(z_rows, 'feat', axis=0, tiled=False)]
    all_to_all x1, waiting for transfers between devices: 24.4 us -> 34.4 us  [exchange(): return lax.all_to_all(blocks, axes, split_axis=0, concat_axis=0, tiled=True)]
    dynamic_slice x1, local copies, waits for them, and re-layouts: 1.73 us -> 7.85 us  [body(): one_view = lax.dynamic_index_in_dim(embeds, odd, 1, keepdims=False)]
    all_to_all x5 -> x7, blocking collectives: 136 us -> 139 us  [exchange(): return lax.all_to_all(blocks, axes, split_axis=0, concat_axis=0, tiled=True)]
  transfers between devices with their start and end apart: 8 -> 8, of which waited for: 6 -> 5; matrix products, arithmetic and copies ran while one was open for 9% -> 7% of each run, Pallas kernels for 0% -> 0%
where the time goes in v5:
time: 287 us; the launch traced here: 286 us
  blocking collectives  152 us (53%)
  waiting for transfers between devices  45.8 us (16%)
  starting transfers between devices  30.8 us (11%)
  local copies, waits for them, and re-layouts  27 us (9%)
  matrix products  14.7 us (5%)
  other arithmetic  9.18 us (3%)
  Pallas kernels  3.69 us (1%)
  between operations  3.59 us (1%)
    all_to_all x7, blocking collectives, exchange(): return lax.all_to_all(blocks, axes, split_axis=0, concat_axis=0, tiled=True)  139 us
    all_to_all x1, waiting for transfers between devices, exchange(): return lax.all_to_all(blocks, axes, split_axis=0, concat_axis=0, tiled=True)  34.4 us
    ppermute x5, starting transfers between devices, swap_core(): return lax.ppermute(a, 'core', [(0, 1), (1, 0)])  19.8 us
    all_to_all x1, blocking collectives, ring_gather(): lax.all_to_all(blocks, BATCH, split_axis=0, concat_axis=0, tiled=True, ax...  12.5 us
    all_to_all x1, waiting for transfers between devices, ring_gather(): lax.all_to_all(blocks, BATCH, split_axis=0, concat_axis=0, tiled=True, ax...  8.15 us
    dynamic_slice x1, local copies, waits for them, and re-layouts, body(): one_view = lax.dynamic_index_in_dim(embeds, odd, 1, keepdims=False)  7.85 us
  transfers between devices with their start and end apart: 8, of which 5 were waited for; matrix products, arithmetic and copies ran while one was open for 7% of the time, Pallas kernels for 0%

profile of v5, /device:TPU:1, one launch (start us, length us, event | category | flops | bytes accessed | tf_op | source)
XLA Modules:
  0.0 286.3 jit_solution(817186021402217935)
XLA Ops:
  0.6 7.9 %dynamic-slice_reduce_fusion = bf16[64,8192]{1,0:T(8,128)(2,1)S(1)} fusion(bf16[64,2,8192]{2,1,0:T(2,128)(2,1)} %param.2, s32[]{:T(128)S(6)} %select_n.102), kind=kLoop, calls=%fused_computation.9 | loop fusion | bytes 2097156 | tf_op jit(solution)/shard_map/embeds_exchange/jit(dynamic_index_in_dim)/dynamic_slice | solution.py:122
  8.8 0.6 copy.37
  9.4 26.8 %all_to_all.50 = bf16[32,64,256]{2,1,0:T(8,128)(2,1)S(1)} all-to-all(bf16[32,64,256]{2,1,0:T(8,128)(2,1)S(1)} %copy.37), channel_id=1, replica_groups=mesh['y'=4,'x'=4,'core'=2,'z1'=4,'z0'=4] {'y','x','core'}, dimensions={0} | all-to-all | bytes 2097152 | tf_op jit(solution)/shard_map/embeds_exchange/all_to_all | solution.py:25
  36.3 12.5 %all_to_all.51 = bf16[4,256,512]{2,1,0:T(8,128)(2,1)S(1)} all-to-all(bf16[4,256,512]{2,1,0:T(8,128)(2,1)S(1)} %broadcast_in_dim.20), channel_id=1, replica_groups={{0,32,64,96},{128,160,192,224},{256,288,320,352},{384,416,448,480},{16,..., dimensions={0} | all-to-all | bytes 2097152 | tf_op jit(solution)/shard_map/weight_gather/all_to_all | solution.py:65
  48.8 2.4 broadcast_in_dim.21
  51.1 5.0 %all-to-all-start.2 = ((bf16[4,4,256,512]{3,2,1,0:T(8,128)(2,1)}), bf16[4,4,256,512]{3,2,1,0:T(8,128)(2,1)}, u32[]{:S(2)}, u32[]{:S(2)}) async-start(bf16[4,4,256,512]{3,2,1,0:T(8,128)(2,1)} %broadcast_in_dim.21), calls=%async_computation.2 | async-start | bytes 8388608 | tf_op jit(solution)/shard_map/weight_gather/all_to_all | solution.py:65
  56.2 3.3 %reshape.195 = bf16[64,2,4,4,2,256]{5,4,3,2,1,0:T(2,128)(2,1)S(1)} reshape(bf16[64,2,8192]{2,1,0:T(2,128)(2,1)} %param.2) | data formatting | bytes 4194304 | tf_op jit(solution)/shard_map/embeds_order/reshape | solution.py:132
  59.5 4.8 %fusion.39 = (bf16[64,2,4,4,1,256]{5,4,3,2,1,0:T(2,128)(2,1)S(1)}, bf16[64,2,4,4,1,256]{5,4,3,2,1,0:T(2,128)(2,1)S(1)}) fusion(bf16[64,2,4,4,2,256]{5,4,3,2,1,0:T(2,128)(2,1)S(1)} %reshape.195), kind=kLoop, calls=%fused_computation.111 | loop fusion | bytes 4194304 | tf_op jit(solution)/shard_map/embeds_order/slice | solution.py:134
  64.4 2.2 broadcast_select_fusion.3
  66.6 0.8 copy.38
  67.4 1.6 select_n.106
  69.0 3.1 %collective-permute-start = (bf16[128,4096]{1,0:T(8,128)(2,1)}, bf16[128,4096]{1,0:T(8,128)(2,1)}, u32[]{:S(2)}, u32[]{:S(2)}) collective-permute-start(bf16[128,4096]{1,0:T(8,128)(2,1)} %select_n.106), channel_id=1, source_target_pairs={{0,16},{16,0},{1,17},{17,1},{2,18},{18,2},{3,19},{19,3},{4,20},{20... | collective-permute-start | bytes 3145736 | tf_op jit(solution)/shard_map/embeds_order/ppermute | solution.py:118
  72.2 0.8 copy.36
  73.0 0.8 select_n.100
  73.8 1.0 collective-permute-done
  74.8 8.1 %all-to-all-done.2 = bf16[4,4,256,512]{3,2,1,0:T(8,128)(2,1)} async-done(((bf16[4,4,256,512]{3,2,1,0:T(8,128)(2,1)}), bf16[4,4,256,512]{3,2,1,0:T(8,128)(2,1)}, u32[]{:S(2)}, u32[]{:S(2)}) %all-to-all-start.2) | async-done | bytes 4194336 | tf_op jit(solution)/shard_map/weight_gather/all_to_all | solution.py:65
  83.0 3.2 %fusion.43 = f32[128,512]{1,0:T(8,128)S(1)} fusion(bf16[128,4096]{1,0:T(8,128)(2,1)} %collective-permute-done, bf16[4096,512]{1,0:T(8,128)(2,1)} %bitcast.7), kind=kOutput, calls=%fused_computation.115 | convolution fusion | flops 536870912 | bytes 5505024 | tf_op jit(solution)/shard_map/project/dot_general | solution.py:139
  86.2 2.9 %fusion.42 = f32[128,512]{1,0:T(8,128)S(1)} fusion(bf16[128,4096]{1,0:T(8,128)(2,1)S(1)} %select_n.100, bf16[4096,512]{1,0:T(8,128)(2,1)} %bitcast.7), kind=kOutput, calls=%fused_computation.114 | convolution fusion | flops 536870912 | bytes 5505024 | tf_op jit(solution)/shard_map/project/dot_general | solution.py:138
  89.2 4.0 %collective-permute-start.1 = (f32[128,512]{1,0:T(8,128)S(1)}, f32[128,512]{1,0:T(8,128)S(1)}, u32[]{:S(2)}, u32[]{:S(2)}) collective-permute-start(f32[128,512]{1,0:T(8,128)S(1)} %pad_maximum_fusion.3), channel_id=1, source_target_pairs={{0,16},{16,0},{1,17},{17,1},{2,18},{18,2},{3,19},{19,3},{4,20},{20... | collective-permute-start | bytes 786440 | tf_op jit(solution)/shard_map/project/ppermute | solution.py:118
  93.2 1.1 collective-permute-done.1
  94.8 1.6 broadcast_in_dim.22
  96.4 3.7 %all-to-all-start.3 = ((bf16[16,144,512]{2,1,0:T(8,128)(2,1)}), bf16[16,144,512]{2,1,0:T(8,128)(2,1)S(1)}, u32[]{:S(2)}, u32[]{:S(2)}) async-start(bf16[16,144,512]{2,1,0:T(8,128)(2,1)} %broadcast_in_dim.22), calls=%async_computation.3 | async-start | bytes 4718592 | tf_op jit(solution)/shard_map/project_gather/all_to_all | solution.py:25
  100.2 2.3 collective-permute-start.2
  102.5 34.4 %all-to-all-done.3.got_ref = bf16[16,144,512]{2,1,0:T(8,128)(2,1)S(1)} async-done(((bf16[16,144,512]{2,1,0:T(8,128)(2,1)}), bf16[16,144,512]{2,1,0:T(8,128)(2,1)S(1)}, u32[]{:S(2)}, u32[]{:S(2)}) %all-to-all-start.3) | async-done | bytes 2359328 | tf_op jit(solution)/shard_map/project_gather/all_to_all | solution.py:25
  137.0 0.7 multiply_reduce_fusion
  137.8 0.6 fusion
  138.7 0.4 fusion.1
  139.1 0.4 fusion.2
  139.9 5.4 %all_to_all.52 = bf16[2,2048,128]{2,1,0:T(8,128)(2,1)S(1)} all-to-all(bf16[2,2048,128]{2,1,0:T(8,128)(2,1)S(1)} %pad_maximum_fusion), channel_id=1, replica_groups=mesh['y'=4,'x'=4,'core'=2,'z1'=4,'z0'=4] {'core'}, dimensions={0} | all-to-all | bytes 2097152 | tf_op jit(solution)/shard_map/gram_core/all_to_all | solution.py:25
  145.3 1.1 reduce_sum.156
  146.4 1.1 pad_maximum_fusion.1
  147.5 18.5 %all_to_all.53 = bf16[4,528,128]{2,1,0:T(8,128)(2,1)S(1)} all-to-all(bf16[4,528,128]{2,1,0:T(8,128)(2,1)S(1)} %pad_maximum_fusion.1), channel_id=1, replica_groups=mesh['y'=4,'x'=4,'core'=2,'z1'=4,'z0'=4] {'z0'}, dimensions={0} | all-to-all | bytes 1081344 | tf_op jit(solution)/shard_map/gram_reduce/all_to_all | solution.py:25
  166.3 25.4 %all_to_all.54 = bf16[4,144,128]{2,1,0:T(8,128)(2,1)S(1)} all-to-all(bf16[4,144,128]{2,1,0:T(8,128)(2,1)S(1)} %pad_maximum_fusion.4), channel_id=1, replica_groups=mesh['y'=4,'x'=4,'core'=2,'z1'=4,'z0'=4] {'z1'}, dimensions={0} | all-to-all | bytes 294912 | tf_op jit(solution)/shard_map/gram_reduce/all_to_all | solution.py:25
  191.8 15.4 %all_to_all.55 = bf16[4,128,128]{2,1,0:T(8,128)(2,1)S(1)} all-to-all(bf16[4,128,128]{2,1,0:T(8,128)(2,1)S(1)} %broadcast_in_dim.25), channel_id=1, replica_groups=mesh['y'=4,'x'=4,'core'=2,'z1'=4,'z0'=4] {'z1'}, dimensions={0} | all-to-all | bytes 262144 | tf_op jit(solution)/shard_map/gram_gather/all_to_all | solution.py:25
  207.3 13.3 %all_to_all.56 = bf16[4,4,128,128]{3,2,1,0:T(8,128)(2,1)S(1)} all-to-all(bf16[4,4,128,128]{3,2,1,0:T(8,128)(2,1)S(1)} %broadcast_in_dim.26), channel_id=1, replica_groups=mesh['y'=4,'x'=4,'core'=2,'z1'=4,'z0'=4] {'z0'}, dimensions={0} | all-to-all | bytes 1048576 | tf_op jit(solution)/shard_map/gram_gather/all_to_all | solution.py:25
  220.5 7.5 %collective-permute-start.3 = (bf16[2048,128]{1,0:T(8,128)(2,1)S(1)}, bf16[2048,128]{1,0:T(8,128)(2,1)S(1)}, u32[]{:S(2)}, u32[]{:S(2)}) collective-permute-start(bf16[2048,128]{1,0:T(8,128)(2,1)S(1)} %bitcast.65), channel_id=1, source_target_pairs={{0,16},{16,0},{1,17},{17,1},{2,18},{18,2},{3,19},{19,3},{4,20},{20... | collective-permute-start | bytes 1572872 | tf_op jit(solution)/shard_map/gram_gather/ppermute | solution.py:118
  228.1 1.9 collective-permute-start.4
  230.0 1.1 collective-permute-done.4
  233.4 34.3 %all_to_all.57.back_ref = bf16[16,144,512]{2,1,0:T(8,128)(2,1)S(1)} all-to-all(bf16[16,144,512]{2,1,0:T(8,128)(2,1)S(1)} %broadcast_in_dim.27), channel_id=1, replica_groups=mesh['y'=4,'x'=4,'core'=2,'z1'=4,'z0'=4] {'y','x'}, dimensions={0} | all-to-all | bytes 4718592 | tf_op jit(solution)/shard_map/back_gather/all_to_all | solution.py:25
  267.7 3.7 %grad.1 = bf16[2048,512]{1,0:T(8,128)(2,1)} custom-call(bf16[16,144,512]{2,1,0:T(8,128)(2,1)S(1)} %all_to_all.57.back_ref, bf16[16,144,512]{2,1,0:T(8,128)(2,1)S(1)} %all-to-all-done.3.got_ref, f32[16,512]{1,0:T(8,128)S(1)} %broadcast_subtract_fusion.shift_ref, f32[1,512]{1,0:T(1,128)S(1)} %bitcast.60, f32[1,512]{1,0:T(1,128)S(1)} %bitcast.61), custom_call_target="tpu_custom_call" | custom-call | flops 20971520 | bytes 8388608 | tf_op jit(solution)/shard_map/grad/grad/pallas_call | solution.py:218
  271.4 3.2 %collective-permute-start.5 = (bf16[2048,512]{1,0:T(8,128)(2,1)}, bf16[2048,512]{1,0:T(8,128)(2,1)S(1)}, u32[]{:S(2)}, u32[]{:S(2)}) collective-permute-start(bf16[2048,512]{1,0:T(8,128)(2,1)} %grad.1), channel_id=1, source_target_pairs={{0,16},{16,0},{1,17},{17,1},{2,18},{18,2},{3,19},{19,3},{4,20},{20... | collective-permute-start | bytes 6291464 | tf_op jit(solution)/shard_map/grad_swap/ppermute | solution.py:118
  274.6 0.6 reduce_sum.164
  275.2 1.4 convert_reduce_fusion.4
  277.9 2.1 fusion.11
  280.0 1.8 fusion.8
  281.8 0.6 convolution_add_fusion
  282.4 1.8 broadcast_select_fusion.11
  284.2 1.0 copy.39
  (68 shorter events, 4.2 us)
Async XLA Ops:
  8.8 27.4 %copy-start.5 = (bf16[256,512]{1,0:T(8,128)(2,1)S(1)}, bf16[256,512]{1,0:T(8,128)(2,1)}, u32[]{:S(2)}) copy-start(bf16[256,512]{1,0:T(8,128)(2,1)} %param.3) | copy-start | bytes 786436
  36.2 64.0 %copy-start.3 = (bf16[32,64,256]{2,1,0:T(8,128)(2,1)}, bf16[32,64,256]{2,1,0:T(8,128)(2,1)S(1)}, u32[]{:S(2)}) copy-start(bf16[32,64,256]{2,1,0:T(8,128)(2,1)S(1)} %all_to_all.50) | copy-start | bytes 3145732
  51.1 31.8 %all-to-all-start.2 = ((bf16[4,4,256,512]{3,2,1,0:T(8,128)(2,1)}), bf16[4,4,256,512]{3,2,1,0:T(8,128)(2,1)}, u32[]{:S(2)}, u32[]{:S(2)}) async-start(bf16[4,4,256,512]{3,2,1,0:T(8,128)(2,1)} %broadcast_in_dim.21), calls=%async_computation.2 | async-start | bytes 8388608 | tf_op jit(solution)/shard_map/weight_gather/all_to_all | solution.py:65
  69.0 5.8 %collective-permute-start = (bf16[128,4096]{1,0:T(8,128)(2,1)}, bf16[128,4096]{1,0:T(8,128)(2,1)}, u32[]{:S(2)}, u32[]{:S(2)}) collective-permute-start(bf16[128,4096]{1,0:T(8,128)(2,1)} %select_n.106), channel_id=1, source_target_pairs={{0,16},{16,0},{1,17},{17,1},{2,18},{18,2},{3,19},{19,3},{4,20},{20... | collective-permute-start | bytes 3145736 | tf_op jit(solution)/shard_map/embeds_order/ppermute | solution.py:118
  89.2 5.2 %collective-permute-start.1 = (f32[128,512]{1,0:T(8,128)S(1)}, f32[128,512]{1,0:T(8,128)S(1)}, u32[]{:S(2)}, u32[]{:S(2)}) collective-permute-start(f32[128,512]{1,0:T(8,128)S(1)} %pad_maximum_fusion.3), channel_id=1, source_target_pairs={{0,16},{16,0},{1,17},{17,1},{2,18},{18,2},{3,19},{19,3},{4,20},{20... | collective-permute-start | bytes 786440 | tf_op jit(solution)/shard_map/project/ppermute | solution.py:118
  96.4 40.5 %all-to-all-start.3 = ((bf16[16,144,512]{2,1,0:T(8,128)(2,1)}), bf16[16,144,512]{2,1,0:T(8,128)(2,1)S(1)}, u32[]{:S(2)}, u32[]{:S(2)}) async-start(bf16[16,144,512]{2,1,0:T(8,128)(2,1)} %broadcast_in_dim.22), calls=%async_computation.3 | async-start | bytes 4718592 | tf_op jit(solution)/shard_map/project_gather/all_to_all | solution.py:25
  100.2 39.7 %collective-permute-start.2 = (bf16[2048,256]{1,0:T(8,128)(2,1)S(1)}, bf16[2048,256]{1,0:T(8,128)(2,1)}, u32[]{:S(2)}, u32[]{:S(2)}) collective-permute-start(bf16[2048,256]{1,0:T(8,128)(2,1)S(1)} %bitcast.66), channel_id=1, source_target_pairs={{0,1},{1,0},{2,3},{3,2},{4,5},{5,4},{6,7},{7,6},{8,9},{9,8},{10,11... | collective-permute-start | bytes 3145736 | tf_op jit(solution)/shard_map/embeds_exchange/ppermute | solution.py:126
  138.3 1.4 copy-start.1
  191.7 39.7 %copy-start.2 = (bf16[2048,512]{1,0:T(8,128)(2,1)S(1)}, bf16[2048,512]{1,0:T(8,128)(2,1)}, u32[]{:S(2)}) copy-start(bf16[2048,512]{1,0:T(8,128)(2,1)} %copy-done.1) | copy-start | bytes 6291460
  220.5 10.5 %collective-permute-start.3 = (bf16[2048,128]{1,0:T(8,128)(2,1)S(1)}, bf16[2048,128]{1,0:T(8,128)(2,1)S(1)}, u32[]{:S(2)}, u32[]{:S(2)}) collective-permute-start(bf16[2048,128]{1,0:T(8,128)(2,1)S(1)} %bitcast.65), channel_id=1, source_target_pairs={{0,16},{16,0},{1,17},{17,1},{2,18},{18,2},{3,19},{19,3},{4,20},{20... | collective-permute-start | bytes 1572872 | tf_op jit(solution)/shard_map/gram_gather/ppermute | solution.py:118
  228.1 3.0 %collective-permute-start.4 = (f32[128]{0:T(128)S(1)}, f32[128]{0:T(128)S(1)}, u32[]{:S(2)}, u32[]{:S(2)}) collective-permute-start(f32[128]{0:T(128)S(1)} %slice_reduce_fusion), channel_id=1, source_target_pairs={{0,16},{16,0},{1,17},{17,1},{2,18},{18,2},{3,19},{19,3},{4,20},{20... | collective-permute-start | bytes 1544 | tf_op jit(solution)/shard_map/back/ppermute | solution.py:118
  267.7 3.7 %copy-start = (bf16[16,144,512]{2,1,0:T(8,128)(2,1)}, bf16[16,144,512]{2,1,0:T(8,128)(2,1)S(1)}, u32[]{:S(2)}) copy-start(bf16[16,144,512]{2,1,0:T(8,128)(2,1)S(1)} %all_to_all.57.back_ref) | copy-start | bytes 7077892
  267.7 10.2 %copy-start.4 = (bf16[32,64,256]{2,1,0:T(8,128)(2,1)S(1)}, bf16[32,64,256]{2,1,0:T(8,128)(2,1)}, u32[]{:S(2)}) copy-start(bf16[32,64,256]{2,1,0:T(8,128)(2,1)} %copy-done.3) | copy-start | bytes 3145732
  271.4 8.6 %collective-permute-start.5 = (bf16[2048,512]{1,0:T(8,128)(2,1)}, bf16[2048,512]{1,0:T(8,128)(2,1)S(1)}, u32[]{:S(2)}, u32[]{:S(2)}) collective-permute-start(bf16[2048,512]{1,0:T(8,128)(2,1)} %grad.1), channel_id=1, source_target_pairs={{0,16},{16,0},{1,17},{17,1},{2,18},{18,2},{3,19},{19,3},{4,20},{20... | collective-permute-start | bytes 6291464 | tf_op jit(solution)/shard_map/grad_swap/ppermute | solution.py:118

commit v6 on v5

--- a/solution.py
+++ b/solution.py
@@ -18,7 +18,7 @@
 PLANE = ("y", "x")
 BATCH = ("y", "x", "core")
 FEAT = ("z1", "z0")
-PAD = 16
+PAD = 8
 
 
 def exchange(blocks, axes):
@@ -51,6 +51,15 @@
     return lax.dot_general(high, view, rows, preferred_element_type=F32) + lax.dot_general(
         low, view, rows, preferred_element_type=F32
     )
+
+
+def with_rows(main, rows):
+    n = main.shape[0]
+    index = lax.broadcasted_iota(jnp.int32, (n + PAD, 1), 0)
+    main = jnp.pad(main, ((0, PAD), (0, 0)))
+    for i, row in enumerate(rows):
+        main = jnp.where(index == n + i, row[None, :], main)
+    return main
 
 
 def ring_groups():
@@ -95,6 +104,56 @@
         return carry
 
     lax.fori_loop(0, n_chip, second, 0)
+
+
+def project_kernel(place_ref, own_ref, other_ref, weight_ref, kept_ref, sent_ref):
+    rows = jnp.concatenate([own_ref[...], other_ref[...]], axis=0)
+    both = jnp.dot(rows, weight_ref[...], preferred_element_type=F32)
+    n, half = both.shape[0] // 4, both.shape[1] // 2
+    first = place_ref[0] == 0
+    for owner in range(2):
+        a = both[2 * owner * n : (2 * owner + 1) * n, :]
+        b = both[(2 * owner + 1) * n : (2 * owner + 2) * n, :]
+        low = jnp.concatenate([a[:, :half], b[:, :half]], axis=1)
+        high = jnp.concatenate([a[:, half:], b[:, half:]], axis=1)
+        kept_ref[owner * n : (owner + 1) * n, :] = jnp.where(first, low, high)
+        sent_ref[owner * n : (owner + 1) * n, :] = jnp.where(first, high, low)
+
+
+def half_grad(odd, one_ref, other_ref, grad_ref, store):
+    half = grad_ref.shape[1] // 2
+
+    def product(a_ref, b_ref):
+        return jnp.dot(a_ref[...], grad_ref[:, :half], preferred_element_type=F32) + jnp.dot(
+            b_ref[...], grad_ref[:, half:], preferred_element_type=F32
+        )
+
+    @pl.when(odd == 0)
+    def _():
+        store(product(one_ref, other_ref))
+
+    @pl.when(odd != 0)
+    def _():
+        store(product(other_ref, one_ref))
+
+
+def own_half_kernel(place_ref, one_ref, other_ref, grad_ref, out_ref):
+    def store(value):
+        out_ref[...] = value
+
+    half_grad(place_ref[1], one_ref, other_ref, grad_ref, store)
+
+
+def other_half_kernel(place_ref, one_ref, other_ref, grad_ref, mine_ref, out_ref):
+    first = place_ref[0] == 0
+    half = mine_ref.shape[1]
+
+    def store(value):
+        mine = mine_ref[...]
+        out_ref[:, :half] = jnp.where(first, mine, value)
+        out_ref[:, half:] = jnp.where(first, value, mine)
+
+    half_grad(place_ref[1], one_ref, other_ref, grad_ref, store)
 
 
 def body(embeds, weight):
@@ -117,9 +176,15 @@
     def swap_core(a):
         return lax.ppermute(a, "core", [(0, 1), (1, 0)])
 
+    odd = lax.axis_index("z0") % 2
+    place = jnp.stack([core, odd]).astype(jnp.int32)
+    vmem = pl.BlockSpec(memory_space=pltpu.VMEM)
+    smem = pl.BlockSpec(memory_space=pltpu.SMEM)
+    params = pltpu.CompilerParams(vmem_limit_bytes=32 * 1024 * 1024)
+
     with jax.named_scope("embeds_exchange"):
-        odd = lax.axis_index("z0") % 2
-        one_view = lax.dynamic_index_in_dim(embeds, odd, 1, keepdims=False)
+        by_view = lax.optimization_barrier(embeds.transpose(1, 0, 2).reshape(2 * local_rows, d_in))
+        one_view = lax.dynamic_slice_in_dim(by_view, odd * local_rows, local_rows, axis=0)
         one_view = one_view.reshape(local_rows, n_batch, depth).transpose(1, 0, 2)
         one_view = exchange(one_view, BATCH).reshape(n_rows, depth)
         weight, one_view = lax.optimization_barrier((weight, one_view))
@@ -129,30 +194,28 @@
         row_weight = ring_gather(weight, first_groups)
         core_weight = ring_gather(row_weight, second_groups).reshape(n_chip * depth, width_out)
     with jax.named_scope("embeds_order"):
-        by_core = embeds.reshape(local_rows, 2, 4, n_chip // 4, 2, depth)
-        rows_zero = by_core[:, :, :, :, 0].transpose(1, 0, 2, 3, 4).reshape(2 * local_rows, n_chip * depth)
-        rows_one = by_core[:, :, :, :, 1].transpose(1, 0, 3, 2, 4).reshape(2 * local_rows, n_chip * depth)
+        by_core = by_view.reshape(2 * local_rows, 4, n_chip // 4, 2, depth)
+        rows_zero = by_core[:, :, :, 0].reshape(2 * local_rows, n_chip * depth)
+        rows_one = by_core[:, :, :, 1].transpose(0, 2, 1, 3).reshape(2 * local_rows, n_chip * depth)
         own_rows = jnp.where(first, rows_zero, rows_one)
         other_rows = swap_core(jnp.where(first, rows_one, rows_zero))
     with jax.named_scope("project"):
-        own = jnp.dot(own_rows, core_weight, preferred_element_type=F32)
-        other = jnp.dot(other_rows, core_weight, preferred_element_type=F32)
-        def by_half(p):
-            a, b = p[:local_rows], p[local_rows:]
-            low = jnp.concatenate([a[:, :half], b[:, :half]], axis=1)
-            high = jnp.concatenate([a[:, half:], b[:, half:]], axis=1)
-            return jnp.where(first, low, high), jnp.where(first, high, low)
-
-        own_kept, own_sent = by_half(own)
-        other_kept, other_sent = by_half(other)
-        got_other, got_own = jnp.split(swap_core(jnp.concatenate([own_sent, other_sent])), 2)
-        projected = in_core_order(own_kept + got_own, other_kept + got_other, 0)
+        kept, sent = pl.pallas_call(
+            project_kernel,
+            out_shape=[jax.ShapeDtypeStruct((2 * local_rows, width_out), F32)] * 2,
+            in_specs=[smem] + [vmem] * 3,
+            out_specs=[vmem, vmem],
+            compiler_params=params,
+            name="project",
+        )(place, own_rows, other_rows, core_weight)
+        got_other, got_own = jnp.split(swap_core(sent), 2)
+        own, other = jnp.split(kept, 2)
+        projected = in_core_order(own + got_own, other + got_other, 0)
     with jax.named_scope("project_gather"):
         chip_mean = jnp.sum(projected, axis=0) / chip_rows
-        block = jnp.concatenate(
-            [(projected - chip_mean).astype(BF16), pad_rows(pieces(chip_mean), width_out)], axis=0
-        )
+        block = with_rows((projected - chip_mean).astype(BF16), pieces(chip_mean))
         got = gather(block, PLANE)
+        one_t, other_t = one_view.T, other_one.T
     with jax.named_scope("standardize"):
         chip_means = jnp.sum(got[:, chip_rows : chip_rows + 3].astype(F32), axis=1)
         row_mean = jnp.sum(chip_means, axis=0) / n_chip
@@ -175,11 +238,13 @@
         part_a = lax.dot_general(view_a, mine[:, :half], contract, preferred_element_type=F32)
         part_b = lax.dot_general(view_b, mine[:, half:], contract, preferred_element_type=F32)
         parts = jnp.stack([part_a.astype(BF16), part_b.astype(BF16)])
-        extra = pad_rows(pieces(diag_local), chip_rows)
         weight_diag = 2.0 * ((1.0 - off_weight) * diagonal - 1.0)
         factor = loss_scale / n_rows * jnp.concatenate([weight_diag, weight_diag])
-        parts, extra, factor, inverse, other_one = lax.optimization_barrier((parts, extra, factor, inverse, other_one))
+        parts, diag_local, factor, inverse, one_t, other_t = lax.optimization_barrier(
+            (parts, diag_local, factor, inverse, one_t, other_t)
+        )
     with jax.named_scope("gram_core"):
+        extra = pad_rows(pieces(diag_local + swap_core(diag_local)), chip_rows)
         parts = jnp.sum(exchange(parts, "core").astype(F32), axis=0)
     with jax.named_scope("gram_reduce"):
         parts = parts.astype(BF16).reshape(n_near, n_rows // n_near, chip_rows)
@@ -192,21 +257,20 @@
         got_z = exchange(jnp.concatenate([parts, extra], axis=1), "z1")
         summed = jnp.sum(got_z.astype(F32), axis=0)
         gram_block = summed[: n_rows // n_feat].astype(BF16)
-        diag_core = jnp.sum(summed[n_rows // n_feat :], axis=0)
-        gram_block, diag_core = lax.optimization_barrier((gram_block, diag_core))
+        diag_terms = jnp.sum(summed[n_rows // n_feat :], axis=0)
+        gram_block, diag_terms = lax.optimization_barrier((gram_block, diag_terms))
     with jax.named_scope("gram_gather"):
         gram_t = gather(gather(gram_block, "z1"), "z0").reshape(n_rows, chip_rows)
-        other_t = swap_core(gram_t)
-        gram_a = jnp.where(first, gram_t, other_t).astype(F32)
-        gram_b = jnp.where(first, other_t, gram_t).astype(F32)
+        other_gram = swap_core(gram_t)
+        gram_a = jnp.where(first, gram_t, other_gram).astype(F32)
+        gram_b = jnp.where(first, other_gram, gram_t).astype(F32)
     with jax.named_scope("back"):
         off_local = jnp.sum(gram_a * gram_b, axis=0)
         back_a = split_product(gram_b, view_a)
         back_b = split_product(gram_a, view_b)
         back = jnp.concatenate([back_a, back_b], axis=1).astype(BF16)
         terms = jnp.concatenate([off_local, jnp.zeros((width_out - chip_rows,), F32)])
-        block = jnp.concatenate([back, pad_rows(pieces(terms), width_out)], axis=0)
-        block, diag_terms = lax.optimization_barrier((block, diag_core + swap_core(diag_core)))
+        block = with_rows(back, pieces(terms))
     with jax.named_scope("back_gather"):
         got_back = gather(block, PLANE)
     with jax.named_scope("grad"):
@@ -214,28 +278,35 @@
         diag_total = jnp.sum(diag_terms)
         loss_value = (off_weight * off_total + diag_total) / D_OUT
         scale_off = 2.0 * off_weight / (n_rows * n_rows)
-        vmem = pl.BlockSpec(memory_space=pltpu.VMEM)
         grad_proj = pl.pallas_call(
             functools.partial(grad_kernel, n_rows, chip_rows, loss_scale * scale_off),
             out_shape=jax.ShapeDtypeStruct((n_rows, width_out), BF16),
             in_specs=[vmem] * 5,
             out_specs=vmem,
             scratch_shapes=[pltpu.VMEM((n_rows, width_out), F32)] * 2,
-            compiler_params=pltpu.CompilerParams(vmem_limit_bytes=32 * 1024 * 1024),
+            compiler_params=params,
             cost_estimate=pl.CostEstimate(flops=20 * n_rows * width_out, bytes_accessed=8 * n_rows * width_out, transcendentals=0),
             name="grad",
         )(got_back, got, shift, inverse[None], factor[None])
     with jax.named_scope("grad_swap"):
         other_proj = swap_core(grad_proj)
     with jax.named_scope("weight_grad"):
-        embeds_a = jnp.where(odd == 0, one_view, other_one)
-        embeds_b = jnp.where(odd == 0, other_one, one_view)
-        def half_grad(g):
-            rows = (((0,), (0,)), ((), ()))
-            return lax.dot_general(embeds_a, g[:, :half], rows, preferred_element_type=F32) + lax.dot_general(
-                embeds_b, g[:, half:], rows, preferred_element_type=F32
-            )
-        grad_weight = in_core_order(half_grad(grad_proj), half_grad(other_proj), 1)
+        mine = pl.pallas_call(
+            own_half_kernel,
+            out_shape=jax.ShapeDtypeStruct((depth, half), F32),
+            in_specs=[smem] + [vmem] * 3,
+            out_specs=vmem,
+            compiler_params=params,
+            name="own_half",
+        )(place, one_t, other_t, grad_proj)
+        grad_weight = pl.pallas_call(
+            other_half_kernel,
+            out_shape=jax.ShapeDtypeStruct((depth, width_out), F32),
+            in_specs=[smem] + [vmem] * 4,
+            out_specs=vmem,
+            compiler_params=params,
+            name="other_half",
+        )(place, one_t, other_t, other_proj, mine)
     return (loss_value, grad_weight)
 
 

time: 287 us -> 276 us (0.962)
  matrix products: 14.7 us -> 2.32 us
  Pallas kernels: 3.69 us -> 12.6 us
  local copies, waits for them, and re-layouts: 27 us -> 18.1 us
  blocking collectives: 152 us -> 148 us
  waiting for transfers between devices: 45.8 us -> 49 us
    dot_general x6 -> x0, matrix products: 12.4 us -> none  [the longest x2 3.88 us: half_grad(): lax.dot_general(embeds_b, g[:, half:], rows, preferred_element_type=F32)]
    pallas_call x0 -> x3, Pallas kernels: none -> 8.94 us  [the longest x1 3.47 us: body(): pl.pallas_call(project_kernel, out_shape=[jax.ShapeDtypeStruct((2 * local...]
    dynamic_slice x1, local copies, waits for them, and re-layouts: 7.85 us -> 0.08 us  [body(): lax.dynamic_slice_in_dim(by_view, odd * local_rows, local_rows, axis=0)]
    slice x3 -> x0, local copies, waits for them, and re-layouts: 4.88 us -> none  [the longest x1 4.84 us: body(): by_core[:, :, :, :, 1].transpose(1, 0, 3, 2, 4)]
    all_to_all x1, waiting for transfers between devices: 8.15 us -> 12.9 us  [ring_gather(): lax.all_to_all(blocks, BATCH, split_axis=0, concat_axis=0, tiled=True, ax...]
    select_n x4 -> x0, local copies, waits for them, and re-layouts: 4.04 us -> none  [the longest x2 2.42 us: body(): other_rows = swap_core(jnp.where(first, rows_one, rows_zero))]
    optimization_barrier x0 -> x2, local copies, waits for them, and re-layouts: none -> 3.99 us  [the longest x1 2.5 us: body(): lax.optimization_barrier(embeds.transpose(1, 0, 2).reshape(2 * local_rows...]
    transpose x0 -> x2, local copies, waits for them, and re-layouts: none -> 3.67 us  [body(): by_core[:, :, :, 1].transpose(0, 2, 1, 3)]
  transfers between devices with their start and end apart: 8 -> 8, of which waited for: 5 -> 5; matrix products, arithmetic and copies ran while one was open for 7% -> 6% of each run, Pallas kernels for 0% -> 1%
where the time goes in v6:
time: 276 us; the launch traced here: 275 us
  blocking collectives  148 us (54%)
  waiting for transfers between devices  49 us (18%)
  starting transfers between devices  32.8 us (12%)
  local copies, waits for them, and re-layouts  18.1 us (7%)
  Pallas kernels  12.6 us (5%)
  other arithmetic  8.5 us (3%)
  between operations  3.47 us (1%)
    all_to_all x7, blocking collectives, exchange(): return lax.all_to_all(blocks, axes, split_axis=0, concat_axis=0, tiled=True)  136 us
    all_to_all x1, waiting for transfers between devices, exchange(): return lax.all_to_all(blocks, axes, split_axis=0, concat_axis=0, tiled=True)  31.5 us
    ppermute x5, starting transfers between devices, swap_core(): return lax.ppermute(a, 'core', [(0, 1), (1, 0)])  22.3 us
    all_to_all x1, waiting for transfers between devices, ring_gather(): lax.all_to_all(blocks, BATCH, split_axis=0, concat_axis=0, tiled=True, ax...  12.9 us
    all_to_all x1, blocking collectives, ring_gather(): lax.all_to_all(blocks, BATCH, split_axis=0, concat_axis=0, tiled=True, ax...  12.5 us
  transfers between devices with their start and end apart: 8, of which 5 were waited for; matrix products, arithmetic and copies ran while one was open for 6% of the time, Pallas kernels for 1%

profile of v6, /device:TPU:1, one launch (start us, length us, event | category | flops | bytes accessed | tf_op | source)
XLA Modules:
  0.0 274.9 jit_solution(8768549051947473860)
XLA Ops:
  0.6 2.8 %copy.19 = bf16[64,2,8192]{2,0,1:T(8,128)(2,1)S(1)} copy(bf16[64,2,8192]{2,1,0:T(2,128)(2,1)} %param.2) | data formatting | bytes 4194304 | tf_op args[0]
  3.8 0.6 copy.23
  4.4 27.5 %all_to_all.50 = bf16[32,64,256]{2,1,0:T(8,128)(2,1)} all-to-all(bf16[32,64,256]{2,1,0:T(8,128)(2,1)S(1)} %copy.23), channel_id=1, replica_groups=mesh['y'=4,'x'=4,'core'=2,'z1'=4,'z0'=4] {'y','x','core'}, dimensions={0} | all-to-all | bytes 2097152 | tf_op jit(solution)/shard_map/embeds_exchange/all_to_all | solution.py:25
  31.9 12.5 %all_to_all.51 = bf16[4,256,512]{2,1,0:T(8,128)(2,1)S(1)} all-to-all(bf16[4,256,512]{2,1,0:T(8,128)(2,1)S(1)} %broadcast_in_dim.132), channel_id=1, replica_groups={{0,32,64,96},{128,160,192,224},{256,288,320,352},{384,416,448,480},{16,..., dimensions={0} | all-to-all | bytes 2097152 | tf_op jit(solution)/shard_map/weight_gather/all_to_all | solution.py:74
  44.4 2.4 broadcast_in_dim.133
  46.8 4.9 %all-to-all-start.2 = ((bf16[4,4,256,512]{3,2,1,0:T(8,128)(2,1)}), bf16[4,4,256,512]{3,2,1,0:T(8,128)(2,1)}, u32[]{:S(2)}, u32[]{:S(2)}) async-start(bf16[4,4,256,512]{3,2,1,0:T(8,128)(2,1)} %broadcast_in_dim.133), calls=%async_computation.2 | async-start | bytes 8388608 | tf_op jit(solution)/shard_map/weight_gather/all_to_all | solution.py:74
  51.6 2.5 copy.20
  54.1 2.7 slice_bitcast_fusion
  56.8 1.0 copy.22
  57.8 0.8 reshape.154
  58.6 1.5 copy.26
  60.3 3.2 %collective-permute-start = (bf16[128,4096]{1,0:T(8,128)(2,1)S(1)}, bf16[128,4096]{1,0:T(8,128)(2,1)S(1)}, u32[]{:S(2)}, u32[]{:S(2)}) collective-permute-start(bf16[128,4096]{1,0:T(8,128)(2,1)S(1)} %get-tuple-element.39), channel_id=1, source_target_pairs={{0,16},{16,0},{1,17},{17,1},{2,18},{18,2},{3,19},{19,3},{4,20},{20... | collective-permute-start | bytes 3145736 | tf_op jit(solution)/shard_map/embeds_order/ppermute | solution.py:177
  63.5 2.2 collective-permute-done.other_ref
  65.7 12.9 %all-to-all-done.2 = bf16[4,4,256,512]{3,2,1,0:T(8,128)(2,1)} async-done(((bf16[4,4,256,512]{3,2,1,0:T(8,128)(2,1)}), bf16[4,4,256,512]{3,2,1,0:T(8,128)(2,1)}, u32[]{:S(2)}, u32[]{:S(2)}) %all-to-all-start.2) | async-done | bytes 4194336 | tf_op jit(solution)/shard_map/weight_gather/all_to_all | solution.py:74
  78.6 3.5 %project.1 = (f32[128,512]{1,0:T(8,128)S(1)}, f32[128,512]{1,0:T(8,128)S(1)}) custom-call(s32[2]{0:T(128)S(1)} %pad_add_fusion.place_ref, bf16[128,4096]{1,0:T(8,128)(2,1)S(1)} %get-tuple-element.40.own_ref, bf16[128,4096]{1,0:T(8,128)(2,1)S(1)} %collective-permute-done.other_ref, bf16[4096,512]{1,0:T(8,128)(2,1)} %bitcast.10.weight_ref), custom_call_target="tpu_custom_call" | custom-call | tf_op jit(solution)/shard_map/project/project/pallas_call | solution.py:203
  82.1 4.0 %collective-permute-start.1 = (f32[128,512]{1,0:T(8,128)S(1)}, f32[128,512]{1,0:T(8,128)S(1)}, u32[]{:S(2)}, u32[]{:S(2)}) collective-permute-start(f32[128,512]{1,0:T(8,128)S(1)} %get-tuple-element.16), channel_id=1, source_target_pairs={{0,16},{16,0},{1,17},{17,1},{2,18},{18,2},{3,19},{19,3},{4,20},{20... | collective-permute-start | bytes 786440 | tf_op jit(solution)/shard_map/project/ppermute | solution.py:177
  86.1 1.1 collective-permute-done.1
  87.5 1.5 broadcast_in_dim.139
  89.0 3.7 %all-to-all-start.3 = ((bf16[16,136,512]{2,1,0:T(8,128)(2,1)}), bf16[16,136,512]{2,1,0:T(8,128)(2,1)S(1)}, u32[]{:S(2)}, u32[]{:S(2)}) async-start(bf16[16,136,512]{2,1,0:T(8,128)(2,1)} %broadcast_in_dim.139), calls=%async_computation.3 | async-start | bytes 4456448 | tf_op jit(solution)/shard_map/project_gather/all_to_all | solution.py:25
  92.7 1.5 copy.24
  94.2 1.9 collective-permute-start.2
  96.2 31.5 %all-to-all-done.3.got_ref = bf16[16,136,512]{2,1,0:T(8,128)(2,1)S(1)} async-done(((bf16[16,136,512]{2,1,0:T(8,128)(2,1)}), bf16[16,136,512]{2,1,0:T(8,128)(2,1)S(1)}, u32[]{:S(2)}, u32[]{:S(2)}) %all-to-all-start.3) | async-done | bytes 2228256 | tf_op jit(solution)/shard_map/project_gather/all_to_all | solution.py:25
  127.8 0.7 multiply_reduce_fusion
  128.5 0.6 fusion
  129.1 0.3 multiply_reduce_fusion.1
  129.4 0.4 fusion.1
  129.9 0.4 fusion.2
  130.6 3.1 %collective-permute-start.3 = (f32[128]{0:T(128)S(1)}, f32[128]{0:T(128)S(1)}, u32[]{:S(2)}, u32[]{:S(2)}) collective-permute-start(f32[128]{0:T(128)S(1)} %slice_add_fusion.2), channel_id=1, source_target_pairs={{0,16},{16,0},{1,17},{17,1},{2,18},{18,2},{3,19},{19,3},{4,20},{20... | collective-permute-start | bytes 1544 | tf_op jit(solution)/shard_map/gram_core/ppermute | solution.py:177
  133.8 5.0 %all_to_all.52 = bf16[2,2048,128]{2,1,0:T(8,128)(2,1)} all-to-all(bf16[2,2048,128]{2,1,0:T(8,128)(2,1)S(1)} %pad_maximum_fusion), channel_id=1, replica_groups=mesh['y'=4,'x'=4,'core'=2,'z1'=4,'z0'=4] {'core'}, dimensions={0} | all-to-all | bytes 2097152 | tf_op jit(solution)/shard_map/gram_core/all_to_all | solution.py:25
  138.8 2.3 reduce_sum.150
  141.2 1.1 pad_maximum_fusion.1
  142.3 17.8 %all_to_all.53 = bf16[4,520,128]{2,1,0:T(8,128)(2,1)S(1)} all-to-all(bf16[4,520,128]{2,1,0:T(8,128)(2,1)S(1)} %pad_maximum_fusion.1), channel_id=1, replica_groups=mesh['y'=4,'x'=4,'core'=2,'z1'=4,'z0'=4] {'z0'}, dimensions={0} | all-to-all | bytes 1064960 | tf_op jit(solution)/shard_map/gram_reduce/all_to_all | solution.py:25
  160.3 25.3 %all_to_all.54 = bf16[4,136,128]{2,1,0:T(8,128)(2,1)S(1)} all-to-all(bf16[4,136,128]{2,1,0:T(8,128)(2,1)S(1)} %pad_maximum_fusion.2), channel_id=1, replica_groups=mesh['y'=4,'x'=4,'core'=2,'z1'=4,'z0'=4] {'z1'}, dimensions={0} | all-to-all | bytes 278528 | tf_op jit(solution)/shard_map/gram_reduce/all_to_all | solution.py:25
  185.8 15.5 %all_to_all.55 = bf16[4,128,128]{2,1,0:T(8,128)(2,1)S(1)} all-to-all(bf16[4,128,128]{2,1,0:T(8,128)(2,1)S(1)} %broadcast_in_dim.142), channel_id=1, replica_groups=mesh['y'=4,'x'=4,'core'=2,'z1'=4,'z0'=4] {'z1'}, dimensions={0} | all-to-all | bytes 262144 | tf_op jit(solution)/shard_map/gram_gather/all_to_all | solution.py:25
  201.4 11.8 %all_to_all.56 = bf16[4,4,128,128]{3,2,1,0:T(8,128)(2,1)S(1)} all-to-all(bf16[4,4,128,128]{3,2,1,0:T(8,128)(2,1)S(1)} %broadcast_in_dim.143), channel_id=1, replica_groups=mesh['y'=4,'x'=4,'core'=2,'z1'=4,'z0'=4] {'z0'}, dimensions={0} | all-to-all | bytes 1048576 | tf_op jit(solution)/shard_map/gram_gather/all_to_all | solution.py:25
  213.2 8.7 %collective-permute-start.4 = (bf16[2048,128]{1,0:T(8,128)(2,1)S(1)}, bf16[2048,128]{1,0:T(8,128)(2,1)S(1)}, u32[]{:S(2)}, u32[]{:S(2)}) collective-permute-start(bf16[2048,128]{1,0:T(8,128)(2,1)S(1)} %bitcast.63), channel_id=1, source_target_pairs={{0,16},{16,0},{1,17},{17,1},{2,18},{18,2},{3,19},{19,3},{4,20},{20... | collective-permute-start | bytes 1572872 | tf_op jit(solution)/shard_map/gram_gather/ppermute | solution.py:177
  221.9 1.3 collective-permute-done.4
  223.5 0.3 fusion.12
  223.9 0.4 fusion.3
  224.3 0.3 fusion.8
  224.6 0.4 fusion.4
  225.3 32.6 %all_to_all.57.back_ref = bf16[16,136,512]{2,1,0:T(8,128)(2,1)S(1)} all-to-all(bf16[16,136,512]{2,1,0:T(8,128)(2,1)S(1)} %broadcast_in_dim.147), channel_id=1, replica_groups=mesh['y'=4,'x'=4,'core'=2,'z1'=4,'z0'=4] {'y','x'}, dimensions={0} | all-to-all | bytes 4456448 | tf_op jit(solution)/shard_map/back_gather/all_to_all | solution.py:25
  257.9 3.7 %grad.1.grad_ref = bf16[2048,512]{1,0:T(8,128)(2,1)} custom-call(bf16[16,136,512]{2,1,0:T(8,128)(2,1)S(1)} %all_to_all.57.back_ref, bf16[16,136,512]{2,1,0:T(8,128)(2,1)S(1)} %all-to-all-done.3.got_ref, f32[16,512]{1,0:T(8,128)S(1)} %broadcast_subtract_fusion.shift_ref, f32[1,512]{1,0:T(1,128)S(1)} %bitcast.53, f32[1,512]{1,0:T(1,128)S(1)} %bitcast.54), custom_call_target="tpu_custom_call" | custom-call | flops 20971520 | bytes 8388608 | tf_op jit(solution)/shard_map/grad/grad/pallas_call | solution.py:281
  261.6 3.4 %collective-permute-start.5 = (bf16[2048,512]{1,0:T(8,128)(2,1)}, bf16[2048,512]{1,0:T(8,128)(2,1)S(1)}, u32[]{:S(2)}, u32[]{:S(2)}) collective-permute-start(bf16[2048,512]{1,0:T(8,128)(2,1)} %grad.1.grad_ref), channel_id=1, source_target_pairs={{0,16},{16,0},{1,17},{17,1},{2,18},{18,2},{3,19},{19,3},{4,20},{20... | collective-permute-start | bytes 6291464 | tf_op jit(solution)/shard_map/grad_swap/ppermute | solution.py:177
  265.0 0.6 reduce_sum.158
  265.6 2.7 own_half.1.mine_ref
  268.3 1.4 convert_reduce_fusion.4
  270.9 2.8 %other_half.1 = f32[256,512]{1,0:T(8,128)} custom-call(s32[2]{0:T(128)S(1)} %pad_add_fusion.place_ref, bf16[256,2048]{1,0:T(8,128)(2,1)S(1)} %bitcast.52, bf16[256,2048]{1,0:T(8,128)(2,1)} %bitcast.15.other_ref, bf16[2048,512]{1,0:T(8,128)(2,1)S(1)} %collective-permute-done.5.grad_ref, f32[256,256]{1,0:T(8,128)S(1)} %own_half.1.mine_ref), custom_call_target="tpu_custom_call" | custom-call | tf_op jit(solution)/shard_map/weight_grad/other_half/pallas_call | solution.py:302
  (52 shorter events, 2.3 us)
Async XLA Ops:
  3.8 28.1 %copy-start.3 = (bf16[256,512]{1,0:T(8,128)(2,1)S(1)}, bf16[256,512]{1,0:T(8,128)(2,1)}, u32[]{:S(2)}) copy-start(bf16[256,512]{1,0:T(8,128)(2,1)} %param.3) | copy-start | bytes 786436
  46.8 31.8 %all-to-all-start.2 = ((bf16[4,4,256,512]{3,2,1,0:T(8,128)(2,1)}), bf16[4,4,256,512]{3,2,1,0:T(8,128)(2,1)}, u32[]{:S(2)}, u32[]{:S(2)}) async-start(bf16[4,4,256,512]{3,2,1,0:T(8,128)(2,1)} %broadcast_in_dim.133), calls=%async_computation.2 | async-start | bytes 8388608 | tf_op jit(solution)/shard_map/weight_gather/all_to_all | solution.py:74
  60.3 5.4 %collective-permute-start = (bf16[128,4096]{1,0:T(8,128)(2,1)S(1)}, bf16[128,4096]{1,0:T(8,128)(2,1)S(1)}, u32[]{:S(2)}, u32[]{:S(2)}) collective-permute-start(bf16[128,4096]{1,0:T(8,128)(2,1)S(1)} %get-tuple-element.39), channel_id=1, source_target_pairs={{0,16},{16,0},{1,17},{17,1},{2,18},{18,2},{3,19},{19,3},{4,20},{20... | collective-permute-start | bytes 3145736 | tf_op jit(solution)/shard_map/embeds_order/ppermute | solution.py:177
  82.1 5.2 %collective-permute-start.1 = (f32[128,512]{1,0:T(8,128)S(1)}, f32[128,512]{1,0:T(8,128)S(1)}, u32[]{:S(2)}, u32[]{:S(2)}) collective-permute-start(f32[128,512]{1,0:T(8,128)S(1)} %get-tuple-element.16), channel_id=1, source_target_pairs={{0,16},{16,0},{1,17},{17,1},{2,18},{18,2},{3,19},{19,3},{4,20},{20... | collective-permute-start | bytes 786440 | tf_op jit(solution)/shard_map/project/ppermute | solution.py:177
  89.0 38.6 %all-to-all-start.3 = ((bf16[16,136,512]{2,1,0:T(8,128)(2,1)}), bf16[16,136,512]{2,1,0:T(8,128)(2,1)S(1)}, u32[]{:S(2)}, u32[]{:S(2)}) async-start(bf16[16,136,512]{2,1,0:T(8,128)(2,1)} %broadcast_in_dim.139), calls=%async_computation.3 | async-start | bytes 4456448 | tf_op jit(solution)/shard_map/project_gather/all_to_all | solution.py:25
  94.2 36.3 %collective-permute-start.2 = (bf16[2048,256]{0,1:T(8,128)(2,1)S(1)}, bf16[2048,256]{0,1:T(8,128)(2,1)}, u32[]{:S(2)}, u32[]{:S(2)}) collective-permute-start(bf16[2048,256]{0,1:T(8,128)(2,1)S(1)} %copy.24), channel_id=1, source_target_pairs={{0,1},{1,0},{2,3},{3,2},{4,5},{5,4},{6,7},{7,6},{8,9},{9,8},{10,11... | collective-permute-start | bytes 3145736 | tf_op jit(solution)/shard_map/embeds_exchange/ppermute | solution.py:191
  129.1 1.4 copy-start.1
  130.6 10.6 %collective-permute-start.3 = (f32[128]{0:T(128)S(1)}, f32[128]{0:T(128)S(1)}, u32[]{:S(2)}, u32[]{:S(2)}) collective-permute-start(f32[128]{0:T(128)S(1)} %slice_add_fusion.2), channel_id=1, source_target_pairs={{0,16},{16,0},{1,17},{17,1},{2,18},{18,2},{3,19},{19,3},{4,20},{20... | collective-permute-start | bytes 1544 | tf_op jit(solution)/shard_map/gram_core/ppermute | solution.py:177
  185.7 37.8 %copy-start.2 = (bf16[2048,512]{1,0:T(8,128)(2,1)S(1)}, bf16[2048,512]{1,0:T(8,128)(2,1)}, u32[]{:S(2)}) copy-start(bf16[2048,512]{1,0:T(8,128)(2,1)} %copy-done.1) | copy-start | bytes 6291460
  213.2 10.0 %collective-permute-start.4 = (bf16[2048,128]{1,0:T(8,128)(2,1)S(1)}, bf16[2048,128]{1,0:T(8,128)(2,1)S(1)}, u32[]{:S(2)}, u32[]{:S(2)}) collective-permute-start(bf16[2048,128]{1,0:T(8,128)(2,1)S(1)} %bitcast.63), channel_id=1, source_target_pairs={{0,16},{16,0},{1,17},{17,1},{2,18},{18,2},{3,19},{19,3},{4,20},{20... | collective-permute-start | bytes 1572872 | tf_op jit(solution)/shard_map/gram_gather/ppermute | solution.py:177
  257.9 3.7 %copy-start = (bf16[16,136,512]{2,1,0:T(8,128)(2,1)}, bf16[16,136,512]{2,1,0:T(8,128)(2,1)S(1)}, u32[]{:S(2)}) copy-start(bf16[16,136,512]{2,1,0:T(8,128)(2,1)S(1)} %all_to_all.57.back_ref) | copy-start | bytes 6684676
  261.6 9.4 %collective-permute-start.5 = (bf16[2048,512]{1,0:T(8,128)(2,1)}, bf16[2048,512]{1,0:T(8,128)(2,1)S(1)}, u32[]{:S(2)}, u32[]{:S(2)}) collective-permute-start(bf16[2048,512]{1,0:T(8,128)(2,1)} %grad.1.grad_ref), channel_id=1, source_target_pairs={{0,16},{16,0},{1,17},{17,1},{2,18},{18,2},{3,19},{19,3},{4,20},{20... | collective-permute-start | bytes 6291464 | tf_op jit(solution)/shard_map/grad_swap/ppermute | solution.py:177

commit v7 on v6

--- a/solution.py
+++ b/solution.py
@@ -74,7 +74,7 @@
     return lax.all_to_all(blocks, BATCH, split_axis=0, concat_axis=0, tiled=True, axis_index_groups=groups)
 
 
-def grad_kernel(n_rows, chip_rows, scale, back_ref, got_ref, shift_ref, inv_ref, cross_ref, out_ref, grad_ref, std_ref):
+def grad_kernel(n_rows, chip_rows, scale, back_ref, got_ref, shift_ref, inv_ref, cross_ref, diag_ref, out_ref, loss_ref, grad_ref, std_ref):
     n_chip, _, width = got_ref.shape
     half = width // 2
     inv, factor = inv_ref[...], cross_ref[...]
@@ -93,6 +93,12 @@
         std_ref[rows, :] = standard
         return sums[0] + fold(grad), sums[1] + fold(grad * standard)
 
+    off_terms = jnp.zeros((1, chip_rows), F32)
+    for p in range(n_chip):
+        spare = back_ref[p, chip_rows:, :chip_rows].astype(F32)
+        off_terms = off_terms + jnp.sum(spare, axis=0, keepdims=True)
+    loss_ref[0] = jnp.sum(off_weight / (n_rows * n_rows) * off_terms + diag_ref[...]) / D_OUT
+
     zero = jnp.zeros((8, width), F32)
     total, cross = lax.fori_loop(0, n_chip, first, (zero, zero))
     grad_mean = jnp.sum(total, axis=0, keepdims=True) / n_rows
@@ -104,6 +110,26 @@
         return carry
 
     lax.fori_loop(0, n_chip, second, 0)
+
+
+def order_kernel(place_ref, rows_ref, own_ref, sent_ref):
+    depth = rows_ref.shape[1] // 32
+
+    def pick(core, out_ref):
+        for j in range(16):
+            chip = j if core == 0 else (j % 4) * 4 + j // 4
+            source = (2 * chip + core) * depth
+            out_ref[:, j * depth : (j + 1) * depth] = rows_ref[:, source : source + depth]
+
+    @pl.when(place_ref[0] == 0)
+    def _():
+        pick(0, own_ref)
+        pick(1, sent_ref)
+
+    @pl.when(place_ref[0] != 0)
+    def _():
+        pick(1, own_ref)
+        pick(0, sent_ref)
 
 
 def project_kernel(place_ref, own_ref, other_ref, weight_ref, kept_ref, sent_ref):
@@ -184,21 +210,26 @@
 
     with jax.named_scope("embeds_exchange"):
         by_view = lax.optimization_barrier(embeds.transpose(1, 0, 2).reshape(2 * local_rows, d_in))
-        one_view = lax.dynamic_slice_in_dim(by_view, odd * local_rows, local_rows, axis=0)
-        one_view = one_view.reshape(local_rows, n_batch, depth).transpose(1, 0, 2)
-        one_view = exchange(one_view, BATCH).reshape(n_rows, depth)
-        weight, one_view = lax.optimization_barrier((weight, one_view))
-        other_one = lax.ppermute(one_view, "z0", [(0, 1), (1, 0), (2, 3), (3, 2)])
+        upper = lax.axis_index("z0") // 2
+        part = local_rows // 2
+        quarter = lax.dynamic_slice_in_dim(by_view, (2 * odd + upper) * part, part, axis=0)
+        quarter = quarter.reshape(part, n_batch, depth).transpose(1, 0, 2)
+        quarter = exchange(quarter, BATCH)
+    with jax.named_scope("embeds_order"):
+        own_rows, sent_rows = pl.pallas_call(
+            order_kernel,
+            out_shape=[jax.ShapeDtypeStruct((2 * local_rows, n_chip * depth), BF16)] * 2,
+            in_specs=[smem, vmem],
+            out_specs=[vmem, vmem],
+            compiler_params=params,
+            name="order",
+        )(place, by_view)
+        other_rows = swap_core(sent_rows)
     with jax.named_scope("weight_gather"):
+        weight, quarter, own_rows, other_rows = lax.optimization_barrier((weight, quarter, own_rows, other_rows))
         first_groups, second_groups = ring_groups()
         row_weight = ring_gather(weight, first_groups)
         core_weight = ring_gather(row_weight, second_groups).reshape(n_chip * depth, width_out)
-    with jax.named_scope("embeds_order"):
-        by_core = by_view.reshape(2 * local_rows, 4, n_chip // 4, 2, depth)
-        rows_zero = by_core[:, :, :, 0].reshape(2 * local_rows, n_chip * depth)
-        rows_one = by_core[:, :, :, 1].transpose(0, 2, 1, 3).reshape(2 * local_rows, n_chip * depth)
-        own_rows = jnp.where(first, rows_zero, rows_one)
-        other_rows = swap_core(jnp.where(first, rows_one, rows_zero))
     with jax.named_scope("project"):
         kept, sent = pl.pallas_call(
             project_kernel,
@@ -214,8 +245,9 @@
     with jax.named_scope("project_gather"):
         chip_mean = jnp.sum(projected, axis=0) / chip_rows
         block = with_rows((projected - chip_mean).astype(BF16), pieces(chip_mean))
+        block, quarter = lax.optimization_barrier((block, quarter))
+        other_quarter = lax.ppermute(quarter, "z0", [(0, 2), (2, 0), (1, 3), (3, 1)])
         got = gather(block, PLANE)
-        one_t, other_t = one_view.T, other_one.T
     with jax.named_scope("standardize"):
         chip_means = jnp.sum(got[:, chip_rows : chip_rows + 3].astype(F32), axis=1)
         row_mean = jnp.sum(chip_means, axis=0) / n_chip
@@ -240,8 +272,8 @@
         parts = jnp.stack([part_a.astype(BF16), part_b.astype(BF16)])
         weight_diag = 2.0 * ((1.0 - off_weight) * diagonal - 1.0)
         factor = loss_scale / n_rows * jnp.concatenate([weight_diag, weight_diag])
-        parts, diag_local, factor, inverse, one_t, other_t = lax.optimization_barrier(
-            (parts, diag_local, factor, inverse, one_t, other_t)
+        parts, diag_local, factor, inverse, other_quarter = lax.optimization_barrier(
+            (parts, diag_local, factor, inverse, other_quarter)
         )
     with jax.named_scope("gram_core"):
         extra = pad_rows(pieces(diag_local + swap_core(diag_local)), chip_rows)
@@ -272,22 +304,26 @@
         terms = jnp.concatenate([off_local, jnp.zeros((width_out - chip_rows,), F32)])
         block = with_rows(back, pieces(terms))
     with jax.named_scope("back_gather"):
+        block, quarter, other_quarter = lax.optimization_barrier((block, quarter, other_quarter))
+        low = jnp.where(upper == 0, quarter, other_quarter)
+        high = jnp.where(upper == 0, other_quarter, quarter)
+        one_t = jnp.concatenate([low, high], axis=1).reshape(n_rows, depth).T
+        other_t = lax.ppermute(one_t, "z0", [(0, 1), (1, 0), (2, 3), (3, 2)])
         got_back = gather(block, PLANE)
+        got_back, one_t, other_t = lax.optimization_barrier((got_back, one_t, other_t))
     with jax.named_scope("grad"):
-        off_total = jnp.sum(got_back[:, chip_rows : chip_rows + 3, :chip_rows].astype(F32)) / (n_rows * n_rows)
-        diag_total = jnp.sum(diag_terms)
-        loss_value = (off_weight * off_total + diag_total) / D_OUT
         scale_off = 2.0 * off_weight / (n_rows * n_rows)
-        grad_proj = pl.pallas_call(
+        grad_proj, loss = pl.pallas_call(
             functools.partial(grad_kernel, n_rows, chip_rows, loss_scale * scale_off),
-            out_shape=jax.ShapeDtypeStruct((n_rows, width_out), BF16),
-            in_specs=[vmem] * 5,
-            out_specs=vmem,
+            out_shape=[jax.ShapeDtypeStruct((n_rows, width_out), BF16), jax.ShapeDtypeStruct((1,), F32)],
+            in_specs=[vmem] * 6,
+            out_specs=[vmem, smem],
             scratch_shapes=[pltpu.VMEM((n_rows, width_out), F32)] * 2,
             compiler_params=params,
             cost_estimate=pl.CostEstimate(flops=20 * n_rows * width_out, bytes_accessed=8 * n_rows * width_out, transcendentals=0),
             name="grad",
-        )(got_back, got, shift, inverse[None], factor[None])
+        )(got_back, got, shift, inverse[None], factor[None], diag_terms[None])
+        loss_value = loss[0]
     with jax.named_scope("grad_swap"):
         other_proj = swap_core(grad_proj)
     with jax.named_scope("weight_grad"):

time: 276 us -> 273 us (0.989)
  blocking collectives: 148 us -> 132 us
  waiting for transfers between devices: 49 us -> 65 us
  local copies, waits for them, and re-layouts: 18.1 us -> 9.54 us
  starting transfers between devices: 32.8 us -> 41.1 us
    all_to_all x7 -> x6, blocking collectives: 136 us -> 90.6 us  [exchange(): return lax.all_to_all(blocks, axes, split_axis=0, concat_axis=0, tiled=True)]
    all_to_all x1 -> x2, blocking collectives: 12.5 us -> 41.6 us  [ring_gather(): lax.all_to_all(blocks, BATCH, split_axis=0, concat_axis=0, tiled=True, ax...]
    ppermute x1 -> x2, waiting for transfers between devices: 0.01 us -> 24.4 us  [the longest x1 24.4 us: body(): other_t = lax.ppermute(one_t, 'z0', [(0, 1), (1, 0), (2, 3), (3, 2)])]
    all_to_all x1 -> x0, waiting for transfers between devices: 12.9 us -> none  [ring_gather(): lax.all_to_all(blocks, BATCH, split_axis=0, concat_axis=0, tiled=True, ax...]
    ppermute x5, starting transfers between devices: 22.3 us -> 27.8 us  [swap_core(): return lax.ppermute(a, 'core', [(0, 1), (1, 0)])]
    all_to_all x1 -> x0, starting transfers between devices: 4.86 us -> none  [ring_gather(): lax.all_to_all(blocks, BATCH, split_axis=0, concat_axis=0, tiled=True, ax...]
    all_to_all x1 -> x2, starting transfers between devices: 3.72 us -> 8.15 us  [exchange(): return lax.all_to_all(blocks, axes, split_axis=0, concat_axis=0, tiled=True)]
    all_to_all x1 -> x2, waiting for transfers between devices: 31.5 us -> 35.5 us  [exchange(): return lax.all_to_all(blocks, axes, split_axis=0, concat_axis=0, tiled=True)]
  transfers between devices with their start and end apart: 8 -> 9, of which waited for: 5 -> 6; matrix products, arithmetic and copies ran while one was open for 6% -> 3% of each run, Pallas kernels for 1% -> 0%
where the time goes in v7:
time: 273 us; the launch traced here: 272 us
  blocking collectives  132 us (48%)
  waiting for transfers between devices  65 us (24%)
  starting transfers between devices  41.1 us (15%)
  Pallas kernels  12.3 us (5%)
  local copies, waits for them, and re-layouts  9.54 us (3%)
  other arithmetic  8.65 us (3%)
    all_to_all x6, blocking collectives, exchange(): return lax.all_to_all(blocks, axes, split_axis=0, concat_axis=0, tiled=True)  90.6 us
    all_to_all x2, blocking collectives, ring_gather(): lax.all_to_all(blocks, BATCH, split_axis=0, concat_axis=0, tiled=True, ax...  41.6 us
    all_to_all x2, waiting for transfers between devices, exchange(): return lax.all_to_all(blocks, axes, split_axis=0, concat_axis=0, tiled=True)  35.5 us
    ppermute x5, starting transfers between devices, swap_core(): return lax.ppermute(a, 'core', [(0, 1), (1, 0)])  27.8 us
    ppermute x1, waiting for transfers between devices, body(): other_t = lax.ppermute(one_t, 'z0', [(0, 1), (1, 0), (2, 3), (3, 2)])  24.4 us
    all_to_all x2, starting transfers between devices, exchange(): return lax.all_to_all(blocks, axes, split_axis=0, concat_axis=0, tiled=True)  8.15 us
  transfers between devices with their start and end apart: 9, of which 6 were waited for; matrix products, arithmetic and copies ran while one was open for 3% of the time, Pallas kernels for 0%

profile of v7, /device:TPU:1, one launch (start us, length us, event | category | flops | bytes accessed | tf_op | source)
XLA Modules:
  0.0 272.2 jit_solution(661147593857713855)
XLA Ops:
  0.6 2.8 %copy.11 = bf16[2,64,8192]{2,1,0:T(8,128)(2,1)S(1)} copy(bf16[2,64,8192]{2,0,1:T(2,128)(2,1)} %bitcast.55) | data formatting | bytes 4194304 | tf_op jit(solution)/shard_map/embeds_exchange/transpose | solution.py:212
  3.5 1.7 order.1
  5.2 8.8 %collective-permute-start = (bf16[128,4096]{1,0:T(8,128)(2,1)}, bf16[128,4096]{1,0:T(8,128)(2,1)}, u32[]{:S(2)}, u32[]{:S(2)}) collective-permute-start(bf16[128,4096]{1,0:T(8,128)(2,1)} %get-tuple-element.28), channel_id=1, source_target_pairs={{0,16},{16,0},{1,17},{17,1},{2,18},{18,2},{3,19},{19,3},{4,20},{20... | collective-permute-start | bytes 3145736 | tf_op jit(solution)/shard_map/embeds_order/ppermute | solution.py:203
  14.5 15.0 %all_to_all.50 = bf16[32,32,256]{2,1,0:T(8,128)(2,1)} all-to-all(bf16[32,32,256]{2,1,0:T(8,128)(2,1)S(1)} %copy.12), channel_id=1, replica_groups=mesh['y'=4,'x'=4,'core'=2,'z1'=4,'z0'=4] {'y','x','core'}, dimensions={0} | all-to-all | bytes 1048576 | tf_op jit(solution)/shard_map/embeds_exchange/all_to_all | solution.py:25
  29.6 12.5 %all_to_all.51 = bf16[4,256,512]{2,1,0:T(8,128)(2,1)S(1)} all-to-all(bf16[4,256,512]{2,1,0:T(8,128)(2,1)S(1)} %broadcast_in_dim.135), channel_id=1, replica_groups={{0,32,64,96},{128,160,192,224},{256,288,320,352},{384,416,448,480},{16,..., dimensions={0} | all-to-all | bytes 2097152 | tf_op jit(solution)/shard_map/weight_gather/all_to_all | solution.py:74
  42.1 0.4 broadcast_in_dim.136
  42.5 29.2 %all_to_all.52 = bf16[4,4,256,512]{3,2,1,0:T(8,128)(2,1)S(1)} all-to-all(bf16[4,4,256,512]{3,2,1,0:T(8,128)(2,1)S(1)} %broadcast_in_dim.136), channel_id=1, replica_groups={{0,128,256,384},{32,160,288,416},{64,192,320,448},{96,224,352,480},{16,..., dimensions={0} | all-to-all | bytes 8388608 | tf_op jit(solution)/shard_map/weight_gather/all_to_all | solution.py:74
  71.6 2.5 project.1
  74.1 4.4 %collective-permute-start.1 = (f32[128,512]{1,0:T(8,128)S(1)}, f32[128,512]{1,0:T(8,128)S(1)}, u32[]{:S(2)}, u32[]{:S(2)}) collective-permute-start(f32[128,512]{1,0:T(8,128)S(1)} %get-tuple-element.33), channel_id=1, source_target_pairs={{0,16},{16,0},{1,17},{17,1},{2,18},{18,2},{3,19},{19,3},{4,20},{20... | collective-permute-start | bytes 786440 | tf_op jit(solution)/shard_map/project/ppermute | solution.py:203
  78.5 1.1 collective-permute-done.1
  79.9 1.5 broadcast_in_dim.142
  81.4 3.7 %all-to-all-start.3 = ((bf16[16,136,512]{2,1,0:T(8,128)(2,1)}), bf16[16,136,512]{2,1,0:T(8,128)(2,1)S(1)}, u32[]{:S(2)}, u32[]{:S(2)}) async-start(bf16[16,136,512]{2,1,0:T(8,128)(2,1)} %broadcast_in_dim.142), calls=%async_computation.3 | async-start | bytes 4456448 | tf_op jit(solution)/shard_map/project_gather/all_to_all | solution.py:25
  85.2 3.2 %collective-permute-start.2 = (bf16[32,32,256]{2,1,0:T(8,128)(2,1)}, bf16[32,32,256]{2,1,0:T(8,128)(2,1)}, u32[]{:S(2)}, u32[]{:S(2)}) collective-permute-start(bf16[32,32,256]{2,1,0:T(8,128)(2,1)} %all_to_all.50), channel_id=1, source_target_pairs={{0,2},{2,0},{1,3},{3,1},{4,6},{6,4},{5,7},{7,5},{8,10},{10,8},{9,1... | collective-permute-start | bytes 1572872 | tf_op jit(solution)/shard_map/project_gather/ppermute | solution.py:249
  88.4 31.7 %all-to-all-done.3.got_ref = bf16[16,136,512]{2,1,0:T(8,128)(2,1)S(1)} async-done(((bf16[16,136,512]{2,1,0:T(8,128)(2,1)}), bf16[16,136,512]{2,1,0:T(8,128)(2,1)S(1)}, u32[]{:S(2)}, u32[]{:S(2)}) %all-to-all-start.3) | async-done | bytes 2228256 | tf_op jit(solution)/shard_map/project_gather/all_to_all | solution.py:25
  120.2 0.7 multiply_reduce_fusion
  120.9 0.6 fusion
  121.5 0.3 multiply_reduce_fusion.1
  121.8 0.4 fusion.1
  122.2 0.4 fusion.2
  123.0 3.1 %collective-permute-start.3 = (f32[128]{0:T(128)S(1)}, f32[128]{0:T(128)S(1)}, u32[]{:S(2)}, u32[]{:S(2)}) collective-permute-start(f32[128]{0:T(128)S(1)} %slice_add_fusion.2), channel_id=1, source_target_pairs={{0,16},{16,0},{1,17},{17,1},{2,18},{18,2},{3,19},{19,3},{4,20},{20... | collective-permute-start | bytes 1544 | tf_op jit(solution)/shard_map/gram_core/ppermute | solution.py:203
  126.2 5.0 %all_to_all.53 = bf16[2,2048,128]{2,1,0:T(8,128)(2,1)} all-to-all(bf16[2,2048,128]{2,1,0:T(8,128)(2,1)S(1)} %pad_maximum_fusion), channel_id=1, replica_groups=mesh['y'=4,'x'=4,'core'=2,'z1'=4,'z0'=4] {'core'}, dimensions={0} | all-to-all | bytes 2097152 | tf_op jit(solution)/shard_map/gram_core/all_to_all | solution.py:25
  131.2 2.3 reduce_sum.132
  133.6 1.1 pad_maximum_fusion.2
  134.7 17.9 %all_to_all.54 = bf16[4,520,128]{2,1,0:T(8,128)(2,1)S(1)} all-to-all(bf16[4,520,128]{2,1,0:T(8,128)(2,1)S(1)} %pad_maximum_fusion.2), channel_id=1, replica_groups=mesh['y'=4,'x'=4,'core'=2,'z1'=4,'z0'=4] {'z0'}, dimensions={0} | all-to-all | bytes 1064960 | tf_op jit(solution)/shard_map/gram_reduce/all_to_all | solution.py:25
  152.8 25.3 %all_to_all.55 = bf16[4,136,128]{2,1,0:T(8,128)(2,1)S(1)} all-to-all(bf16[4,136,128]{2,1,0:T(8,128)(2,1)S(1)} %pad_maximum_fusion.3), channel_id=1, replica_groups=mesh['y'=4,'x'=4,'core'=2,'z1'=4,'z0'=4] {'z1'}, dimensions={0} | all-to-all | bytes 278528 | tf_op jit(solution)/shard_map/gram_reduce/all_to_all | solution.py:25
  178.3 15.5 %all_to_all.56 = bf16[4,128,128]{2,1,0:T(8,128)(2,1)S(1)} all-to-all(bf16[4,128,128]{2,1,0:T(8,128)(2,1)S(1)} %broadcast_in_dim.145), channel_id=1, replica_groups=mesh['y'=4,'x'=4,'core'=2,'z1'=4,'z0'=4] {'z1'}, dimensions={0} | all-to-all | bytes 262144 | tf_op jit(solution)/shard_map/gram_gather/all_to_all | solution.py:25
  193.9 11.8 %all_to_all.57 = bf16[4,4,128,128]{3,2,1,0:T(8,128)(2,1)S(1)} all-to-all(bf16[4,4,128,128]{3,2,1,0:T(8,128)(2,1)S(1)} %broadcast_in_dim.146), channel_id=1, replica_groups=mesh['y'=4,'x'=4,'core'=2,'z1'=4,'z0'=4] {'z0'}, dimensions={0} | all-to-all | bytes 1048576 | tf_op jit(solution)/shard_map/gram_gather/all_to_all | solution.py:25
  205.7 8.5 %collective-permute-start.4 = (bf16[2048,128]{1,0:T(8,128)(2,1)S(1)}, bf16[2048,128]{1,0:T(8,128)(2,1)S(1)}, u32[]{:S(2)}, u32[]{:S(2)}) collective-permute-start(bf16[2048,128]{1,0:T(8,128)(2,1)S(1)} %bitcast.59), channel_id=1, source_target_pairs={{0,16},{16,0},{1,17},{17,1},{2,18},{18,2},{3,19},{19,3},{4,20},{20... | collective-permute-start | bytes 1572872 | tf_op jit(solution)/shard_map/gram_gather/ppermute | solution.py:203
  214.2 1.5 collective-permute-done.4
  215.7 0.3 fusion.6
  216.1 0.3 fusion.12
  216.4 0.4 fusion.3
  216.8 0.3 fusion.8
  217.1 0.4 fusion.4
  217.7 1.5 broadcast_in_dim.150
  219.2 4.4 %all-to-all-start.9 = ((bf16[16,136,512]{2,1,0:T(8,128)(2,1)}), bf16[16,136,512]{2,1,0:T(8,128)(2,1)}, u32[]{:S(2)}, u32[]{:S(2)}) async-start(bf16[16,136,512]{2,1,0:T(8,128)(2,1)} %broadcast_in_dim.150), calls=%async_computation.9 | async-start | bytes 4456448 | tf_op jit(solution)/shard_map/back_gather/all_to_all | solution.py:25
  223.6 1.3 broadcast_select_fusion.1
  224.9 1.1 pad_maximum_fusion.1
  226.0 1.5 copy.13
  227.4 1.9 collective-permute-start.5
  229.4 24.4 %collective-permute-done.5.other_ref = bf16[256,2048]{1,0:T(8,128)(2,1)S(1)} collective-permute-done((bf16[256,2048]{1,0:T(8,128)(2,1)S(1)}, bf16[256,2048]{1,0:T(8,128)(2,1)S(1)}, u32[]{:S(2)}, u32[]{:S(2)}) %collective-permute-start.5) | collective-permute-done | bytes 1048608 | tf_op jit(solution)/shard_map/back_gather/ppermute | solution.py:311
  253.8 1.0 copy-done
  254.8 3.8 %all-to-all-done.9.back_ref = bf16[16,136,512]{2,1,0:T(8,128)(2,1)} async-done(((bf16[16,136,512]{2,1,0:T(8,128)(2,1)}), bf16[16,136,512]{2,1,0:T(8,128)(2,1)}, u32[]{:S(2)}, u32[]{:S(2)}) %all-to-all-start.9) | async-done | bytes 2228256 | tf_op jit(solution)/shard_map/back_gather/all_to_all | solution.py:25
  258.6 4.7 %grad.1 = (bf16[2048,512]{1,0:T(8,128)(2,1)S(1)}, f32[1]{0:T(128)}) custom-call(bf16[16,136,512]{2,1,0:T(8,128)(2,1)} %all-to-all-done.9.back_ref, bf16[16,136,512]{2,1,0:T(8,128)(2,1)S(1)} %all-to-all-done.3.got_ref, f32[16,512]{1,0:T(8,128)S(1)} %broadcast_subtract_fusion.shift_ref, f32[1,512]{1,0:T(1,128)S(1)} %bitcast.51, f32[1,512]{1,0:T(1,128)S(1)} %bitcast.52, ...), custom_call_target="tpu_custom_call" | custom-call | flops 20971520 | bytes 8388608 | tf_op jit(solution)/shard_map/grad/grad/pallas_call | solution.py:316
  263.3 3.1 %collective-permute-start.6 = (bf16[2048,512]{1,0:T(8,128)(2,1)S(1)}, bf16[2048,512]{1,0:T(8,128)(2,1)S(1)}, u32[]{:S(2)}, u32[]{:S(2)}) collective-permute-start(bf16[2048,512]{1,0:T(8,128)(2,1)S(1)} %get-tuple-element.51.grad_ref), channel_id=1, source_target_pairs={{0,16},{16,0},{1,17},{17,1},{2,18},{18,2},{3,19},{19,3},{4,20},{20... | collective-permute-start | bytes 6291464 | tf_op jit(solution)/shard_map/grad_swap/ppermute | solution.py:203
  266.4 1.3 own_half.1.mine_ref
  267.7 2.5 collective-permute-done.6.grad_ref
  270.2 2.1 other_half.1
  (51 shorter events, 1.9 us)
Async XLA Ops:
  5.2 24.3 %collective-permute-start = (bf16[128,4096]{1,0:T(8,128)(2,1)}, bf16[128,4096]{1,0:T(8,128)(2,1)}, u32[]{:S(2)}, u32[]{:S(2)}) collective-permute-start(bf16[128,4096]{1,0:T(8,128)(2,1)} %get-tuple-element.28), channel_id=1, source_target_pairs={{0,16},{16,0},{1,17},{17,1},{2,18},{18,2},{3,19},{19,3},{4,20},{20... | collective-permute-start | bytes 3145736 | tf_op jit(solution)/shard_map/embeds_order/ppermute | solution.py:203
  14.0 15.5 %copy-start.4 = (bf16[256,512]{1,0:T(8,128)(2,1)S(1)}, bf16[256,512]{1,0:T(8,128)(2,1)}, u32[]{:S(2)}) copy-start(bf16[256,512]{1,0:T(8,128)(2,1)} %param.3) | copy-start | bytes 786436
  74.1 5.5 %collective-permute-start.1 = (f32[128,512]{1,0:T(8,128)S(1)}, f32[128,512]{1,0:T(8,128)S(1)}, u32[]{:S(2)}, u32[]{:S(2)}) collective-permute-start(f32[128,512]{1,0:T(8,128)S(1)} %get-tuple-element.33), channel_id=1, source_target_pairs={{0,16},{16,0},{1,17},{17,1},{2,18},{18,2},{3,19},{19,3},{4,20},{20... | collective-permute-start | bytes 786440 | tf_op jit(solution)/shard_map/project/ppermute | solution.py:203
  81.4 38.6 %all-to-all-start.3 = ((bf16[16,136,512]{2,1,0:T(8,128)(2,1)}), bf16[16,136,512]{2,1,0:T(8,128)(2,1)S(1)}, u32[]{:S(2)}, u32[]{:S(2)}) async-start(bf16[16,136,512]{2,1,0:T(8,128)(2,1)} %broadcast_in_dim.142), calls=%async_computation.3 | async-start | bytes 4456448 | tf_op jit(solution)/shard_map/project_gather/all_to_all | solution.py:25
  85.2 37.8 %collective-permute-start.2 = (bf16[32,32,256]{2,1,0:T(8,128)(2,1)}, bf16[32,32,256]{2,1,0:T(8,128)(2,1)}, u32[]{:S(2)}, u32[]{:S(2)}) collective-permute-start(bf16[32,32,256]{2,1,0:T(8,128)(2,1)} %all_to_all.50), channel_id=1, source_target_pairs={{0,2},{2,0},{1,3},{3,1},{4,6},{6,4},{5,7},{7,5},{8,10},{10,8},{9,1... | collective-permute-start | bytes 1572872 | tf_op jit(solution)/shard_map/project_gather/ppermute | solution.py:249
  121.5 1.4 copy-start.2
  123.0 10.6 %collective-permute-start.3 = (f32[128]{0:T(128)S(1)}, f32[128]{0:T(128)S(1)}, u32[]{:S(2)}, u32[]{:S(2)}) collective-permute-start(f32[128]{0:T(128)S(1)} %slice_add_fusion.2), channel_id=1, source_target_pairs={{0,16},{16,0},{1,17},{17,1},{2,18},{18,2},{3,19},{19,3},{4,20},{20... | collective-permute-start | bytes 1544 | tf_op jit(solution)/shard_map/gram_core/ppermute | solution.py:203
  178.2 37.8 %copy-start.3 = (bf16[2048,512]{1,0:T(8,128)(2,1)S(1)}, bf16[2048,512]{1,0:T(8,128)(2,1)}, u32[]{:S(2)}) copy-start(bf16[2048,512]{1,0:T(8,128)(2,1)} %copy-done.2) | copy-start | bytes 6291460
  205.7 10.0 %collective-permute-start.4 = (bf16[2048,128]{1,0:T(8,128)(2,1)S(1)}, bf16[2048,128]{1,0:T(8,128)(2,1)S(1)}, u32[]{:S(2)}, u32[]{:S(2)}) collective-permute-start(bf16[2048,128]{1,0:T(8,128)(2,1)S(1)} %bitcast.59), channel_id=1, source_target_pairs={{0,16},{16,0},{1,17},{17,1},{2,18},{18,2},{3,19},{19,3},{4,20},{20... | collective-permute-start | bytes 1572872 | tf_op jit(solution)/shard_map/gram_gather/ppermute | solution.py:203
  219.2 39.4 %all-to-all-start.9 = ((bf16[16,136,512]{2,1,0:T(8,128)(2,1)}), bf16[16,136,512]{2,1,0:T(8,128)(2,1)}, u32[]{:S(2)}, u32[]{:S(2)}) async-start(bf16[16,136,512]{2,1,0:T(8,128)(2,1)} %broadcast_in_dim.150), calls=%async_computation.9 | async-start | bytes 4456448 | tf_op jit(solution)/shard_map/back_gather/all_to_all | solution.py:25
  227.4 26.4 %collective-permute-start.5 = (bf16[256,2048]{1,0:T(8,128)(2,1)S(1)}, bf16[256,2048]{1,0:T(8,128)(2,1)S(1)}, u32[]{:S(2)}, u32[]{:S(2)}) collective-permute-start(bf16[256,2048]{1,0:T(8,128)(2,1)S(1)} %bitcast.48), channel_id=1, source_target_pairs={{0,1},{1,0},{2,3},{3,2},{4,5},{5,4},{6,7},{7,6},{8,9},{9,8},{10,11... | collective-permute-start | bytes 3145736 | tf_op jit(solution)/shard_map/back_gather/ppermute | solution.py:311
  253.8 1.0 copy-start
  258.6 7.8 %copy-start.1 = (bf16[256,2048]{1,0:T(8,128)(2,1)S(1)}, bf16[256,2048]{1,0:T(8,128)(2,1)}, u32[]{:S(2)}) copy-start(bf16[256,2048]{1,0:T(8,128)(2,1)} %copy-done) | copy-start | bytes 3145732
  263.3 6.9 %collective-permute-start.6 = (bf16[2048,512]{1,0:T(8,128)(2,1)S(1)}, bf16[2048,512]{1,0:T(8,128)(2,1)S(1)}, u32[]{:S(2)}, u32[]{:S(2)}) collective-permute-start(bf16[2048,512]{1,0:T(8,128)(2,1)S(1)} %get-tuple-element.51.grad_ref), channel_id=1, source_target_pairs={{0,16},{16,0},{1,17},{17,1},{2,18},{18,2},{3,19},{19,3},{4,20},{20... | collective-permute-start | bytes 6291464 | tf_op jit(solution)/shard_map/grad_swap/ppermute | solution.py:203

commit v8 on v7

--- a/solution.py
+++ b/solution.py
@@ -74,7 +74,7 @@
     return lax.all_to_all(blocks, BATCH, split_axis=0, concat_axis=0, tiled=True, axis_index_groups=groups)
 
 
-def grad_kernel(n_rows, chip_rows, scale, back_ref, got_ref, shift_ref, inv_ref, cross_ref, diag_ref, out_ref, loss_ref, grad_ref, std_ref):
+def grad_kernel(n_rows, chip_rows, scale, back_ref, got_ref, shift_ref, inv_ref, cross_ref, diag_ref, out_ref, grad_ref, std_ref):
     n_chip, _, width = got_ref.shape
     half = width // 2
     inv, factor = inv_ref[...], cross_ref[...]
@@ -93,11 +93,12 @@
         std_ref[rows, :] = standard
         return sums[0] + fold(grad), sums[1] + fold(grad * standard)
 
-    off_terms = jnp.zeros((1, chip_rows), F32)
-    for p in range(n_chip):
-        spare = back_ref[p, chip_rows:, :chip_rows].astype(F32)
-        off_terms = off_terms + jnp.sum(spare, axis=0, keepdims=True)
-    loss_ref[0] = jnp.sum(off_weight / (n_rows * n_rows) * off_terms + diag_ref[...]) / D_OUT
+    diag = diag_ref[...]
+    high = diag.astype(BF16).astype(F32)
+    middle = (diag - high).astype(BF16).astype(F32)
+    row = lax.broadcasted_iota(jnp.int32, (16, chip_rows), 0)
+    terms = jnp.where(row == 0, high, jnp.where(row == 1, middle, jnp.where(row == 2, diag - high - middle, 0.0)))
+    out_ref[n_rows:, :] = jnp.concatenate([terms, jnp.zeros((16, width - chip_rows), F32)], axis=1).astype(BF16)
 
     zero = jnp.zeros((8, width), F32)
     total, cross = lax.fori_loop(0, n_chip, first, (zero, zero))
@@ -147,11 +148,11 @@
 
 
 def half_grad(odd, one_ref, other_ref, grad_ref, store):
-    half = grad_ref.shape[1] // 2
+    rows, half = one_ref.shape[1], grad_ref.shape[1] // 2
 
     def product(a_ref, b_ref):
-        return jnp.dot(a_ref[...], grad_ref[:, :half], preferred_element_type=F32) + jnp.dot(
-            b_ref[...], grad_ref[:, half:], preferred_element_type=F32
+        return jnp.dot(a_ref[...], grad_ref[:rows, :half], preferred_element_type=F32) + jnp.dot(
+            b_ref[...], grad_ref[:rows, half:], preferred_element_type=F32
         )
 
     @pl.when(odd == 0)
@@ -170,8 +171,11 @@
     half_grad(place_ref[1], one_ref, other_ref, grad_ref, store)
 
 
-def other_half_kernel(place_ref, one_ref, other_ref, grad_ref, mine_ref, out_ref):
+def other_half_kernel(off_factor, place_ref, one_ref, other_ref, grad_ref, mine_ref, off_ref, diag_ref, out_ref, loss_ref):
     first = place_ref[0] == 0
+    rows, terms = one_ref.shape[1], diag_ref.shape[1]
+    other_diag = jnp.sum(grad_ref[rows:, :terms].astype(F32), axis=0, keepdims=True)
+    loss_ref[0] = jnp.sum(off_factor * off_ref[...] + diag_ref[...] + other_diag) / D_OUT
     half = mine_ref.shape[1]
 
     def store(value):
@@ -210,11 +214,9 @@
 
     with jax.named_scope("embeds_exchange"):
         by_view = lax.optimization_barrier(embeds.transpose(1, 0, 2).reshape(2 * local_rows, d_in))
-        upper = lax.axis_index("z0") // 2
-        part = local_rows // 2
-        quarter = lax.dynamic_slice_in_dim(by_view, (2 * odd + upper) * part, part, axis=0)
-        quarter = quarter.reshape(part, n_batch, depth).transpose(1, 0, 2)
-        quarter = exchange(quarter, BATCH)
+        one_view = lax.dynamic_slice_in_dim(by_view, odd * local_rows, local_rows, axis=0)
+        one_view = one_view.reshape(local_rows, n_batch, depth).transpose(1, 0, 2)
+        one_view = exchange(one_view, BATCH).reshape(n_rows, depth)
     with jax.named_scope("embeds_order"):
         own_rows, sent_rows = pl.pallas_call(
             order_kernel,
@@ -226,7 +228,7 @@
         )(place, by_view)
         other_rows = swap_core(sent_rows)
     with jax.named_scope("weight_gather"):
-        weight, quarter, own_rows, other_rows = lax.optimization_barrier((weight, quarter, own_rows, other_rows))
+        weight, one_view, own_rows, other_rows = lax.optimization_barrier((weight, one_view, own_rows, other_rows))
         first_groups, second_groups = ring_groups()
         row_weight = ring_gather(weight, first_groups)
         core_weight = ring_gather(row_weight, second_groups).reshape(n_chip * depth, width_out)
@@ -245,8 +247,9 @@
     with jax.named_scope("project_gather"):
         chip_mean = jnp.sum(projected, axis=0) / chip_rows
         block = with_rows((projected - chip_mean).astype(BF16), pieces(chip_mean))
-        block, quarter = lax.optimization_barrier((block, quarter))
-        other_quarter = lax.ppermute(quarter, "z0", [(0, 2), (2, 0), (1, 3), (3, 1)])
+        block, one_view = lax.optimization_barrier((block, one_view))
+        one_t = one_view.T
+        other_t = lax.ppermute(one_t, "z0", [(0, 1), (1, 0), (2, 3), (3, 2)])
         got = gather(block, PLANE)
     with jax.named_scope("standardize"):
         chip_means = jnp.sum(got[:, chip_rows : chip_rows + 3].astype(F32), axis=1)
@@ -265,19 +268,20 @@
         diag_local = diag_terms[:chip_rows] + diag_terms[chip_rows:]
 
     with jax.named_scope("gram"):
-        mine = lax.dynamic_slice_in_dim(normed, chip * chip_rows, chip_rows, axis=0)
-        contract = (((1,), (1,)), ((), ()))
-        part_a = lax.dot_general(view_a, mine[:, :half], contract, preferred_element_type=F32)
-        part_b = lax.dot_general(view_b, mine[:, half:], contract, preferred_element_type=F32)
-        parts = jnp.stack([part_a.astype(BF16), part_b.astype(BF16)])
+        def partial(view):
+            mine = lax.dynamic_slice_in_dim(view, chip * chip_rows, chip_rows, axis=0)
+            return lax.dot_general(view, mine, (((1,), (1,)), ((), ())), preferred_element_type=F32)
+
+        sent = partial(jnp.where(first, view_b, view_a)).astype(BF16)
+        kept = partial(jnp.where(first, view_a, view_b))
         weight_diag = 2.0 * ((1.0 - off_weight) * diagonal - 1.0)
         factor = loss_scale / n_rows * jnp.concatenate([weight_diag, weight_diag])
-        parts, diag_local, factor, inverse, other_quarter = lax.optimization_barrier(
-            (parts, diag_local, factor, inverse, other_quarter)
+        sent, kept, diag_local, factor, inverse, one_t, other_t = lax.optimization_barrier(
+            (sent, kept, diag_local, factor, inverse, one_t, other_t)
         )
     with jax.named_scope("gram_core"):
-        extra = pad_rows(pieces(diag_local + swap_core(diag_local)), chip_rows)
-        parts = jnp.sum(exchange(parts, "core").astype(F32), axis=0)
+        extra = pad_rows(pieces(diag_local), chip_rows)
+        parts = kept + swap_core(sent).astype(F32)
     with jax.named_scope("gram_reduce"):
         parts = parts.astype(BF16).reshape(n_near, n_rows // n_near, chip_rows)
         extra = jnp.broadcast_to(extra[None], (n_near, PAD, chip_rows))
@@ -304,26 +308,20 @@
         terms = jnp.concatenate([off_local, jnp.zeros((width_out - chip_rows,), F32)])
         block = with_rows(back, pieces(terms))
     with jax.named_scope("back_gather"):
-        block, quarter, other_quarter = lax.optimization_barrier((block, quarter, other_quarter))
-        low = jnp.where(upper == 0, quarter, other_quarter)
-        high = jnp.where(upper == 0, other_quarter, quarter)
-        one_t = jnp.concatenate([low, high], axis=1).reshape(n_rows, depth).T
-        other_t = lax.ppermute(one_t, "z0", [(0, 1), (1, 0), (2, 3), (3, 2)])
         got_back = gather(block, PLANE)
-        got_back, one_t, other_t = lax.optimization_barrier((got_back, one_t, other_t))
     with jax.named_scope("grad"):
         scale_off = 2.0 * off_weight / (n_rows * n_rows)
-        grad_proj, loss = pl.pallas_call(
+        off_terms = jnp.sum(got_back[:, chip_rows:, :chip_rows].astype(F32), axis=(0, 1))[None]
+        grad_proj = pl.pallas_call(
             functools.partial(grad_kernel, n_rows, chip_rows, loss_scale * scale_off),
-            out_shape=[jax.ShapeDtypeStruct((n_rows, width_out), BF16), jax.ShapeDtypeStruct((1,), F32)],
+            out_shape=jax.ShapeDtypeStruct((n_rows + 16, width_out), BF16),
             in_specs=[vmem] * 6,
-            out_specs=[vmem, smem],
+            out_specs=vmem,
             scratch_shapes=[pltpu.VMEM((n_rows, width_out), F32)] * 2,
             compiler_params=params,
             cost_estimate=pl.CostEstimate(flops=20 * n_rows * width_out, bytes_accessed=8 * n_rows * width_out, transcendentals=0),
             name="grad",
         )(got_back, got, shift, inverse[None], factor[None], diag_terms[None])
-        loss_value = loss[0]
     with jax.named_scope("grad_swap"):
         other_proj = swap_core(grad_proj)
     with jax.named_scope("weight_grad"):
@@ -335,15 +333,15 @@
             compiler_params=params,
             name="own_half",
         )(place, one_t, other_t, grad_proj)
-        grad_weight = pl.pallas_call(
-            other_half_kernel,
-            out_shape=jax.ShapeDtypeStruct((depth, width_out), F32),
-            in_specs=[smem] + [vmem] * 4,
-            out_specs=vmem,
+        grad_weight, loss = pl.pallas_call(
+            functools.partial(other_half_kernel, off_weight / (n_rows * n_rows)),
+            out_shape=[jax.ShapeDtypeStruct((depth, width_out), F32), jax.ShapeDtypeStruct((1,), F32)],
+            in_specs=[smem] + [vmem] * 6,
+            out_specs=[vmem, smem],
             compiler_params=params,
             name="other_half",
-        )(place, one_t, other_t, other_proj, mine)
-    return (loss_value, grad_weight)
+        )(place, one_t, other_t, other_proj, mine, off_terms, diag_terms[None])
+    return (loss[0], grad_weight)
 
 
 def solution(mesh):

time: 273 us -> 262 us (0.960)
  blocking collectives: 132 us -> 166 us
  waiting for transfers between devices: 65 us -> 37.2 us
  starting transfers between devices: 41.1 us -> 33.4 us
  other arithmetic: 8.65 us -> 3.11 us
    all_to_all x6, blocking collectives: 90.6 us -> 124 us  [exchange(): return lax.all_to_all(blocks, axes, split_axis=0, concat_axis=0, tiled=True)]
    ppermute x1, waiting for transfers between devices: 24.4 us -> 0.01 us  [body(): other_t = lax.ppermute(one_t, 'z0', [(0, 1), (1, 0), (2, 3), (3, 2)])]
    all_to_all x2 -> x1, starting transfers between devices: 8.15 us -> 3.72 us  [exchange(): return lax.all_to_all(blocks, axes, split_axis=0, concat_axis=0, tiled=True)]
    all_to_all x2 -> x1, waiting for transfers between devices: 35.5 us -> 31.5 us  [exchange(): return lax.all_to_all(blocks, axes, split_axis=0, concat_axis=0, tiled=True)]
    ppermute x1 -> x0, starting transfers between devices: 3.19 us -> none  [body(): lax.ppermute(quarter, 'z0', [(0, 2), (2, 0), (1, 3), (3, 1)])]
  transfers between devices with their start and end apart: 9 -> 7, of which waited for: 6 -> 5; matrix products, arithmetic and copies ran while one was open for 3% -> 2% of each run, Pallas kernels for 0% -> 1%
where the time goes in v8:
time: 262 us
  blocking collectives  166 us (63%)
  waiting for transfers between devices  37.2 us (14%)
  starting transfers between devices  33.4 us (13%)
  Pallas kernels  11.5 us (4%)
  local copies, waits for them, and re-layouts  7.54 us (3%)
  other arithmetic  3.11 us (1%)
    all_to_all x6, blocking collectives, exchange(): return lax.all_to_all(blocks, axes, split_axis=0, concat_axis=0, tiled=True)  124 us
    all_to_all x2, blocking collectives, ring_gather(): lax.all_to_all(blocks, BATCH, split_axis=0, concat_axis=0, tiled=True, ax...  41.9 us
    all_to_all x1, waiting for transfers between devices, exchange(): return lax.all_to_all(blocks, axes, split_axis=0, concat_axis=0, tiled=True)  31.5 us
    ppermute x5, starting transfers between devices, swap_core(): return lax.ppermute(a, 'core', [(0, 1), (1, 0)])  27.8 us
    ppermute x5, waiting for transfers between devices, swap_core(): return lax.ppermute(a, 'core', [(0, 1), (1, 0)])  5.74 us
  transfers between devices with their start and end apart: 7, of which 5 were waited for; matrix products, arithmetic and copies ran while one was open for 2% of the time, Pallas kernels for 1%

profile of v8, /device:TPU:1, one launch (start us, length us, event | category | flops | bytes accessed | tf_op | source)
XLA Modules:
  0.0 261.7 jit_solution(5851942750992000692)
XLA Ops:
  0.6 2.8 %copy.11 = bf16[2,64,8192]{2,1,0:T(8,128)(2,1)S(1)} copy(bf16[2,64,8192]{2,0,1:T(2,128)(2,1)} %bitcast.58) | data formatting | bytes 4194304 | tf_op jit(solution)/shard_map/embeds_exchange/transpose | solution.py:216
  3.5 1.7 order.1
  5.2 8.8 %collective-permute-start = (bf16[128,4096]{1,0:T(8,128)(2,1)}, bf16[128,4096]{1,0:T(8,128)(2,1)}, u32[]{:S(2)}, u32[]{:S(2)}) collective-permute-start(bf16[128,4096]{1,0:T(8,128)(2,1)} %get-tuple-element.24), channel_id=1, source_target_pairs={{0,16},{16,0},{1,17},{17,1},{2,18},{18,2},{3,19},{19,3},{4,20},{20... | collective-permute-start | bytes 3145736 | tf_op jit(solution)/shard_map/embeds_order/ppermute | solution.py:207
  14.1 0.3 copy.14
  14.4 0.6 copy.12
  15.0 20.6 %all_to_all.45 = bf16[32,64,256]{2,1,0:T(8,128)(2,1)} all-to-all(bf16[32,64,256]{2,1,0:T(8,128)(2,1)S(1)} %copy.12), channel_id=1, replica_groups=mesh['y'=4,'x'=4,'core'=2,'z1'=4,'z0'=4] {'y','x','core'}, dimensions={0} | all-to-all | bytes 2097152 | tf_op jit(solution)/shard_map/embeds_exchange/all_to_all | solution.py:25
  35.7 12.5 %all_to_all.46 = bf16[4,256,512]{2,1,0:T(8,128)(2,1)S(1)} all-to-all(bf16[4,256,512]{2,1,0:T(8,128)(2,1)S(1)} %broadcast_in_dim.139), channel_id=1, replica_groups={{0,32,64,96},{128,160,192,224},{256,288,320,352},{384,416,448,480},{16,..., dimensions={0} | all-to-all | bytes 2097152 | tf_op jit(solution)/shard_map/weight_gather/all_to_all | solution.py:74
  48.1 0.4 broadcast_in_dim.140
  48.5 29.5 %all_to_all.47 = bf16[4,4,256,512]{3,2,1,0:T(8,128)(2,1)S(1)} all-to-all(bf16[4,4,256,512]{3,2,1,0:T(8,128)(2,1)S(1)} %broadcast_in_dim.140), channel_id=1, replica_groups={{0,128,256,384},{32,160,288,416},{64,192,320,448},{96,224,352,480},{16,..., dimensions={0} | all-to-all | bytes 8388608 | tf_op jit(solution)/shard_map/weight_gather/all_to_all | solution.py:74
  78.0 2.5 project.1
  80.5 4.0 %collective-permute-start.1 = (f32[128,512]{1,0:T(8,128)S(1)}, f32[128,512]{1,0:T(8,128)S(1)}, u32[]{:S(2)}, u32[]{:S(2)}) collective-permute-start(f32[128,512]{1,0:T(8,128)S(1)} %get-tuple-element.29), channel_id=1, source_target_pairs={{0,16},{16,0},{1,17},{17,1},{2,18},{18,2},{3,19},{19,3},{4,20},{20... | collective-permute-start | bytes 786440 | tf_op jit(solution)/shard_map/project/ppermute | solution.py:207
  84.6 1.1 collective-permute-done.1
  85.8 0.1 select_select_fusion
  85.9 1.5 broadcast_in_dim.146
  87.4 3.7 %all-to-all-start.3 = ((bf16[16,136,512]{2,1,0:T(8,128)(2,1)}), bf16[16,136,512]{2,1,0:T(8,128)(2,1)S(1)}, u32[]{:S(2)}, u32[]{:S(2)}) async-start(bf16[16,136,512]{2,1,0:T(8,128)(2,1)} %broadcast_in_dim.146), calls=%async_computation.3 | async-start | bytes 4456448 | tf_op jit(solution)/shard_map/project_gather/all_to_all | solution.py:25
  91.2 1.5 copy.13
  92.7 1.9 collective-permute-start.2
  94.6 31.5 %all-to-all-done.3.got_ref = bf16[16,136,512]{2,1,0:T(8,128)(2,1)S(1)} async-done(((bf16[16,136,512]{2,1,0:T(8,128)(2,1)}), bf16[16,136,512]{2,1,0:T(8,128)(2,1)S(1)}, u32[]{:S(2)}, u32[]{:S(2)}) %all-to-all-start.3) | async-done | bytes 2228256 | tf_op jit(solution)/shard_map/project_gather/all_to_all | solution.py:25
  126.1 0.1 convert_reduce_fusion.2
  126.2 0.7 multiply_reduce_fusion
  126.9 0.6 fusion
  127.5 0.3 multiply_reduce_fusion.1
  127.8 0.1 broadcast_select_fusion
  128.0 0.4 convolution_convert_fusion
  128.4 0.4 fusion.21
  128.9 3.1 %collective-permute-start.3 = (bf16[2048,128]{1,0:T(8,128)(2,1)S(1)}, bf16[2048,128]{1,0:T(8,128)(2,1)S(1)}, u32[]{:S(2)}, u32[]{:S(2)}) collective-permute-start(bf16[2048,128]{1,0:T(8,128)(2,1)S(1)} %convolution_convert_fusion), channel_id=1, source_target_pairs={{0,16},{16,0},{1,17},{17,1},{2,18},{18,2},{3,19},{19,3},{4,20},{20... | collective-permute-start | bytes 1572872 | tf_op jit(solution)/shard_map/gram_core/ppermute | solution.py:207
  132.2 1.3 collective-permute-done.3
  133.5 0.1 add_convert_fusion
  133.7 17.9 %all_to_all.48 = bf16[4,520,128]{2,1,0:T(8,128)(2,1)S(1)} all-to-all(bf16[4,520,128]{2,1,0:T(8,128)(2,1)S(1)} %pad_maximum_fusion), channel_id=1, replica_groups=mesh['y'=4,'x'=4,'core'=2,'z1'=4,'z0'=4] {'z0'}, dimensions={0} | all-to-all | bytes 1064960 | tf_op jit(solution)/shard_map/gram_reduce/all_to_all | solution.py:25
  151.8 25.3 %all_to_all.49 = bf16[4,136,128]{2,1,0:T(8,128)(2,1)S(1)} all-to-all(bf16[4,136,128]{2,1,0:T(8,128)(2,1)S(1)} %pad_maximum_fusion.1), channel_id=1, replica_groups=mesh['y'=4,'x'=4,'core'=2,'z1'=4,'z0'=4] {'z1'}, dimensions={0} | all-to-all | bytes 278528 | tf_op jit(solution)/shard_map/gram_reduce/all_to_all | solution.py:25
  177.2 15.4 %all_to_all.50 = bf16[4,128,128]{2,1,0:T(8,128)(2,1)S(1)} all-to-all(bf16[4,128,128]{2,1,0:T(8,128)(2,1)S(1)} %broadcast_in_dim.149), channel_id=1, replica_groups=mesh['y'=4,'x'=4,'core'=2,'z1'=4,'z0'=4] {'z1'}, dimensions={0} | all-to-all | bytes 262144 | tf_op jit(solution)/shard_map/gram_gather/all_to_all | solution.py:25
  192.6 0.1 broadcast_in_dim.150
  192.7 11.8 %all_to_all.51 = bf16[4,4,128,128]{3,2,1,0:T(8,128)(2,1)S(1)} all-to-all(bf16[4,4,128,128]{3,2,1,0:T(8,128)(2,1)S(1)} %broadcast_in_dim.150), channel_id=1, replica_groups=mesh['y'=4,'x'=4,'core'=2,'z1'=4,'z0'=4] {'z0'}, dimensions={0} | all-to-all | bytes 1048576 | tf_op jit(solution)/shard_map/gram_gather/all_to_all | solution.py:25
  204.6 8.5 %collective-permute-start.4 = (bf16[2048,128]{1,0:T(8,128)(2,1)S(1)}, bf16[2048,128]{1,0:T(8,128)(2,1)S(1)}, u32[]{:S(2)}, u32[]{:S(2)}) collective-permute-start(bf16[2048,128]{1,0:T(8,128)(2,1)S(1)} %bitcast.59), channel_id=1, source_target_pairs={{0,16},{16,0},{1,17},{17,1},{2,18},{18,2},{3,19},{19,3},{4,20},{20... | collective-permute-start | bytes 1572872 | tf_op jit(solution)/shard_map/gram_gather/ppermute | solution.py:207
  213.1 1.5 collective-permute-done.4
  214.6 0.3 fusion.4
  214.9 0.3 fusion.6
  215.3 0.4 fusion.1
  215.6 0.3 fusion.9
  216.0 0.4 fusion.2
  216.4 0.1 fusion.20
  216.5 0.1 broadcast_in_dim.154
  216.7 32.6 %all_to_all.52.back_ref = bf16[16,136,512]{2,1,0:T(8,128)(2,1)S(1)} all-to-all(bf16[16,136,512]{2,1,0:T(8,128)(2,1)S(1)} %broadcast_in_dim.154), channel_id=1, replica_groups=mesh['y'=4,'x'=4,'core'=2,'z1'=4,'z0'=4] {'y','x'}, dimensions={0} | all-to-all | bytes 4456448 | tf_op jit(solution)/shard_map/back_gather/all_to_all | solution.py:25
  249.2 2.4 grad.1.grad_ref
  251.7 3.4 %collective-permute-start.5 = (bf16[2064,512]{1,0:T(8,128)(2,1)S(1)}, bf16[2064,512]{1,0:T(8,128)(2,1)S(1)}, u32[]{:S(2)}, u32[]{:S(2)}) collective-permute-start(bf16[2064,512]{1,0:T(8,128)(2,1)S(1)} %grad.1.grad_ref), channel_id=1, source_target_pairs={{0,16},{16,0},{1,17},{17,1},{2,18},{18,2},{3,19},{19,3},{4,20},{20... | collective-permute-start | bytes 6340616 | tf_op jit(solution)/shard_map/grad_swap/ppermute | solution.py:207
  255.1 2.0 own_half.1.mine_ref
  257.1 1.8 collective-permute-done.5.grad_ref
  258.8 2.9 %other_half.1 = (f32[256,512]{1,0:T(8,128)}, f32[1]{0:T(128)}) custom-call(s32[2]{0:T(128)S(1)} %pad_add_fusion.place_ref, bf16[256,2048]{1,0:T(8,128)(2,1)S(1)} %bitcast.49, bf16[256,2048]{1,0:T(8,128)(2,1)} %collective-permute-done.2.other_ref, bf16[2064,512]{1,0:T(8,128)(2,1)S(1)} %collective-permute-done.5.grad_ref, f32[256,256]{1,0:T(8,128)S(1)} %own_half.1.mine_ref, ...), custom_call_target="tpu_custom_call" | custom-call | tf_op jit(solution)/shard_map/weight_grad/other_half/pallas_call | solution.py:336
  (38 shorter events, 0.9 us)
Async XLA Ops:
  5.2 30.4 %collective-permute-start = (bf16[128,4096]{1,0:T(8,128)(2,1)}, bf16[128,4096]{1,0:T(8,128)(2,1)}, u32[]{:S(2)}, u32[]{:S(2)}) collective-permute-start(bf16[128,4096]{1,0:T(8,128)(2,1)} %get-tuple-element.24), channel_id=1, source_target_pairs={{0,16},{16,0},{1,17},{17,1},{2,18},{18,2},{3,19},{19,3},{4,20},{20... | collective-permute-start | bytes 3145736 | tf_op jit(solution)/shard_map/embeds_order/ppermute | solution.py:207
  14.4 21.2 %copy-start = (bf16[256,512]{1,0:T(8,128)(2,1)S(1)}, bf16[256,512]{1,0:T(8,128)(2,1)}, u32[]{:S(2)}) copy-start(bf16[256,512]{1,0:T(8,128)(2,1)} %param.3) | copy-start | bytes 786436
  80.5 5.2 %collective-permute-start.1 = (f32[128,512]{1,0:T(8,128)S(1)}, f32[128,512]{1,0:T(8,128)S(1)}, u32[]{:S(2)}, u32[]{:S(2)}) collective-permute-start(f32[128,512]{1,0:T(8,128)S(1)} %get-tuple-element.29), channel_id=1, source_target_pairs={{0,16},{16,0},{1,17},{17,1},{2,18},{18,2},{3,19},{19,3},{4,20},{20... | collective-permute-start | bytes 786440 | tf_op jit(solution)/shard_map/project/ppermute | solution.py:207
  87.4 38.6 %all-to-all-start.3 = ((bf16[16,136,512]{2,1,0:T(8,128)(2,1)}), bf16[16,136,512]{2,1,0:T(8,128)(2,1)S(1)}, u32[]{:S(2)}, u32[]{:S(2)}) async-start(bf16[16,136,512]{2,1,0:T(8,128)(2,1)} %broadcast_in_dim.146), calls=%async_computation.3 | async-start | bytes 4456448 | tf_op jit(solution)/shard_map/project_gather/all_to_all | solution.py:25
  92.7 36.2 %collective-permute-start.2 = (bf16[256,2048]{1,0:T(8,128)(2,1)S(1)}, bf16[256,2048]{1,0:T(8,128)(2,1)}, u32[]{:S(2)}, u32[]{:S(2)}) collective-permute-start(bf16[256,2048]{1,0:T(8,128)(2,1)S(1)} %bitcast.47), channel_id=1, source_target_pairs={{0,1},{1,0},{2,3},{3,2},{4,5},{5,4},{6,7},{7,6},{8,9},{9,8},{10,11... | collective-permute-start | bytes 3145736 | tf_op jit(solution)/shard_map/project_gather/ppermute | solution.py:252
  128.9 4.6 %collective-permute-start.3 = (bf16[2048,128]{1,0:T(8,128)(2,1)S(1)}, bf16[2048,128]{1,0:T(8,128)(2,1)S(1)}, u32[]{:S(2)}, u32[]{:S(2)}) collective-permute-start(bf16[2048,128]{1,0:T(8,128)(2,1)S(1)} %convolution_convert_fusion), channel_id=1, source_target_pairs={{0,16},{16,0},{1,17},{17,1},{2,18},{18,2},{3,19},{19,3},{4,20},{20... | collective-permute-start | bytes 1572872 | tf_op jit(solution)/shard_map/gram_core/ppermute | solution.py:207
  204.6 10.0 %collective-permute-start.4 = (bf16[2048,128]{1,0:T(8,128)(2,1)S(1)}, bf16[2048,128]{1,0:T(8,128)(2,1)S(1)}, u32[]{:S(2)}, u32[]{:S(2)}) collective-permute-start(bf16[2048,128]{1,0:T(8,128)(2,1)S(1)} %bitcast.59), channel_id=1, source_target_pairs={{0,16},{16,0},{1,17},{17,1},{2,18},{18,2},{3,19},{19,3},{4,20},{20... | collective-permute-start | bytes 1572872 | tf_op jit(solution)/shard_map/gram_gather/ppermute | solution.py:207
  251.7 7.2 %collective-permute-start.5 = (bf16[2064,512]{1,0:T(8,128)(2,1)S(1)}, bf16[2064,512]{1,0:T(8,128)(2,1)S(1)}, u32[]{:S(2)}, u32[]{:S(2)}) collective-permute-start(bf16[2064,512]{1,0:T(8,128)(2,1)S(1)} %grad.1.grad_ref), channel_id=1, source_target_pairs={{0,16},{16,0},{1,17},{17,1},{2,18},{18,2},{3,19},{19,3},{4,20},{20... | collective-permute-start | bytes 6340616 | tf_op jit(solution)/shard_map/grad_swap/ppermute | solution.py:207

commit v9 on v8

--- a/solution.py
+++ b/solution.py
@@ -216,7 +216,6 @@
         by_view = lax.optimization_barrier(embeds.transpose(1, 0, 2).reshape(2 * local_rows, d_in))
         one_view = lax.dynamic_slice_in_dim(by_view, odd * local_rows, local_rows, axis=0)
         one_view = one_view.reshape(local_rows, n_batch, depth).transpose(1, 0, 2)
-        one_view = exchange(one_view, BATCH).reshape(n_rows, depth)
     with jax.named_scope("embeds_order"):
         own_rows, sent_rows = pl.pallas_call(
             order_kernel,
@@ -226,12 +225,14 @@
             compiler_params=params,
             name="order",
         )(place, by_view)
-        other_rows = swap_core(sent_rows)
     with jax.named_scope("weight_gather"):
-        weight, one_view, own_rows, other_rows = lax.optimization_barrier((weight, one_view, own_rows, other_rows))
         first_groups, second_groups = ring_groups()
         row_weight = ring_gather(weight, first_groups)
+        row_weight, one_view, own_rows, sent_rows = lax.optimization_barrier((row_weight, one_view, own_rows, sent_rows))
         core_weight = ring_gather(row_weight, second_groups).reshape(n_chip * depth, width_out)
+        core_weight, one_view, sent_rows = lax.optimization_barrier((core_weight, one_view, sent_rows))
+        one_view = exchange(one_view, BATCH).reshape(n_rows, depth)
+        other_rows = swap_core(sent_rows)
     with jax.named_scope("project"):
         kept, sent = pl.pallas_call(
             project_kernel,
@@ -241,6 +242,7 @@
             compiler_params=params,
             name="project",
         )(place, own_rows, other_rows, core_weight)
+        kept, sent, one_view = lax.optimization_barrier((kept, sent, one_view))
         got_other, got_own = jnp.split(swap_core(sent), 2)
         own, other = jnp.split(kept, 2)
         projected = in_core_order(own + got_own, other + got_other, 0)

time: 262 us -> 261 us (level)
  blocking collectives: 166 us -> 131 us
  waiting for transfers between devices: 37.2 us -> 54.3 us
  starting transfers between devices: 33.4 us -> 41.8 us
  local copies, waits for them, and re-layouts: 7.54 us -> 15.9 us
    all_to_all x6 -> x5, blocking collectives: 124 us -> 100 us  [exchange(): return lax.all_to_all(blocks, axes, split_axis=0, concat_axis=0, tiled=True)]
    all_to_all x1 -> x2, waiting for transfers between devices: 31.5 us -> 44.6 us  [exchange(): return lax.all_to_all(blocks, axes, split_axis=0, concat_axis=0, tiled=True)]
    all_to_all x2 -> x1, blocking collectives: 41.9 us -> 31 us  [ring_gather(): lax.all_to_all(blocks, BATCH, split_axis=0, concat_axis=0, tiled=True, ax...]
    all_to_all x0 -> x1, starting transfers between devices: none -> 5.01 us  [ring_gather(): lax.all_to_all(blocks, BATCH, split_axis=0, concat_axis=0, tiled=True, ax...]
    all_to_all x1 -> x2, starting transfers between devices: 3.72 us -> 8.18 us  [exchange(): return lax.all_to_all(blocks, axes, split_axis=0, concat_axis=0, tiled=True)]
    unnamed x3 -> x9, local copies, waits for them, and re-layouts: 0.26 us -> 4.44 us
    all_to_all x0 -> x1, waiting for transfers between devices: none -> 3.91 us  [ring_gather(): lax.all_to_all(blocks, BATCH, split_axis=0, concat_axis=0, tiled=True, ax...]
    broadcast_in_dim x2, local copies, waits for them, and re-layouts: 0.48 us -> 3.69 us  [ring_gather(): blocks = jnp.broadcast_to(block[None], (4,) + block.shape)]
  transfers between devices with their start and end apart: 7 -> 9, of which waited for: 5 -> 7; matrix products, arithmetic and copies ran while one was open for 2% -> 4% of each run, Pallas kernels for 1% -> 2%
where the time goes in v9:
time: 261 us; the launch traced here: 260 us
  blocking collectives  131 us (50%)
  waiting for transfers between devices  54.3 us (21%)
  starting transfers between devices  41.8 us (16%)
  local copies, waits for them, and re-layouts  15.9 us (6%)
  Pallas kernels  9.78 us (4%)
  other arithmetic  3.16 us (1%)
    all_to_all x5, blocking collectives, exchange(): return lax.all_to_all(blocks, axes, split_axis=0, concat_axis=0, tiled=True)  100 us
    all_to_all x2, waiting for transfers between devices, exchange(): return lax.all_to_all(blocks, axes, split_axis=0, concat_axis=0, tiled=True)  44.6 us
    all_to_all x1, blocking collectives, ring_gather(): lax.all_to_all(blocks, BATCH, split_axis=0, concat_axis=0, tiled=True, ax...  31 us
    ppermute x5, starting transfers between devices, swap_core(): return lax.ppermute(a, 'core', [(0, 1), (1, 0)])  26.7 us
    all_to_all x2, starting transfers between devices, exchange(): return lax.all_to_all(blocks, axes, split_axis=0, concat_axis=0, tiled=True)  8.18 us
    ppermute x5, waiting for transfers between devices, swap_core(): return lax.ppermute(a, 'core', [(0, 1), (1, 0)])  5.72 us
  transfers between devices with their start and end apart: 9, of which 7 were waited for; matrix products, arithmetic and copies ran while one was open for 4% of the time, Pallas kernels for 2%

profile of v9, /device:TPU:1, one launch (start us, length us, event | category | flops | bytes accessed | tf_op | source)
XLA Modules:
  0.0 259.7 jit_solution(9075661052722381129)
XLA Ops:
  0.6 2.1 broadcast_in_dim.139
  2.7 5.0 %all-to-all-start = ((bf16[4,256,512]{2,1,0:T(8,128)(2,1)}), bf16[4,256,512]{2,1,0:T(8,128)(2,1)}, u32[]{:S(2)}, u32[]{:S(2)}) async-start(bf16[4,256,512]{2,1,0:T(8,128)(2,1)} %broadcast_in_dim.139), calls=%async_computation | async-start | bytes 2097152 | tf_op jit(solution)/shard_map/weight_gather/all_to_all | solution.py:74
  7.7 2.7 %copy.11 = bf16[2,64,8192]{2,1,0:T(8,128)(2,1)S(1)} copy(bf16[2,64,8192]{2,0,1:T(2,128)(2,1)} %bitcast.57) | data formatting | bytes 4194304 | tf_op jit(solution)/shard_map/embeds_exchange/transpose | solution.py:216
  10.6 1.2 copy.14
  11.9 0.8 order.1
  12.6 1.0 copy-done.1
  13.6 3.9 %all-to-all-done = bf16[4,256,512]{2,1,0:T(8,128)(2,1)} async-done(((bf16[4,256,512]{2,1,0:T(8,128)(2,1)}), bf16[4,256,512]{2,1,0:T(8,128)(2,1)}, u32[]{:S(2)}, u32[]{:S(2)}) %all-to-all-start) | async-done | bytes 1048608 | tf_op jit(solution)/shard_map/weight_gather/all_to_all | solution.py:74
  17.6 1.6 broadcast_in_dim.140
  19.2 31.0 %all_to_all.45 = bf16[4,4,256,512]{3,2,1,0:T(8,128)(2,1)} all-to-all(bf16[4,4,256,512]{3,2,1,0:T(8,128)(2,1)S(1)} %broadcast_in_dim.140), channel_id=1, replica_groups={{0,128,256,384},{32,160,288,416},{64,192,320,448},{96,224,352,480},{16,..., dimensions={0} | all-to-all | bytes 8388608 | tf_op jit(solution)/shard_map/weight_gather/all_to_all | solution.py:74
  50.2 9.5 %collective-permute-start = (bf16[128,4096]{1,0:T(8,128)(2,1)S(1)}, bf16[128,4096]{1,0:T(8,128)(2,1)S(1)}, u32[]{:S(2)}, u32[]{:S(2)}) collective-permute-start(bf16[128,4096]{1,0:T(8,128)(2,1)S(1)} %copy-done.2), channel_id=1, source_target_pairs={{0,16},{16,0},{1,17},{17,1},{2,18},{18,2},{3,19},{19,3},{4,20},{20... | collective-permute-start | bytes 3145736 | tf_op jit(solution)/shard_map/weight_gather/ppermute | solution.py:207
  59.6 1.6 copy.12
  61.2 4.5 %all-to-all-start.2 = ((bf16[32,64,256]{2,1,0:T(8,128)(2,1)}), bf16[32,64,256]{2,1,0:T(8,128)(2,1)}, u32[]{:S(2)}, u32[]{:S(2)}) async-start(bf16[32,64,256]{2,1,0:T(8,128)(2,1)} %copy.12), calls=%async_computation.2 | async-start | bytes 2097152 | tf_op jit(solution)/shard_map/weight_gather/all_to_all | solution.py:25
  65.7 2.2 copy-done
  67.9 1.8 project.1
  69.7 13.1 %all-to-all-done.2 = bf16[32,64,256]{2,1,0:T(8,128)(2,1)} async-done(((bf16[32,64,256]{2,1,0:T(8,128)(2,1)}), bf16[32,64,256]{2,1,0:T(8,128)(2,1)}, u32[]{:S(2)}, u32[]{:S(2)}) %all-to-all-start.2) | async-done | bytes 1048608 | tf_op jit(solution)/shard_map/weight_gather/all_to_all | solution.py:25
  82.8 2.3 collective-permute-start.1
  85.2 1.1 collective-permute-done.1
  86.5 1.5 broadcast_in_dim.146
  88.0 3.7 %all-to-all-start.3 = ((bf16[16,136,512]{2,1,0:T(8,128)(2,1)}), bf16[16,136,512]{2,1,0:T(8,128)(2,1)S(1)}, u32[]{:S(2)}, u32[]{:S(2)}) async-start(bf16[16,136,512]{2,1,0:T(8,128)(2,1)} %broadcast_in_dim.146), calls=%async_computation.3 | async-start | bytes 4456448 | tf_op jit(solution)/shard_map/project_gather/all_to_all | solution.py:25
  91.8 1.5 copy.13
  93.3 1.9 collective-permute-start.2
  95.2 31.5 %all-to-all-done.3.got_ref = bf16[16,136,512]{2,1,0:T(8,128)(2,1)S(1)} async-done(((bf16[16,136,512]{2,1,0:T(8,128)(2,1)}), bf16[16,136,512]{2,1,0:T(8,128)(2,1)S(1)}, u32[]{:S(2)}, u32[]{:S(2)}) %all-to-all-start.3) | async-done | bytes 2228256 | tf_op jit(solution)/shard_map/project_gather/all_to_all | solution.py:25
  126.8 0.7 multiply_reduce_fusion
  127.5 0.6 fusion
  128.1 0.3 multiply_reduce_fusion.1
  128.5 0.1 broadcast_select_fusion
  128.6 0.4 convolution_convert_fusion
  129.1 0.4 fusion.21
  129.5 3.1 %collective-permute-start.3 = (bf16[2048,128]{1,0:T(8,128)(2,1)S(1)}, bf16[2048,128]{1,0:T(8,128)(2,1)S(1)}, u32[]{:S(2)}, u32[]{:S(2)}) collective-permute-start(bf16[2048,128]{1,0:T(8,128)(2,1)S(1)} %convolution_convert_fusion), channel_id=1, source_target_pairs={{0,16},{16,0},{1,17},{17,1},{2,18},{18,2},{3,19},{19,3},{4,20},{20... | collective-permute-start | bytes 1572872 | tf_op jit(solution)/shard_map/gram_core/ppermute | solution.py:207
  132.8 1.3 collective-permute-done.3
  134.3 16.8 %all_to_all.46 = bf16[4,520,128]{2,1,0:T(8,128)(2,1)S(1)} all-to-all(bf16[4,520,128]{2,1,0:T(8,128)(2,1)S(1)} %pad_maximum_fusion), channel_id=1, replica_groups=mesh['y'=4,'x'=4,'core'=2,'z1'=4,'z0'=4] {'z0'}, dimensions={0} | all-to-all | bytes 1064960 | tf_op jit(solution)/shard_map/gram_reduce/all_to_all | solution.py:25
  151.4 23.8 %all_to_all.47 = bf16[4,136,128]{2,1,0:T(8,128)(2,1)S(1)} all-to-all(bf16[4,136,128]{2,1,0:T(8,128)(2,1)S(1)} %pad_maximum_fusion.1), channel_id=1, replica_groups=mesh['y'=4,'x'=4,'core'=2,'z1'=4,'z0'=4] {'z1'}, dimensions={0} | all-to-all | bytes 278528 | tf_op jit(solution)/shard_map/gram_reduce/all_to_all | solution.py:25
  175.3 15.4 %all_to_all.48 = bf16[4,128,128]{2,1,0:T(8,128)(2,1)S(1)} all-to-all(bf16[4,128,128]{2,1,0:T(8,128)(2,1)S(1)} %broadcast_in_dim.149), channel_id=1, replica_groups=mesh['y'=4,'x'=4,'core'=2,'z1'=4,'z0'=4] {'z1'}, dimensions={0} | all-to-all | bytes 262144 | tf_op jit(solution)/shard_map/gram_gather/all_to_all | solution.py:25
  190.7 11.8 %all_to_all.49 = bf16[4,4,128,128]{3,2,1,0:T(8,128)(2,1)S(1)} all-to-all(bf16[4,4,128,128]{3,2,1,0:T(8,128)(2,1)S(1)} %broadcast_in_dim.150), channel_id=1, replica_groups=mesh['y'=4,'x'=4,'core'=2,'z1'=4,'z0'=4] {'z0'}, dimensions={0} | all-to-all | bytes 1048576 | tf_op jit(solution)/shard_map/gram_gather/all_to_all | solution.py:25
  202.6 8.5 %collective-permute-start.4 = (bf16[2048,128]{1,0:T(8,128)(2,1)S(1)}, bf16[2048,128]{1,0:T(8,128)(2,1)S(1)}, u32[]{:S(2)}, u32[]{:S(2)}) collective-permute-start(bf16[2048,128]{1,0:T(8,128)(2,1)S(1)} %bitcast.58), channel_id=1, source_target_pairs={{0,16},{16,0},{1,17},{17,1},{2,18},{18,2},{3,19},{19,3},{4,20},{20... | collective-permute-start | bytes 1572872 | tf_op jit(solution)/shard_map/gram_gather/ppermute | solution.py:207
  211.1 1.5 collective-permute-done.4
  212.6 0.3 fusion.4
  212.9 0.3 fusion.6
  213.3 0.4 fusion.1
  213.7 0.3 fusion.9
  214.0 0.4 fusion.2
  214.5 0.1 broadcast_in_dim.154
  214.7 32.6 %all_to_all.50.back_ref = bf16[16,136,512]{2,1,0:T(8,128)(2,1)S(1)} all-to-all(bf16[16,136,512]{2,1,0:T(8,128)(2,1)S(1)} %broadcast_in_dim.154), channel_id=1, replica_groups=mesh['y'=4,'x'=4,'core'=2,'z1'=4,'z0'=4] {'y','x'}, dimensions={0} | all-to-all | bytes 4456448 | tf_op jit(solution)/shard_map/back_gather/all_to_all | solution.py:25
  247.3 2.4 grad.1.grad_ref
  249.7 3.4 %collective-permute-start.5 = (bf16[2064,512]{1,0:T(8,128)(2,1)S(1)}, bf16[2064,512]{1,0:T(8,128)(2,1)S(1)}, u32[]{:S(2)}, u32[]{:S(2)}) collective-permute-start(bf16[2064,512]{1,0:T(8,128)(2,1)S(1)} %grad.1.grad_ref), channel_id=1, source_target_pairs={{0,16},{16,0},{1,17},{17,1},{2,18},{18,2},{3,19},{19,3},{4,20},{20... | collective-permute-start | bytes 6340616 | tf_op jit(solution)/shard_map/grad_swap/ppermute | solution.py:207
  253.1 2.0 own_half.1.mine_ref
  255.1 1.8 collective-permute-done.5.grad_ref
  256.9 2.8 %other_half.1 = (f32[256,512]{1,0:T(8,128)}, f32[1]{0:T(128)}) custom-call(s32[2]{0:T(128)S(1)} %pad_add_fusion.place_ref, bf16[256,2048]{1,0:T(8,128)(2,1)S(1)} %bitcast.49, bf16[256,2048]{1,0:T(8,128)(2,1)} %collective-permute-done.2.other_ref, bf16[2064,512]{1,0:T(8,128)(2,1)S(1)} %collective-permute-done.5.grad_ref, f32[256,256]{1,0:T(8,128)S(1)} %own_half.1.mine_ref, ...), custom_call_target="tpu_custom_call" | custom-call | tf_op jit(solution)/shard_map/weight_grad/other_half/pallas_call | solution.py:338
  (46 shorter events, 1.4 us)
Async XLA Ops:
  2.7 14.9 %all-to-all-start = ((bf16[4,256,512]{2,1,0:T(8,128)(2,1)}), bf16[4,256,512]{2,1,0:T(8,128)(2,1)}, u32[]{:S(2)}, u32[]{:S(2)}) async-start(bf16[4,256,512]{2,1,0:T(8,128)(2,1)} %broadcast_in_dim.139), calls=%async_computation | async-start | bytes 2097152 | tf_op jit(solution)/shard_map/weight_gather/all_to_all | solution.py:74
  12.6 1.0 copy-start.1
  19.2 31.0 %copy-start.2 = (bf16[128,4096]{1,0:T(8,128)(2,1)S(1)}, bf16[128,4096]{1,0:T(8,128)(2,1)}, u32[]{:S(2)}) copy-start(bf16[128,4096]{1,0:T(8,128)(2,1)} %copy-done.1) | copy-start | bytes 3145732
  19.2 40.4 %copy-start.3 = (bf16[8,8,32,256]{3,2,1,0:T(8,128)(2,1)S(1)}, bf16[8,8,32,256]{3,2,1,0:T(8,128)(2,1)}, u32[]{:S(2)}) copy-start(bf16[8,8,32,256]{3,2,1,0:T(8,128)(2,1)} %copy.14) | copy-start | bytes 3145732
  50.2 15.5 %collective-permute-start = (bf16[128,4096]{1,0:T(8,128)(2,1)S(1)}, bf16[128,4096]{1,0:T(8,128)(2,1)S(1)}, u32[]{:S(2)}, u32[]{:S(2)}) collective-permute-start(bf16[128,4096]{1,0:T(8,128)(2,1)S(1)} %copy-done.2), channel_id=1, source_target_pairs={{0,16},{16,0},{1,17},{17,1},{2,18},{18,2},{3,19},{19,3},{4,20},{20... | collective-permute-start | bytes 3145736 | tf_op jit(solution)/shard_map/weight_gather/ppermute | solution.py:207
  61.2 21.6 %all-to-all-start.2 = ((bf16[32,64,256]{2,1,0:T(8,128)(2,1)}), bf16[32,64,256]{2,1,0:T(8,128)(2,1)}, u32[]{:S(2)}, u32[]{:S(2)}) async-start(bf16[32,64,256]{2,1,0:T(8,128)(2,1)} %copy.12), calls=%async_computation.2 | async-start | bytes 2097152 | tf_op jit(solution)/shard_map/weight_gather/all_to_all | solution.py:25
  65.7 2.2 copy-start
  82.8 3.4 %collective-permute-start.1 = (f32[128,512]{1,0:T(8,128)S(1)}, f32[128,512]{1,0:T(8,128)S(1)}, u32[]{:S(2)}, u32[]{:S(2)}) collective-permute-start(f32[128,512]{1,0:T(8,128)S(1)} %get-tuple-element.41), channel_id=1, source_target_pairs={{0,16},{16,0},{1,17},{17,1},{2,18},{18,2},{3,19},{19,3},{4,20},{20... | collective-permute-start | bytes 786440 | tf_op jit(solution)/shard_map/project/ppermute | solution.py:207
  88.0 38.6 %all-to-all-start.3 = ((bf16[16,136,512]{2,1,0:T(8,128)(2,1)}), bf16[16,136,512]{2,1,0:T(8,128)(2,1)S(1)}, u32[]{:S(2)}, u32[]{:S(2)}) async-start(bf16[16,136,512]{2,1,0:T(8,128)(2,1)} %broadcast_in_dim.146), calls=%async_computation.3 | async-start | bytes 4456448 | tf_op jit(solution)/shard_map/project_gather/all_to_all | solution.py:25
  93.3 36.3 %collective-permute-start.2 = (bf16[256,2048]{1,0:T(8,128)(2,1)S(1)}, bf16[256,2048]{1,0:T(8,128)(2,1)}, u32[]{:S(2)}, u32[]{:S(2)}) collective-permute-start(bf16[256,2048]{1,0:T(8,128)(2,1)S(1)} %bitcast.47), channel_id=1, source_target_pairs={{0,1},{1,0},{2,3},{3,2},{4,5},{5,4},{6,7},{7,6},{8,9},{9,8},{10,11... | collective-permute-start | bytes 3145736 | tf_op jit(solution)/shard_map/project_gather/ppermute | solution.py:254
  129.5 4.6 %collective-permute-start.3 = (bf16[2048,128]{1,0:T(8,128)(2,1)S(1)}, bf16[2048,128]{1,0:T(8,128)(2,1)S(1)}, u32[]{:S(2)}, u32[]{:S(2)}) collective-permute-start(bf16[2048,128]{1,0:T(8,128)(2,1)S(1)} %convolution_convert_fusion), channel_id=1, source_target_pairs={{0,16},{16,0},{1,17},{17,1},{2,18},{18,2},{3,19},{19,3},{4,20},{20... | collective-permute-start | bytes 1572872 | tf_op jit(solution)/shard_map/gram_core/ppermute | solution.py:207
  202.6 10.0 %collective-permute-start.4 = (bf16[2048,128]{1,0:T(8,128)(2,1)S(1)}, bf16[2048,128]{1,0:T(8,128)(2,1)S(1)}, u32[]{:S(2)}, u32[]{:S(2)}) collective-permute-start(bf16[2048,128]{1,0:T(8,128)(2,1)S(1)} %bitcast.58), channel_id=1, source_target_pairs={{0,16},{16,0},{1,17},{17,1},{2,18},{18,2},{3,19},{19,3},{4,20},{20... | collective-permute-start | bytes 1572872 | tf_op jit(solution)/shard_map/gram_gather/ppermute | solution.py:207
  249.7 7.2 %collective-permute-start.5 = (bf16[2064,512]{1,0:T(8,128)(2,1)S(1)}, bf16[2064,512]{1,0:T(8,128)(2,1)S(1)}, u32[]{:S(2)}, u32[]{:S(2)}) collective-permute-start(bf16[2064,512]{1,0:T(8,128)(2,1)S(1)} %grad.1.grad_ref), channel_id=1, source_target_pairs={{0,16},{16,0},{1,17},{17,1},{2,18},{18,2},{3,19},{19,3},{4,20},{20... | collective-permute-start | bytes 6340616 | tf_op jit(solution)/shard_map/grad_swap/ppermute | solution.py:207

commit v10 on v9

--- a/solution.py
+++ b/solution.py
@@ -113,8 +113,21 @@
     lax.fori_loop(0, n_chip, second, 0)
 
 
-def order_kernel(place_ref, rows_ref, own_ref, sent_ref):
-    depth = rows_ref.shape[1] // 32
+def order_kernel(place_ref, rows_ref, own_ref, sent_ref, view_ref):
+    n, width = rows_ref.shape
+    depth = width // 32
+
+    def blocks(view):
+        for j in range(32):
+            view_ref[j] = rows_ref[view * n // 2 : (view + 1) * n // 2, j * depth : (j + 1) * depth]
+
+    @pl.when(place_ref[1] == 0)
+    def _():
+        blocks(0)
+
+    @pl.when(place_ref[1] != 0)
+    def _():
+        blocks(1)
 
     def pick(core, out_ref):
         for j in range(16):
@@ -214,14 +227,13 @@
 
     with jax.named_scope("embeds_exchange"):
         by_view = lax.optimization_barrier(embeds.transpose(1, 0, 2).reshape(2 * local_rows, d_in))
-        one_view = lax.dynamic_slice_in_dim(by_view, odd * local_rows, local_rows, axis=0)
-        one_view = one_view.reshape(local_rows, n_batch, depth).transpose(1, 0, 2)
     with jax.named_scope("embeds_order"):
-        own_rows, sent_rows = pl.pallas_call(
+        own_rows, sent_rows, one_view = pl.pallas_call(
             order_kernel,
-            out_shape=[jax.ShapeDtypeStruct((2 * local_rows, n_chip * depth), BF16)] * 2,
+            out_shape=[jax.ShapeDtypeStruct((2 * local_rows, n_chip * depth), BF16)] * 2
+            + [jax.ShapeDtypeStruct((n_batch, local_rows, depth), BF16)],
             in_specs=[smem, vmem],
-            out_specs=[vmem, vmem],
+            out_specs=[vmem] * 3,
             compiler_params=params,
             name="order",
         )(place, by_view)
@@ -300,13 +312,12 @@
     with jax.named_scope("gram_gather"):
         gram_t = gather(gather(gram_block, "z1"), "z0").reshape(n_rows, chip_rows)
         other_gram = swap_core(gram_t)
-        gram_a = jnp.where(first, gram_t, other_gram).astype(F32)
-        gram_b = jnp.where(first, other_gram, gram_t).astype(F32)
     with jax.named_scope("back"):
-        off_local = jnp.sum(gram_a * gram_b, axis=0)
-        back_a = split_product(gram_b, view_a)
-        back_b = split_product(gram_a, view_b)
-        back = jnp.concatenate([back_a, back_b], axis=1).astype(BF16)
+        own_gram, other_gram = gram_t.astype(F32), other_gram.astype(F32)
+        with_own = split_product(own_gram, jnp.where(first, view_b, view_a))
+        with_other = split_product(other_gram, jnp.where(first, view_a, view_b))
+        off_local = jnp.sum(own_gram * other_gram, axis=0)
+        back = in_core_order(with_other, with_own, 1).astype(BF16)
         terms = jnp.concatenate([off_local, jnp.zeros((width_out - chip_rows,), F32)])
         block = with_rows(back, pieces(terms))
     with jax.named_scope("back_gather"):

time: 261 us -> 258 us (0.989)
  local copies, waits for them, and re-layouts: 15.9 us -> 13 us
  transfers between devices with their start and end apart: 9 -> 9, of which waited for: 7 -> 7; matrix products, arithmetic and copies ran while one was open for 4% -> 3% of each run, Pallas kernels for 2% -> 2%
where the time goes in v10:
time: 258 us; the launch traced here: 257 us
  blocking collectives  131 us (51%)
  waiting for transfers between devices  53.8 us (21%)
  starting transfers between devices  41.9 us (16%)
  local copies, waits for them, and re-layouts  13 us (5%)
  Pallas kernels  10.9 us (4%)
  other arithmetic  3.12 us (1%)
    all_to_all x5, blocking collectives, exchange(): return lax.all_to_all(blocks, axes, split_axis=0, concat_axis=0, tiled=True)  100 us
    all_to_all x2, waiting for transfers between devices, exchange(): return lax.all_to_all(blocks, axes, split_axis=0, concat_axis=0, tiled=True)  44.6 us
    all_to_all x1, blocking collectives, ring_gather(): lax.all_to_all(blocks, BATCH, split_axis=0, concat_axis=0, tiled=True, ax...  31 us
    ppermute x5, starting transfers between devices, swap_core(): return lax.ppermute(a, 'core', [(0, 1), (1, 0)])  26.7 us
    all_to_all x2, starting transfers between devices, exchange(): return lax.all_to_all(blocks, axes, split_axis=0, concat_axis=0, tiled=True)  8.19 us
  transfers between devices with their start and end apart: 9, of which 7 were waited for; matrix products, arithmetic and copies ran while one was open for 3% of the time, Pallas kernels for 2%

profile of v10, /device:TPU:1, one launch (start us, length us, event | category | flops | bytes accessed | tf_op | source)
XLA Modules:
  0.0 257.3 jit_solution(12438879584638304831)
XLA Ops:
  0.6 2.1 broadcast_in_dim.139
  2.7 5.0 %all-to-all-start = ((bf16[4,256,512]{2,1,0:T(8,128)(2,1)}), bf16[4,256,512]{2,1,0:T(8,128)(2,1)}, u32[]{:S(2)}, u32[]{:S(2)}) async-start(bf16[4,256,512]{2,1,0:T(8,128)(2,1)} %broadcast_in_dim.139), calls=%async_computation | async-start | bytes 2097152 | tf_op jit(solution)/shard_map/weight_gather/all_to_all | solution.py:74
  7.7 2.7 %copy.8 = bf16[2,64,8192]{2,1,0:T(8,128)(2,1)S(1)} copy(bf16[2,64,8192]{2,0,1:T(2,128)(2,1)} %bitcast.54) | data formatting | bytes 4194304 | tf_op jit(solution)/shard_map/embeds_exchange/transpose | solution.py:229
  10.5 1.8 order.1
  12.4 1.0 copy-done.1
  13.4 4.2 %all-to-all-done = bf16[4,256,512]{2,1,0:T(8,128)(2,1)} async-done(((bf16[4,256,512]{2,1,0:T(8,128)(2,1)}), bf16[4,256,512]{2,1,0:T(8,128)(2,1)}, u32[]{:S(2)}, u32[]{:S(2)}) %all-to-all-start) | async-done | bytes 1048608 | tf_op jit(solution)/shard_map/weight_gather/all_to_all | solution.py:74
  17.6 1.6 broadcast_in_dim.140
  19.2 31.0 %all_to_all.45 = bf16[4,4,256,512]{3,2,1,0:T(8,128)(2,1)} all-to-all(bf16[4,4,256,512]{3,2,1,0:T(8,128)(2,1)S(1)} %broadcast_in_dim.140), channel_id=1, replica_groups={{0,128,256,384},{32,160,288,416},{64,192,320,448},{96,224,352,480},{16,..., dimensions={0} | all-to-all | bytes 8388608 | tf_op jit(solution)/shard_map/weight_gather/all_to_all | solution.py:74
  50.2 9.5 %collective-permute-start = (bf16[128,4096]{1,0:T(8,128)(2,1)S(1)}, bf16[128,4096]{1,0:T(8,128)(2,1)S(1)}, u32[]{:S(2)}, u32[]{:S(2)}) collective-permute-start(bf16[128,4096]{1,0:T(8,128)(2,1)S(1)} %copy-done.2), channel_id=1, source_target_pairs={{0,16},{16,0},{1,17},{17,1},{2,18},{18,2},{3,19},{19,3},{4,20},{20... | collective-permute-start | bytes 3145736 | tf_op jit(solution)/shard_map/weight_gather/ppermute | solution.py:220
  59.6 4.5 %all-to-all-start.2 = ((bf16[32,64,256]{2,1,0:T(8,128)(2,1)}), bf16[32,64,256]{2,1,0:T(8,128)(2,1)}, u32[]{:S(2)}, u32[]{:S(2)}) async-start(bf16[32,64,256]{2,1,0:T(8,128)(2,1)} %get-tuple-element.41), calls=%async_computation.2 | async-start | bytes 2097152 | tf_op jit(solution)/shard_map/weight_gather/all_to_all | solution.py:25
  64.1 2.2 copy-done
  66.3 1.8 project.1
  68.1 13.1 %all-to-all-done.2 = bf16[32,64,256]{2,1,0:T(8,128)(2,1)} async-done(((bf16[32,64,256]{2,1,0:T(8,128)(2,1)}), bf16[32,64,256]{2,1,0:T(8,128)(2,1)}, u32[]{:S(2)}, u32[]{:S(2)}) %all-to-all-start.2) | async-done | bytes 1048608 | tf_op jit(solution)/shard_map/weight_gather/all_to_all | solution.py:25
  81.2 2.3 collective-permute-start.1
  83.6 1.1 collective-permute-done.1
  84.8 0.1 select_select_fusion
  84.9 1.5 broadcast_in_dim.146
  86.4 3.7 %all-to-all-start.3 = ((bf16[16,136,512]{2,1,0:T(8,128)(2,1)}), bf16[16,136,512]{2,1,0:T(8,128)(2,1)S(1)}, u32[]{:S(2)}, u32[]{:S(2)}) async-start(bf16[16,136,512]{2,1,0:T(8,128)(2,1)} %broadcast_in_dim.146), calls=%async_computation.3 | async-start | bytes 4456448 | tf_op jit(solution)/shard_map/project_gather/all_to_all | solution.py:25
  90.2 1.5 copy.9
  91.7 1.9 collective-permute-start.2
  93.6 31.5 %all-to-all-done.3.got_ref = bf16[16,136,512]{2,1,0:T(8,128)(2,1)S(1)} async-done(((bf16[16,136,512]{2,1,0:T(8,128)(2,1)}), bf16[16,136,512]{2,1,0:T(8,128)(2,1)S(1)}, u32[]{:S(2)}, u32[]{:S(2)}) %all-to-all-start.3) | async-done | bytes 2228256 | tf_op jit(solution)/shard_map/project_gather/all_to_all | solution.py:25
  125.2 0.7 multiply_reduce_fusion
  125.9 0.6 fusion
  126.5 0.3 multiply_reduce_fusion.1
  126.8 0.1 broadcast_select_fusion
  127.0 0.4 convolution_convert_fusion
  127.4 0.4 fusion.14
  127.9 3.1 %collective-permute-start.3 = (bf16[2048,128]{1,0:T(8,128)(2,1)S(1)}, bf16[2048,128]{1,0:T(8,128)(2,1)S(1)}, u32[]{:S(2)}, u32[]{:S(2)}) collective-permute-start(bf16[2048,128]{1,0:T(8,128)(2,1)S(1)} %convolution_convert_fusion), channel_id=1, source_target_pairs={{0,16},{16,0},{1,17},{17,1},{2,18},{18,2},{3,19},{19,3},{4,20},{20... | collective-permute-start | bytes 1572872 | tf_op jit(solution)/shard_map/gram_core/ppermute | solution.py:220
  131.2 1.3 collective-permute-done.3
  132.7 16.8 %all_to_all.46 = bf16[4,520,128]{2,1,0:T(8,128)(2,1)S(1)} all-to-all(bf16[4,520,128]{2,1,0:T(8,128)(2,1)S(1)} %pad_maximum_fusion), channel_id=1, replica_groups=mesh['y'=4,'x'=4,'core'=2,'z1'=4,'z0'=4] {'z0'}, dimensions={0} | all-to-all | bytes 1064960 | tf_op jit(solution)/shard_map/gram_reduce/all_to_all | solution.py:25
  149.7 23.8 %all_to_all.47 = bf16[4,136,128]{2,1,0:T(8,128)(2,1)S(1)} all-to-all(bf16[4,136,128]{2,1,0:T(8,128)(2,1)S(1)} %pad_maximum_fusion.1), channel_id=1, replica_groups=mesh['y'=4,'x'=4,'core'=2,'z1'=4,'z0'=4] {'z1'}, dimensions={0} | all-to-all | bytes 278528 | tf_op jit(solution)/shard_map/gram_reduce/all_to_all | solution.py:25
  173.6 15.4 %all_to_all.48 = bf16[4,128,128]{2,1,0:T(8,128)(2,1)S(1)} all-to-all(bf16[4,128,128]{2,1,0:T(8,128)(2,1)S(1)} %broadcast_in_dim.149), channel_id=1, replica_groups=mesh['y'=4,'x'=4,'core'=2,'z1'=4,'z0'=4] {'z1'}, dimensions={0} | all-to-all | bytes 262144 | tf_op jit(solution)/shard_map/gram_gather/all_to_all | solution.py:25
  189.1 11.8 %all_to_all.49 = bf16[4,4,128,128]{3,2,1,0:T(8,128)(2,1)S(1)} all-to-all(bf16[4,4,128,128]{3,2,1,0:T(8,128)(2,1)S(1)} %broadcast_in_dim.150), channel_id=1, replica_groups=mesh['y'=4,'x'=4,'core'=2,'z1'=4,'z0'=4] {'z0'}, dimensions={0} | all-to-all | bytes 1048576 | tf_op jit(solution)/shard_map/gram_gather/all_to_all | solution.py:25
  200.9 8.5 %collective-permute-start.4 = (bf16[2048,128]{1,0:T(8,128)(2,1)S(1)}, bf16[2048,128]{1,0:T(8,128)(2,1)S(1)}, u32[]{:S(2)}, u32[]{:S(2)}) collective-permute-start(bf16[2048,128]{1,0:T(8,128)(2,1)S(1)} %bitcast.51), channel_id=1, source_target_pairs={{0,16},{16,0},{1,17},{17,1},{2,18},{18,2},{3,19},{19,3},{4,20},{20... | collective-permute-start | bytes 1572872 | tf_op jit(solution)/shard_map/gram_gather/ppermute | solution.py:220
  209.4 0.3 fusion.28
  209.8 0.4 convolution_add_fusion
  210.1 0.8 collective-permute-done.4
  210.9 0.3 fusion.2
  211.3 0.3 fusion.4
  211.6 0.4 select_convert_fusion.1
  212.0 0.1 fusion.13
  212.1 0.1 broadcast_in_dim.154
  212.3 32.6 %all_to_all.50.back_ref = bf16[16,136,512]{2,1,0:T(8,128)(2,1)S(1)} all-to-all(bf16[16,136,512]{2,1,0:T(8,128)(2,1)S(1)} %broadcast_in_dim.154), channel_id=1, replica_groups=mesh['y'=4,'x'=4,'core'=2,'z1'=4,'z0'=4] {'y','x'}, dimensions={0} | all-to-all | bytes 4456448 | tf_op jit(solution)/shard_map/back_gather/all_to_all | solution.py:25
  244.9 2.4 grad.1.grad_ref
  247.3 3.4 %collective-permute-start.5 = (bf16[2064,512]{1,0:T(8,128)(2,1)S(1)}, bf16[2064,512]{1,0:T(8,128)(2,1)S(1)}, u32[]{:S(2)}, u32[]{:S(2)}) collective-permute-start(bf16[2064,512]{1,0:T(8,128)(2,1)S(1)} %grad.1.grad_ref), channel_id=1, source_target_pairs={{0,16},{16,0},{1,17},{17,1},{2,18},{18,2},{3,19},{19,3},{4,20},{20... | collective-permute-start | bytes 6340616 | tf_op jit(solution)/shard_map/grad_swap/ppermute | solution.py:220
  250.7 2.0 own_half.1.mine_ref
  252.7 1.8 collective-permute-done.5.grad_ref
  254.5 2.9 %other_half.1 = (f32[256,512]{1,0:T(8,128)}, f32[1]{0:T(128)}) custom-call(s32[2]{0:T(128)S(1)} %pad_add_fusion.place_ref, bf16[256,2048]{1,0:T(8,128)(2,1)S(1)} %bitcast.44, bf16[256,2048]{1,0:T(8,128)(2,1)} %collective-permute-done.2.other_ref, bf16[2064,512]{1,0:T(8,128)(2,1)S(1)} %collective-permute-done.5.grad_ref, f32[256,256]{1,0:T(8,128)S(1)} %own_half.1.mine_ref, ...), custom_call_target="tpu_custom_call" | custom-call | tf_op jit(solution)/shard_map/weight_grad/other_half/pallas_call | solution.py:349
  (41 shorter events, 1.0 us)
Async XLA Ops:
  2.7 14.9 %all-to-all-start = ((bf16[4,256,512]{2,1,0:T(8,128)(2,1)}), bf16[4,256,512]{2,1,0:T(8,128)(2,1)}, u32[]{:S(2)}, u32[]{:S(2)}) async-start(bf16[4,256,512]{2,1,0:T(8,128)(2,1)} %broadcast_in_dim.139), calls=%async_computation | async-start | bytes 2097152 | tf_op jit(solution)/shard_map/weight_gather/all_to_all | solution.py:74
  12.4 1.0 copy-start.1
  19.2 31.0 %copy-start.2 = (bf16[128,4096]{1,0:T(8,128)(2,1)S(1)}, bf16[128,4096]{1,0:T(8,128)(2,1)}, u32[]{:S(2)}) copy-start(bf16[128,4096]{1,0:T(8,128)(2,1)} %copy-done.1) | copy-start | bytes 3145732
  50.2 13.9 %collective-permute-start = (bf16[128,4096]{1,0:T(8,128)(2,1)S(1)}, bf16[128,4096]{1,0:T(8,128)(2,1)S(1)}, u32[]{:S(2)}, u32[]{:S(2)}) collective-permute-start(bf16[128,4096]{1,0:T(8,128)(2,1)S(1)} %copy-done.2), channel_id=1, source_target_pairs={{0,16},{16,0},{1,17},{17,1},{2,18},{18,2},{3,19},{19,3},{4,20},{20... | collective-permute-start | bytes 3145736 | tf_op jit(solution)/shard_map/weight_gather/ppermute | solution.py:220
  59.6 21.6 %all-to-all-start.2 = ((bf16[32,64,256]{2,1,0:T(8,128)(2,1)}), bf16[32,64,256]{2,1,0:T(8,128)(2,1)}, u32[]{:S(2)}, u32[]{:S(2)}) async-start(bf16[32,64,256]{2,1,0:T(8,128)(2,1)} %get-tuple-element.41), calls=%async_computation.2 | async-start | bytes 2097152 | tf_op jit(solution)/shard_map/weight_gather/all_to_all | solution.py:25
  64.1 2.2 copy-start
  81.2 3.4 %collective-permute-start.1 = (f32[128,512]{1,0:T(8,128)S(1)}, f32[128,512]{1,0:T(8,128)S(1)}, u32[]{:S(2)}, u32[]{:S(2)}) collective-permute-start(f32[128,512]{1,0:T(8,128)S(1)} %get-tuple-element.43), channel_id=1, source_target_pairs={{0,16},{16,0},{1,17},{17,1},{2,18},{18,2},{3,19},{19,3},{4,20},{20... | collective-permute-start | bytes 786440 | tf_op jit(solution)/shard_map/project/ppermute | solution.py:220
  86.4 38.6 %all-to-all-start.3 = ((bf16[16,136,512]{2,1,0:T(8,128)(2,1)}), bf16[16,136,512]{2,1,0:T(8,128)(2,1)S(1)}, u32[]{:S(2)}, u32[]{:S(2)}) async-start(bf16[16,136,512]{2,1,0:T(8,128)(2,1)} %broadcast_in_dim.146), calls=%async_computation.3 | async-start | bytes 4456448 | tf_op jit(solution)/shard_map/project_gather/all_to_all | solution.py:25
  91.7 36.2 %collective-permute-start.2 = (bf16[256,2048]{1,0:T(8,128)(2,1)S(1)}, bf16[256,2048]{1,0:T(8,128)(2,1)}, u32[]{:S(2)}, u32[]{:S(2)}) collective-permute-start(bf16[256,2048]{1,0:T(8,128)(2,1)S(1)} %bitcast.42), channel_id=1, source_target_pairs={{0,1},{1,0},{2,3},{3,2},{4,5},{5,4},{6,7},{7,6},{8,9},{9,8},{10,11... | collective-permute-start | bytes 3145736 | tf_op jit(solution)/shard_map/project_gather/ppermute | solution.py:266
  127.9 4.6 %collective-permute-start.3 = (bf16[2048,128]{1,0:T(8,128)(2,1)S(1)}, bf16[2048,128]{1,0:T(8,128)(2,1)S(1)}, u32[]{:S(2)}, u32[]{:S(2)}) collective-permute-start(bf16[2048,128]{1,0:T(8,128)(2,1)S(1)} %convolution_convert_fusion), channel_id=1, source_target_pairs={{0,16},{16,0},{1,17},{17,1},{2,18},{18,2},{3,19},{19,3},{4,20},{20... | collective-permute-start | bytes 1572872 | tf_op jit(solution)/shard_map/gram_core/ppermute | solution.py:220
  200.9 10.0 %collective-permute-start.4 = (bf16[2048,128]{1,0:T(8,128)(2,1)S(1)}, bf16[2048,128]{1,0:T(8,128)(2,1)S(1)}, u32[]{:S(2)}, u32[]{:S(2)}) collective-permute-start(bf16[2048,128]{1,0:T(8,128)(2,1)S(1)} %bitcast.51), channel_id=1, source_target_pairs={{0,16},{16,0},{1,17},{17,1},{2,18},{18,2},{3,19},{19,3},{4,20},{20... | collective-permute-start | bytes 1572872 | tf_op jit(solution)/shard_map/gram_gather/ppermute | solution.py:220
  247.3 7.2 %collective-permute-start.5 = (bf16[2064,512]{1,0:T(8,128)(2,1)S(1)}, bf16[2064,512]{1,0:T(8,128)(2,1)S(1)}, u32[]{:S(2)}, u32[]{:S(2)}) collective-permute-start(bf16[2064,512]{1,0:T(8,128)(2,1)S(1)} %grad.1.grad_ref), channel_id=1, source_target_pairs={{0,16},{16,0},{1,17},{17,1},{2,18},{18,2},{3,19},{19,3},{4,20},{20... | collective-permute-start | bytes 6340616 | tf_op jit(solution)/shard_map/grad_swap/ppermute | solution.py:220

commit v11 on v10

--- a/solution.py
+++ b/solution.py
@@ -254,12 +254,12 @@
             compiler_params=params,
             name="project",
         )(place, own_rows, other_rows, core_weight)
-        kept, sent, one_view = lax.optimization_barrier((kept, sent, one_view))
         got_other, got_own = jnp.split(swap_core(sent), 2)
         own, other = jnp.split(kept, 2)
         projected = in_core_order(own + got_own, other + got_other, 0)
     with jax.named_scope("project_gather"):
         chip_mean = jnp.sum(projected, axis=0) / chip_rows
+        projected, chip_mean, one_view = lax.optimization_barrier((projected, chip_mean, one_view))
         block = with_rows((projected - chip_mean).astype(BF16), pieces(chip_mean))
         block, one_view = lax.optimization_barrier((block, one_view))
         one_t = one_view.T

time: 258 us -> 255 us (0.988)
  waiting for transfers between devices: 53.8 us -> 50.3 us
    all_to_all x2, waiting for transfers between devices: 44.6 us -> 41 us  [exchange(): return lax.all_to_all(blocks, axes, split_axis=0, concat_axis=0, tiled=True)]
where the time goes in v11:
time: 255 us; the launch traced here: 254 us
  blocking collectives  131 us (51%)
  waiting for transfers between devices  50.3 us (20%)
  starting transfers between devices  41.7 us (16%)
  local copies, waits for them, and re-layouts  13 us (5%)
  Pallas kernels  10.9 us (4%)
  other arithmetic  3.13 us (1%)
    all_to_all x5, blocking collectives, exchange(): return lax.all_to_all(blocks, axes, split_axis=0, concat_axis=0, tiled=True)  100 us
    all_to_all x2, waiting for transfers between devices, exchange(): return lax.all_to_all(blocks, axes, split_axis=0, concat_axis=0, tiled=True)  41 us
    all_to_all x1, blocking collectives, ring_gather(): lax.all_to_all(blocks, BATCH, split_axis=0, concat_axis=0, tiled=True, ax...  31 us
    ppermute x5, starting transfers between devices, swap_core(): return lax.ppermute(a, 'core', [(0, 1), (1, 0)])  26.6 us
    all_to_all x2, starting transfers between devices, exchange(): return lax.all_to_all(blocks, axes, split_axis=0, concat_axis=0, tiled=True)  8.19 us
    ppermute x5, waiting for transfers between devices, swap_core(): return lax.ppermute(a, 'core', [(0, 1), (1, 0)])  5.17 us
  transfers between devices with their start and end apart: 9, of which 7 were waited for; matrix products, arithmetic and copies ran while one was open for 3% of the time, Pallas kernels for 2%

profile of v11, /device:TPU:1, one launch (start us, length us, event | category | flops | bytes accessed | tf_op | source)
XLA Modules:
  0.0 253.8 jit_solution(4433538499589493003)
XLA Ops:
  0.6 2.1 broadcast_in_dim.139
  2.7 5.0 %all-to-all-start = ((bf16[4,256,512]{2,1,0:T(8,128)(2,1)}), bf16[4,256,512]{2,1,0:T(8,128)(2,1)}, u32[]{:S(2)}, u32[]{:S(2)}) async-start(bf16[4,256,512]{2,1,0:T(8,128)(2,1)} %broadcast_in_dim.139), calls=%async_computation | async-start | bytes 2097152 | tf_op jit(solution)/shard_map/weight_gather/all_to_all | solution.py:74
  7.7 2.7 %copy.8 = bf16[2,64,8192]{2,1,0:T(8,128)(2,1)S(1)} copy(bf16[2,64,8192]{2,0,1:T(2,128)(2,1)} %bitcast.54) | data formatting | bytes 4194304 | tf_op jit(solution)/shard_map/embeds_exchange/transpose | solution.py:229
  10.5 1.8 order.1
  12.4 1.0 copy-done.1
  13.4 4.2 %all-to-all-done = bf16[4,256,512]{2,1,0:T(8,128)(2,1)} async-done(((bf16[4,256,512]{2,1,0:T(8,128)(2,1)}), bf16[4,256,512]{2,1,0:T(8,128)(2,1)}, u32[]{:S(2)}, u32[]{:S(2)}) %all-to-all-start) | async-done | bytes 1048608 | tf_op jit(solution)/shard_map/weight_gather/all_to_all | solution.py:74
  17.6 1.6 broadcast_in_dim.140
  19.2 31.0 %all_to_all.45 = bf16[4,4,256,512]{3,2,1,0:T(8,128)(2,1)} all-to-all(bf16[4,4,256,512]{3,2,1,0:T(8,128)(2,1)S(1)} %broadcast_in_dim.140), channel_id=1, replica_groups={{0,128,256,384},{32,160,288,416},{64,192,320,448},{96,224,352,480},{16,..., dimensions={0} | all-to-all | bytes 8388608 | tf_op jit(solution)/shard_map/weight_gather/all_to_all | solution.py:74
  50.2 9.5 %collective-permute-start = (bf16[128,4096]{1,0:T(8,128)(2,1)S(1)}, bf16[128,4096]{1,0:T(8,128)(2,1)S(1)}, u32[]{:S(2)}, u32[]{:S(2)}) collective-permute-start(bf16[128,4096]{1,0:T(8,128)(2,1)S(1)} %copy-done.2), channel_id=1, source_target_pairs={{0,16},{16,0},{1,17},{17,1},{2,18},{18,2},{3,19},{19,3},{4,20},{20... | collective-permute-start | bytes 3145736 | tf_op jit(solution)/shard_map/weight_gather/ppermute | solution.py:220
  59.6 4.5 %all-to-all-start.2 = ((bf16[32,64,256]{2,1,0:T(8,128)(2,1)}), bf16[32,64,256]{2,1,0:T(8,128)(2,1)}, u32[]{:S(2)}, u32[]{:S(2)}) async-start(bf16[32,64,256]{2,1,0:T(8,128)(2,1)} %get-tuple-element.41), calls=%async_computation.2 | async-start | bytes 2097152 | tf_op jit(solution)/shard_map/weight_gather/all_to_all | solution.py:25
  64.1 2.2 copy-done
  66.3 1.8 project.1
  68.1 2.1 collective-permute-start.1
  70.3 1.3 collective-permute-done.1
  71.6 9.6 %all-to-all-done.2 = bf16[32,64,256]{2,1,0:T(8,128)(2,1)} async-done(((bf16[32,64,256]{2,1,0:T(8,128)(2,1)}), bf16[32,64,256]{2,1,0:T(8,128)(2,1)}, u32[]{:S(2)}, u32[]{:S(2)}) %all-to-all-start.2) | async-done | bytes 1048608 | tf_op jit(solution)/shard_map/weight_gather/all_to_all | solution.py:25
  81.3 0.1 select_select_fusion
  81.4 1.5 broadcast_in_dim.146
  82.9 3.7 %all-to-all-start.3 = ((bf16[16,136,512]{2,1,0:T(8,128)(2,1)}), bf16[16,136,512]{2,1,0:T(8,128)(2,1)S(1)}, u32[]{:S(2)}, u32[]{:S(2)}) async-start(bf16[16,136,512]{2,1,0:T(8,128)(2,1)} %broadcast_in_dim.146), calls=%async_computation.3 | async-start | bytes 4456448 | tf_op jit(solution)/shard_map/project_gather/all_to_all | solution.py:25
  86.7 1.5 copy.9
  88.2 1.9 collective-permute-start.2
  90.1 31.4 %all-to-all-done.3.got_ref = bf16[16,136,512]{2,1,0:T(8,128)(2,1)S(1)} async-done(((bf16[16,136,512]{2,1,0:T(8,128)(2,1)}), bf16[16,136,512]{2,1,0:T(8,128)(2,1)S(1)}, u32[]{:S(2)}, u32[]{:S(2)}) %all-to-all-start.3) | async-done | bytes 2228256 | tf_op jit(solution)/shard_map/project_gather/all_to_all | solution.py:25
  121.6 0.7 multiply_reduce_fusion
  122.3 0.6 fusion
  122.9 0.3 multiply_reduce_fusion.1
  123.2 0.1 broadcast_select_fusion
  123.4 0.4 convolution_convert_fusion
  123.8 0.4 fusion.13
  124.3 3.1 %collective-permute-start.3 = (bf16[2048,128]{1,0:T(8,128)(2,1)S(1)}, bf16[2048,128]{1,0:T(8,128)(2,1)S(1)}, u32[]{:S(2)}, u32[]{:S(2)}) collective-permute-start(bf16[2048,128]{1,0:T(8,128)(2,1)S(1)} %convolution_convert_fusion), channel_id=1, source_target_pairs={{0,16},{16,0},{1,17},{17,1},{2,18},{18,2},{3,19},{19,3},{4,20},{20... | collective-permute-start | bytes 1572872 | tf_op jit(solution)/shard_map/gram_core/ppermute | solution.py:220
  127.6 1.3 collective-permute-done.3
  129.1 16.8 %all_to_all.46 = bf16[4,520,128]{2,1,0:T(8,128)(2,1)S(1)} all-to-all(bf16[4,520,128]{2,1,0:T(8,128)(2,1)S(1)} %pad_maximum_fusion), channel_id=1, replica_groups=mesh['y'=4,'x'=4,'core'=2,'z1'=4,'z0'=4] {'z0'}, dimensions={0} | all-to-all | bytes 1064960 | tf_op jit(solution)/shard_map/gram_reduce/all_to_all | solution.py:25
  146.1 23.8 %all_to_all.47 = bf16[4,136,128]{2,1,0:T(8,128)(2,1)S(1)} all-to-all(bf16[4,136,128]{2,1,0:T(8,128)(2,1)S(1)} %pad_maximum_fusion.2), channel_id=1, replica_groups=mesh['y'=4,'x'=4,'core'=2,'z1'=4,'z0'=4] {'z1'}, dimensions={0} | all-to-all | bytes 278528 | tf_op jit(solution)/shard_map/gram_reduce/all_to_all | solution.py:25
  170.0 15.4 %all_to_all.48 = bf16[4,128,128]{2,1,0:T(8,128)(2,1)S(1)} all-to-all(bf16[4,128,128]{2,1,0:T(8,128)(2,1)S(1)} %broadcast_in_dim.149), channel_id=1, replica_groups=mesh['y'=4,'x'=4,'core'=2,'z1'=4,'z0'=4] {'z1'}, dimensions={0} | all-to-all | bytes 262144 | tf_op jit(solution)/shard_map/gram_gather/all_to_all | solution.py:25
  185.5 11.8 %all_to_all.49 = bf16[4,4,128,128]{3,2,1,0:T(8,128)(2,1)S(1)} all-to-all(bf16[4,4,128,128]{3,2,1,0:T(8,128)(2,1)S(1)} %broadcast_in_dim.150), channel_id=1, replica_groups=mesh['y'=4,'x'=4,'core'=2,'z1'=4,'z0'=4] {'z0'}, dimensions={0} | all-to-all | bytes 1048576 | tf_op jit(solution)/shard_map/gram_gather/all_to_all | solution.py:25
  197.4 8.5 %collective-permute-start.4 = (bf16[2048,128]{1,0:T(8,128)(2,1)S(1)}, bf16[2048,128]{1,0:T(8,128)(2,1)S(1)}, u32[]{:S(2)}, u32[]{:S(2)}) collective-permute-start(bf16[2048,128]{1,0:T(8,128)(2,1)S(1)} %bitcast.51), channel_id=1, source_target_pairs={{0,16},{16,0},{1,17},{17,1},{2,18},{18,2},{3,19},{19,3},{4,20},{20... | collective-permute-start | bytes 1572872 | tf_op jit(solution)/shard_map/gram_gather/ppermute | solution.py:220
  205.9 0.3 fusion.27
  206.2 0.4 convolution_add_fusion
  206.6 0.8 collective-permute-done.4
  207.4 0.3 fusion.2
  207.7 0.3 fusion.4
  208.1 0.4 select_convert_fusion.1
  208.4 0.1 fusion.12
  208.6 0.1 broadcast_in_dim.154
  208.7 32.6 %all_to_all.50.back_ref = bf16[16,136,512]{2,1,0:T(8,128)(2,1)S(1)} all-to-all(bf16[16,136,512]{2,1,0:T(8,128)(2,1)S(1)} %broadcast_in_dim.154), channel_id=1, replica_groups=mesh['y'=4,'x'=4,'core'=2,'z1'=4,'z0'=4] {'y','x'}, dimensions={0} | all-to-all | bytes 4456448 | tf_op jit(solution)/shard_map/back_gather/all_to_all | solution.py:25
  241.3 2.4 grad.1.grad_ref
  243.7 3.4 %collective-permute-start.5 = (bf16[2064,512]{1,0:T(8,128)(2,1)S(1)}, bf16[2064,512]{1,0:T(8,128)(2,1)S(1)}, u32[]{:S(2)}, u32[]{:S(2)}) collective-permute-start(bf16[2064,512]{1,0:T(8,128)(2,1)S(1)} %grad.1.grad_ref), channel_id=1, source_target_pairs={{0,16},{16,0},{1,17},{17,1},{2,18},{18,2},{3,19},{19,3},{4,20},{20... | collective-permute-start | bytes 6340616 | tf_op jit(solution)/shard_map/grad_swap/ppermute | solution.py:220
  247.1 2.0 own_half.1.mine_ref
  249.2 1.8 collective-permute-done.5.grad_ref
  250.9 2.9 %other_half.1 = (f32[256,512]{1,0:T(8,128)}, f32[1]{0:T(128)}) custom-call(s32[2]{0:T(128)S(1)} %pad_add_fusion.place_ref, bf16[256,2048]{1,0:T(8,128)(2,1)S(1)} %bitcast.44, bf16[256,2048]{1,0:T(8,128)(2,1)} %collective-permute-done.2.other_ref, bf16[2064,512]{1,0:T(8,128)(2,1)S(1)} %collective-permute-done.5.grad_ref, f32[256,256]{1,0:T(8,128)S(1)} %own_half.1.mine_ref, ...), custom_call_target="tpu_custom_call" | custom-call | tf_op jit(solution)/shard_map/weight_grad/other_half/pallas_call | solution.py:349
  (42 shorter events, 1.1 us)
Async XLA Ops:
  2.7 14.9 %all-to-all-start = ((bf16[4,256,512]{2,1,0:T(8,128)(2,1)}), bf16[4,256,512]{2,1,0:T(8,128)(2,1)}, u32[]{:S(2)}, u32[]{:S(2)}) async-start(bf16[4,256,512]{2,1,0:T(8,128)(2,1)} %broadcast_in_dim.139), calls=%async_computation | async-start | bytes 2097152 | tf_op jit(solution)/shard_map/weight_gather/all_to_all | solution.py:74
  12.4 1.0 copy-start.1
  19.2 31.0 %copy-start.2 = (bf16[128,4096]{1,0:T(8,128)(2,1)S(1)}, bf16[128,4096]{1,0:T(8,128)(2,1)}, u32[]{:S(2)}) copy-start(bf16[128,4096]{1,0:T(8,128)(2,1)} %copy-done.1) | copy-start | bytes 3145732
  50.2 13.9 %collective-permute-start = (bf16[128,4096]{1,0:T(8,128)(2,1)S(1)}, bf16[128,4096]{1,0:T(8,128)(2,1)S(1)}, u32[]{:S(2)}, u32[]{:S(2)}) collective-permute-start(bf16[128,4096]{1,0:T(8,128)(2,1)S(1)} %copy-done.2), channel_id=1, source_target_pairs={{0,16},{16,0},{1,17},{17,1},{2,18},{18,2},{3,19},{19,3},{4,20},{20... | collective-permute-start | bytes 3145736 | tf_op jit(solution)/shard_map/weight_gather/ppermute | solution.py:220
  59.6 21.6 %all-to-all-start.2 = ((bf16[32,64,256]{2,1,0:T(8,128)(2,1)}), bf16[32,64,256]{2,1,0:T(8,128)(2,1)}, u32[]{:S(2)}, u32[]{:S(2)}) async-start(bf16[32,64,256]{2,1,0:T(8,128)(2,1)} %get-tuple-element.41), calls=%async_computation.2 | async-start | bytes 2097152 | tf_op jit(solution)/shard_map/weight_gather/all_to_all | solution.py:25
  64.1 2.2 copy-start
  68.1 3.4 %collective-permute-start.1 = (f32[128,512]{1,0:T(8,128)S(1)}, f32[128,512]{1,0:T(8,128)S(1)}, u32[]{:S(2)}, u32[]{:S(2)}) collective-permute-start(f32[128,512]{1,0:T(8,128)S(1)} %get-tuple-element.40), channel_id=1, source_target_pairs={{0,16},{16,0},{1,17},{17,1},{2,18},{18,2},{3,19},{19,3},{4,20},{20... | collective-permute-start | bytes 786440 | tf_op jit(solution)/shard_map/project/ppermute | solution.py:220
  82.9 38.6 %all-to-all-start.3 = ((bf16[16,136,512]{2,1,0:T(8,128)(2,1)}), bf16[16,136,512]{2,1,0:T(8,128)(2,1)S(1)}, u32[]{:S(2)}, u32[]{:S(2)}) async-start(bf16[16,136,512]{2,1,0:T(8,128)(2,1)} %broadcast_in_dim.146), calls=%async_computation.3 | async-start | bytes 4456448 | tf_op jit(solution)/shard_map/project_gather/all_to_all | solution.py:25
  88.2 36.1 %collective-permute-start.2 = (bf16[256,2048]{1,0:T(8,128)(2,1)S(1)}, bf16[256,2048]{1,0:T(8,128)(2,1)}, u32[]{:S(2)}, u32[]{:S(2)}) collective-permute-start(bf16[256,2048]{1,0:T(8,128)(2,1)S(1)} %bitcast.42), channel_id=1, source_target_pairs={{0,1},{1,0},{2,3},{3,2},{4,5},{5,4},{6,7},{7,6},{8,9},{9,8},{10,11... | collective-permute-start | bytes 3145736 | tf_op jit(solution)/shard_map/project_gather/ppermute | solution.py:266
  124.3 4.7 %collective-permute-start.3 = (bf16[2048,128]{1,0:T(8,128)(2,1)S(1)}, bf16[2048,128]{1,0:T(8,128)(2,1)S(1)}, u32[]{:S(2)}, u32[]{:S(2)}) collective-permute-start(bf16[2048,128]{1,0:T(8,128)(2,1)S(1)} %convolution_convert_fusion), channel_id=1, source_target_pairs={{0,16},{16,0},{1,17},{17,1},{2,18},{18,2},{3,19},{19,3},{4,20},{20... | collective-permute-start | bytes 1572872 | tf_op jit(solution)/shard_map/gram_core/ppermute | solution.py:220
  197.4 10.0 %collective-permute-start.4 = (bf16[2048,128]{1,0:T(8,128)(2,1)S(1)}, bf16[2048,128]{1,0:T(8,128)(2,1)S(1)}, u32[]{:S(2)}, u32[]{:S(2)}) collective-permute-start(bf16[2048,128]{1,0:T(8,128)(2,1)S(1)} %bitcast.51), channel_id=1, source_target_pairs={{0,16},{16,0},{1,17},{17,1},{2,18},{18,2},{3,19},{19,3},{4,20},{20... | collective-permute-start | bytes 1572872 | tf_op jit(solution)/shard_map/gram_gather/ppermute | solution.py:220
  243.7 7.2 %collective-permute-start.5 = (bf16[2064,512]{1,0:T(8,128)(2,1)S(1)}, bf16[2064,512]{1,0:T(8,128)(2,1)S(1)}, u32[]{:S(2)}, u32[]{:S(2)}) collective-permute-start(bf16[2064,512]{1,0:T(8,128)(2,1)S(1)} %grad.1.grad_ref), channel_id=1, source_target_pairs={{0,16},{16,0},{1,17},{17,1},{2,18},{18,2},{3,19},{19,3},{4,20},{20... | collective-permute-start | bytes 6340616 | tf_op jit(solution)/shard_map/grad_swap/ppermute | solution.py:220

commit v12 on v11

--- a/solution.py
+++ b/solution.py
@@ -160,33 +160,38 @@
         sent_ref[owner * n : (owner + 1) * n, :] = jnp.where(first, high, low)
 
 
-def half_grad(odd, one_ref, other_ref, grad_ref, store):
-    rows, half = one_ref.shape[1], grad_ref.shape[1] // 2
-
-    def product(a_ref, b_ref):
-        return jnp.dot(a_ref[...], grad_ref[:rows, :half], preferred_element_type=F32) + jnp.dot(
-            b_ref[...], grad_ref[:rows, half:], preferred_element_type=F32
-        )
+def half_grad(odd, one_refs, other_refs, grad_ref, store):
+    rows, half = one_refs[0].shape[1], grad_ref.shape[1] // 2
+
+    def product(a_refs, b_refs):
+        total = 0.0
+        for i in range(2):
+            part = slice(i * rows, (i + 1) * rows)
+            total += jnp.dot(a_refs[i][...], grad_ref[part, :half], preferred_element_type=F32)
+            total += jnp.dot(b_refs[i][...], grad_ref[part, half:], preferred_element_type=F32)
+        return total
 
     @pl.when(odd == 0)
     def _():
-        store(product(one_ref, other_ref))
+        store(product(one_refs, other_refs))
 
     @pl.when(odd != 0)
     def _():
-        store(product(other_ref, one_ref))
-
-
-def own_half_kernel(place_ref, one_ref, other_ref, grad_ref, out_ref):
+        store(product(other_refs, one_refs))
+
+
+def own_half_kernel(place_ref, one_low, one_high, other_low, other_high, grad_ref, out_ref):
     def store(value):
         out_ref[...] = value
 
-    half_grad(place_ref[1], one_ref, other_ref, grad_ref, store)
-
-
-def other_half_kernel(off_factor, place_ref, one_ref, other_ref, grad_ref, mine_ref, off_ref, diag_ref, out_ref, loss_ref):
+    half_grad(place_ref[1], (one_low, one_high), (other_low, other_high), grad_ref, store)
+
+
+def other_half_kernel(
+    off_factor, place_ref, one_low, one_high, other_low, other_high, grad_ref, mine_ref, off_ref, diag_ref, out_ref, loss_ref
+):
     first = place_ref[0] == 0
-    rows, terms = one_ref.shape[1], diag_ref.shape[1]
+    rows, terms = 2 * one_low.shape[1], diag_ref.shape[1]
     other_diag = jnp.sum(grad_ref[rows:, :terms].astype(F32), axis=0, keepdims=True)
     loss_ref[0] = jnp.sum(off_factor * off_ref[...] + diag_ref[...] + other_diag) / D_OUT
     half = mine_ref.shape[1]
@@ -196,7 +201,7 @@
         out_ref[:, :half] = jnp.where(first, mine, value)
         out_ref[:, half:] = jnp.where(first, value, mine)
 
-    half_grad(place_ref[1], one_ref, other_ref, grad_ref, store)
+    half_grad(place_ref[1], (one_low, one_high), (other_low, other_high), grad_ref, store)
 
 
 def body(embeds, weight):
@@ -262,8 +267,7 @@
         projected, chip_mean, one_view = lax.optimization_barrier((projected, chip_mean, one_view))
         block = with_rows((projected - chip_mean).astype(BF16), pieces(chip_mean))
         block, one_view = lax.optimization_barrier((block, one_view))
-        one_t = one_view.T
-        other_t = lax.ppermute(one_t, "z0", [(0, 1), (1, 0), (2, 3), (3, 2)])
+        one_low, one_high = one_view[: n_rows // 2].T, one_view[n_rows // 2 :].T
         got = gather(block, PLANE)
     with jax.named_scope("standardize"):
         chip_means = jnp.sum(got[:, chip_rows : chip_rows + 3].astype(F32), axis=1)
@@ -290,8 +294,8 @@
         kept = partial(jnp.where(first, view_a, view_b))
         weight_diag = 2.0 * ((1.0 - off_weight) * diagonal - 1.0)
         factor = loss_scale / n_rows * jnp.concatenate([weight_diag, weight_diag])
-        sent, kept, diag_local, factor, inverse, one_t, other_t = lax.optimization_barrier(
-            (sent, kept, diag_local, factor, inverse, one_t, other_t)
+        sent, kept, diag_local, factor, inverse, one_low, one_high = lax.optimization_barrier(
+            (sent, kept, diag_local, factor, inverse, one_low, one_high)
         )
     with jax.named_scope("gram_core"):
         extra = pad_rows(pieces(diag_local), chip_rows)
@@ -304,13 +308,19 @@
         extra = pad_rows(pieces(jnp.sum(summed[n_rows // n_near :], axis=0)), chip_rows)
         parts = summed[: n_rows // n_near].astype(BF16).reshape(n_far, n_rows // n_feat, chip_rows)
         extra = jnp.broadcast_to(extra[None], (n_far, PAD, chip_rows))
+        parts, extra, one_low = lax.optimization_barrier((parts, extra, one_low))
+        other_low = lax.ppermute(one_low, "z0", [(0, 1), (1, 0), (2, 3), (3, 2)])
         got_z = exchange(jnp.concatenate([parts, extra], axis=1), "z1")
         summed = jnp.sum(got_z.astype(F32), axis=0)
         gram_block = summed[: n_rows // n_feat].astype(BF16)
         diag_terms = jnp.sum(summed[n_rows // n_feat :], axis=0)
-        gram_block, diag_terms = lax.optimization_barrier((gram_block, diag_terms))
+        gram_block, diag_terms, other_low, one_high = lax.optimization_barrier(
+            (gram_block, diag_terms, other_low, one_high)
+        )
     with jax.named_scope("gram_gather"):
-        gram_t = gather(gather(gram_block, "z1"), "z0").reshape(n_rows, chip_rows)
+        other_high = lax.ppermute(one_high, "z0", [(0, 1), (1, 0), (2, 3), (3, 2)])
+        gram_far, other_high = lax.optimization_barrier((gather(gram_block, "z1"), other_high))
+        gram_t = gather(gram_far, "z0").reshape(n_rows, chip_rows)
         other_gram = swap_core(gram_t)
     with jax.named_scope("back"):
         own_gram, other_gram = gram_t.astype(F32), other_gram.astype(F32)
@@ -341,19 +351,19 @@
         mine = pl.pallas_call(
             own_half_kernel,
             out_shape=jax.ShapeDtypeStruct((depth, half), F32),
-            in_specs=[smem] + [vmem] * 3,
+            in_specs=[smem] + [vmem] * 5,
             out_specs=vmem,
             compiler_params=params,
             name="own_half",
-        )(place, one_t, other_t, grad_proj)
+        )(place, one_low, one_high, other_low, other_high, grad_proj)
         grad_weight, loss = pl.pallas_call(
             functools.partial(other_half_kernel, off_weight / (n_rows * n_rows)),
             out_shape=[jax.ShapeDtypeStruct((depth, width_out), F32), jax.ShapeDtypeStruct((1,), F32)],
-            in_specs=[smem] + [vmem] * 6,
+            in_specs=[smem] + [vmem] * 8,
             out_specs=[vmem, smem],
             compiler_params=params,
             name="other_half",
-        )(place, one_t, other_t, other_proj, mine, off_terms, diag_terms[None])
+        )(place, one_low, one_high, other_low, other_high, other_proj, mine, off_terms, diag_terms[None])
     return (loss[0], grad_weight)
 
 

time: 255 us -> 272 us (1.067)
  waiting for transfers between devices: 50.3 us -> 66.2 us
  blocking collectives: 131 us -> 119 us
  starting transfers between devices: 41.7 us -> 53 us
    all_to_all x5 -> x4, blocking collectives: 100 us -> 87.9 us  [exchange(): return lax.all_to_all(blocks, axes, split_axis=0, concat_axis=0, tiled=True)]
    all_to_all x2 -> x3, waiting for transfers between devices: 41 us -> 52.4 us  [exchange(): return lax.all_to_all(blocks, axes, split_axis=0, concat_axis=0, tiled=True)]
    all_to_all x2 -> x3, starting transfers between devices: 8.19 us -> 18.8 us  [exchange(): return lax.all_to_all(blocks, axes, split_axis=0, concat_axis=0, tiled=True)]
    ppermute x1 -> x2, waiting for transfers between devices: 0.01 us -> 4.29 us  [the longest x1 4.28 us: body(): other_low = lax.ppermute(one_low, 'z0', [(0, 1), (1, 0), (2, 3), (3, 2)])]
    ppermute x1 -> x2, starting transfers between devices: 1.92 us -> 6.1 us  [the longest x1 4.1 us: body(): other_high = lax.ppermute(one_high, 'z0', [(0, 1), (1, 0), (2, 3), (3, 2)])]
    ppermute x5, starting transfers between devices: 26.6 us -> 23.1 us  [swap_core(): return lax.ppermute(a, 'core', [(0, 1), (1, 0)])]
  transfers between devices with their start and end apart: 9 -> 11, of which waited for: 7 -> 9; matrix products, arithmetic and copies ran while one was open for 3% -> 3% of each run, Pallas kernels for 2% -> 2%
where the time goes in v12:
time: 272 us; the launch traced here: 271 us
  blocking collectives  119 us (44%)
  waiting for transfers between devices  66.2 us (24%)
  starting transfers between devices  53 us (19%)
  local copies, waits for them, and re-layouts  15.2 us (6%)
  Pallas kernels  10.5 us (4%)
  other arithmetic  3.78 us (1%)
    all_to_all x4, blocking collectives, exchange(): return lax.all_to_all(blocks, axes, split_axis=0, concat_axis=0, tiled=True)  87.9 us
    all_to_all x3, waiting for transfers between devices, exchange(): return lax.all_to_all(blocks, axes, split_axis=0, concat_axis=0, tiled=True)  52.4 us
    all_to_all x1, blocking collectives, ring_gather(): lax.all_to_all(blocks, BATCH, split_axis=0, concat_axis=0, tiled=True, ax...  30.9 us
    ppermute x5, starting transfers between devices, swap_core(): return lax.ppermute(a, 'core', [(0, 1), (1, 0)])  23.1 us
    all_to_all x3, starting transfers between devices, exchange(): return lax.all_to_all(blocks, axes, split_axis=0, concat_axis=0, tiled=True)  18.8 us
  transfers between devices with their start and end apart: 11, of which 9 were waited for; matrix products, arithmetic and copies ran while one was open for 3% of the time, Pallas kernels for 2%

profile of v12, /device:TPU:1, one launch (start us, length us, event | category | flops | bytes accessed | tf_op | source)
XLA Modules:
  0.0 270.8 jit_solution(11857875358937338507)
XLA Ops:
  0.6 2.1 broadcast_in_dim.139
  2.7 5.0 %all-to-all-start = ((bf16[4,256,512]{2,1,0:T(8,128)(2,1)}), bf16[4,256,512]{2,1,0:T(8,128)(2,1)}, u32[]{:S(2)}, u32[]{:S(2)}) async-start(bf16[4,256,512]{2,1,0:T(8,128)(2,1)} %broadcast_in_dim.139), calls=%async_computation | async-start | bytes 2097152 | tf_op jit(solution)/shard_map/weight_gather/all_to_all | solution.py:74
  7.7 2.7 %copy.9 = bf16[2,64,8192]{2,1,0:T(8,128)(2,1)S(1)} copy(bf16[2,64,8192]{2,0,1:T(2,128)(2,1)} %bitcast.54) | data formatting | bytes 4194304 | tf_op jit(solution)/shard_map/embeds_exchange/transpose | solution.py:234
  10.5 1.8 order.1
  12.3 1.0 copy-done.1
  13.3 4.2 %all-to-all-done = bf16[4,256,512]{2,1,0:T(8,128)(2,1)} async-done(((bf16[4,256,512]{2,1,0:T(8,128)(2,1)}), bf16[4,256,512]{2,1,0:T(8,128)(2,1)}, u32[]{:S(2)}, u32[]{:S(2)}) %all-to-all-start) | async-done | bytes 1048608 | tf_op jit(solution)/shard_map/weight_gather/all_to_all | solution.py:74
  17.5 1.6 broadcast_in_dim.140
  19.2 30.9 %all_to_all.45 = bf16[4,4,256,512]{3,2,1,0:T(8,128)(2,1)} all-to-all(bf16[4,4,256,512]{3,2,1,0:T(8,128)(2,1)S(1)} %broadcast_in_dim.140), channel_id=1, replica_groups={{0,128,256,384},{32,160,288,416},{64,192,320,448},{96,224,352,480},{16,..., dimensions={0} | all-to-all | bytes 8388608 | tf_op jit(solution)/shard_map/weight_gather/all_to_all | solution.py:74
  50.1 9.4 %collective-permute-start = (bf16[128,4096]{1,0:T(8,128)(2,1)S(1)}, bf16[128,4096]{1,0:T(8,128)(2,1)S(1)}, u32[]{:S(2)}, u32[]{:S(2)}) collective-permute-start(bf16[128,4096]{1,0:T(8,128)(2,1)S(1)} %copy-done.2), channel_id=1, source_target_pairs={{0,16},{16,0},{1,17},{17,1},{2,18},{18,2},{3,19},{19,3},{4,20},{20... | collective-permute-start | bytes 3145736 | tf_op jit(solution)/shard_map/weight_gather/ppermute | solution.py:225
  59.6 4.5 %all-to-all-start.2 = ((bf16[32,64,256]{2,1,0:T(8,128)(2,1)}), bf16[32,64,256]{2,1,0:T(8,128)(2,1)}, u32[]{:S(2)}, u32[]{:S(2)}) async-start(bf16[32,64,256]{2,1,0:T(8,128)(2,1)} %get-tuple-element.48), calls=%async_computation.2 | async-start | bytes 2097152 | tf_op jit(solution)/shard_map/weight_gather/all_to_all | solution.py:25
  64.1 2.2 copy-done
  66.3 1.8 project.1
  68.1 2.1 collective-permute-start.1
  70.3 1.3 collective-permute-done.1
  71.6 9.6 %all-to-all-done.2 = bf16[32,64,256]{2,1,0:T(8,128)(2,1)} async-done(((bf16[32,64,256]{2,1,0:T(8,128)(2,1)}), bf16[32,64,256]{2,1,0:T(8,128)(2,1)}, u32[]{:S(2)}, u32[]{:S(2)}) %all-to-all-start.2) | async-done | bytes 1048608 | tf_op jit(solution)/shard_map/weight_gather/all_to_all | solution.py:25
  81.4 1.5 broadcast_in_dim.146
  82.9 3.7 %all-to-all-start.3 = ((bf16[16,136,512]{2,1,0:T(8,128)(2,1)}), bf16[16,136,512]{2,1,0:T(8,128)(2,1)S(1)}, u32[]{:S(2)}, u32[]{:S(2)}) async-start(bf16[16,136,512]{2,1,0:T(8,128)(2,1)} %broadcast_in_dim.146), calls=%async_computation.3 | async-start | bytes 4456448 | tf_op jit(solution)/shard_map/project_gather/all_to_all | solution.py:25
  86.6 2.3 copy.10
  88.9 1.3 slice_bitcast_fusion
  90.2 31.3 %all-to-all-done.3.got_ref = bf16[16,136,512]{2,1,0:T(8,128)(2,1)S(1)} async-done(((bf16[16,136,512]{2,1,0:T(8,128)(2,1)}), bf16[16,136,512]{2,1,0:T(8,128)(2,1)S(1)}, u32[]{:S(2)}, u32[]{:S(2)}) %all-to-all-start.3) | async-done | bytes 2228256 | tf_op jit(solution)/shard_map/project_gather/all_to_all | solution.py:25
  121.6 0.7 multiply_reduce_fusion
  122.3 0.6 fusion
  123.0 0.3 multiply_reduce_fusion.1
  123.3 0.4 fusion.13
  123.8 0.4 convolution_convert_fusion
  124.4 3.1 %collective-permute-start.2 = (bf16[2048,128]{1,0:T(8,128)(2,1)S(1)}, bf16[2048,128]{1,0:T(8,128)(2,1)S(1)}, u32[]{:S(2)}, u32[]{:S(2)}) collective-permute-start(bf16[2048,128]{1,0:T(8,128)(2,1)S(1)} %convolution_convert_fusion), channel_id=1, source_target_pairs={{0,16},{16,0},{1,17},{17,1},{2,18},{18,2},{3,19},{19,3},{4,20},{20... | collective-permute-start | bytes 1572872 | tf_op jit(solution)/shard_map/gram_core/ppermute | solution.py:225
  127.7 1.3 collective-permute-done.2
  129.2 16.8 %all_to_all.46 = bf16[4,520,128]{2,1,0:T(8,128)(2,1)S(1)} all-to-all(bf16[4,520,128]{2,1,0:T(8,128)(2,1)S(1)} %pad_maximum_fusion), channel_id=1, replica_groups=mesh['y'=4,'x'=4,'core'=2,'z1'=4,'z0'=4] {'z0'}, dimensions={0} | all-to-all | bytes 1064960 | tf_op jit(solution)/shard_map/gram_reduce/all_to_all | solution.py:25
  146.2 0.7 pad_maximum_fusion.2
  146.9 10.6 %all-to-all-start.5 = ((bf16[4,136,128]{2,1,0:T(8,128)(2,1)}), bf16[4,136,128]{2,1,0:T(8,128)(2,1)S(1)}, u32[]{:S(2)}, u32[]{:S(2)}) async-start(bf16[4,136,128]{2,1,0:T(8,128)(2,1)} %pad_maximum_fusion.2), calls=%async_computation.5 | async-start | bytes 278528 | tf_op jit(solution)/shard_map/gram_reduce/all_to_all | solution.py:25
  157.5 2.0 collective-permute-start.3
  159.5 11.5 %all-to-all-done.5 = bf16[4,136,128]{2,1,0:T(8,128)(2,1)S(1)} async-done(((bf16[4,136,128]{2,1,0:T(8,128)(2,1)}), bf16[4,136,128]{2,1,0:T(8,128)(2,1)S(1)}, u32[]{:S(2)}, u32[]{:S(2)}) %all-to-all-start.5) | async-done | bytes 139296 | tf_op jit(solution)/shard_map/gram_reduce/all_to_all | solution.py:25
  171.0 4.3 %collective-permute-done.3.other_low = bf16[256,1024]{1,0:T(8,128)(2,1)} collective-permute-done((bf16[256,1024]{1,0:T(8,128)(2,1)S(1)}, bf16[256,1024]{1,0:T(8,128)(2,1)}, u32[]{:S(2)}, u32[]{:S(2)}) %collective-permute-start.3) | collective-permute-done | bytes 524320 | tf_op jit(solution)/shard_map/gram_reduce/ppermute | solution.py:312
  175.3 4.1 %collective-permute-start.4 = (bf16[256,1024]{1,0:T(8,128)(2,1)S(1)}, bf16[256,1024]{1,0:T(8,128)(2,1)S(1)}, u32[]{:S(2)}, u32[]{:S(2)}) collective-permute-start(bf16[256,1024]{1,0:T(8,128)(2,1)S(1)} %get-tuple-element.62.one_high), channel_id=1, source_target_pairs={{0,1},{1,0},{2,3},{3,2},{4,5},{5,4},{6,7},{7,6},{8,9},{9,8},{10,11... | collective-permute-start | bytes 1572872 | tf_op jit(solution)/shard_map/gram_gather/ppermute | solution.py:321
  179.5 23.0 %all_to_all.47 = bf16[4,128,128]{2,1,0:T(8,128)(2,1)S(1)} all-to-all(bf16[4,128,128]{2,1,0:T(8,128)(2,1)S(1)} %broadcast_in_dim.149), channel_id=1, replica_groups=mesh['y'=4,'x'=4,'core'=2,'z1'=4,'z0'=4] {'z1'}, dimensions={0} | all-to-all | bytes 262144 | tf_op jit(solution)/shard_map/gram_gather/all_to_all | solution.py:25
  202.6 15.5 %all_to_all.48 = bf16[4,4,128,128]{3,2,1,0:T(8,128)(2,1)S(1)} all-to-all(bf16[4,4,128,128]{3,2,1,0:T(8,128)(2,1)S(1)} %broadcast_in_dim.150), channel_id=1, replica_groups=mesh['y'=4,'x'=4,'core'=2,'z1'=4,'z0'=4] {'z0'}, dimensions={0} | all-to-all | bytes 1048576 | tf_op jit(solution)/shard_map/gram_gather/all_to_all | solution.py:25
  218.0 5.0 %collective-permute-start.5 = (bf16[2048,128]{1,0:T(8,128)(2,1)S(1)}, bf16[2048,128]{1,0:T(8,128)(2,1)S(1)}, u32[]{:S(2)}, u32[]{:S(2)}) collective-permute-start(bf16[2048,128]{1,0:T(8,128)(2,1)S(1)} %bitcast.51), channel_id=1, source_target_pairs={{0,16},{16,0},{1,17},{17,1},{2,18},{18,2},{3,19},{19,3},{4,20},{20... | collective-permute-start | bytes 1572872 | tf_op jit(solution)/shard_map/gram_gather/ppermute | solution.py:225
  223.0 0.3 fusion.27
  223.4 0.4 convolution_add_fusion
  223.7 0.8 collective-permute-done.5
  224.9 0.3 fusion.4
  225.2 0.4 select_convert_fusion.1
  225.9 32.6 %all_to_all.49.back_ref = bf16[16,136,512]{2,1,0:T(8,128)(2,1)S(1)} all-to-all(bf16[16,136,512]{2,1,0:T(8,128)(2,1)S(1)} %broadcast_in_dim.154), channel_id=1, replica_groups=mesh['y'=4,'x'=4,'core'=2,'z1'=4,'z0'=4] {'y','x'}, dimensions={0} | all-to-all | bytes 4456448 | tf_op jit(solution)/shard_map/back_gather/all_to_all | solution.py:25
  258.5 2.4 grad.1.grad_ref
  260.9 3.4 %collective-permute-start.6 = (bf16[2064,512]{1,0:T(8,128)(2,1)S(1)}, bf16[2064,512]{1,0:T(8,128)(2,1)S(1)}, u32[]{:S(2)}, u32[]{:S(2)}) collective-permute-start(bf16[2064,512]{1,0:T(8,128)(2,1)S(1)} %grad.1.grad_ref), channel_id=1, source_target_pairs={{0,16},{16,0},{1,17},{17,1},{2,18},{18,2},{3,19},{19,3},{4,20},{20... | collective-permute-start | bytes 6340616 | tf_op jit(solution)/shard_map/grad_swap/ppermute | solution.py:225
  264.3 1.8 own_half.1.mine_ref
  266.1 1.9 collective-permute-done.6.grad_ref
  268.1 2.7 other_half.1
  (54 shorter events, 2.0 us)
Async XLA Ops:
  2.7 14.9 %all-to-all-start = ((bf16[4,256,512]{2,1,0:T(8,128)(2,1)}), bf16[4,256,512]{2,1,0:T(8,128)(2,1)}, u32[]{:S(2)}, u32[]{:S(2)}) async-start(bf16[4,256,512]{2,1,0:T(8,128)(2,1)} %broadcast_in_dim.139), calls=%async_computation | async-start | bytes 2097152 | tf_op jit(solution)/shard_map/weight_gather/all_to_all | solution.py:74
  12.3 1.0 copy-start.1
  19.2 31.0 %copy-start.2 = (bf16[128,4096]{1,0:T(8,128)(2,1)S(1)}, bf16[128,4096]{1,0:T(8,128)(2,1)}, u32[]{:S(2)}) copy-start(bf16[128,4096]{1,0:T(8,128)(2,1)} %copy-done.1) | copy-start | bytes 3145732
  50.1 13.9 %collective-permute-start = (bf16[128,4096]{1,0:T(8,128)(2,1)S(1)}, bf16[128,4096]{1,0:T(8,128)(2,1)S(1)}, u32[]{:S(2)}, u32[]{:S(2)}) collective-permute-start(bf16[128,4096]{1,0:T(8,128)(2,1)S(1)} %copy-done.2), channel_id=1, source_target_pairs={{0,16},{16,0},{1,17},{17,1},{2,18},{18,2},{3,19},{19,3},{4,20},{20... | collective-permute-start | bytes 3145736 | tf_op jit(solution)/shard_map/weight_gather/ppermute | solution.py:225
  59.6 21.6 %all-to-all-start.2 = ((bf16[32,64,256]{2,1,0:T(8,128)(2,1)}), bf16[32,64,256]{2,1,0:T(8,128)(2,1)}, u32[]{:S(2)}, u32[]{:S(2)}) async-start(bf16[32,64,256]{2,1,0:T(8,128)(2,1)} %get-tuple-element.48), calls=%async_computation.2 | async-start | bytes 2097152 | tf_op jit(solution)/shard_map/weight_gather/all_to_all | solution.py:25
  64.1 2.2 copy-start
  68.1 3.4 %collective-permute-start.1 = (f32[128,512]{1,0:T(8,128)S(1)}, f32[128,512]{1,0:T(8,128)S(1)}, u32[]{:S(2)}, u32[]{:S(2)}) collective-permute-start(f32[128,512]{1,0:T(8,128)S(1)} %get-tuple-element.47), channel_id=1, source_target_pairs={{0,16},{16,0},{1,17},{17,1},{2,18},{18,2},{3,19},{19,3},{4,20},{20... | collective-permute-start | bytes 786440 | tf_op jit(solution)/shard_map/project/ppermute | solution.py:225
  82.9 38.6 %all-to-all-start.3 = ((bf16[16,136,512]{2,1,0:T(8,128)(2,1)}), bf16[16,136,512]{2,1,0:T(8,128)(2,1)S(1)}, u32[]{:S(2)}, u32[]{:S(2)}) async-start(bf16[16,136,512]{2,1,0:T(8,128)(2,1)} %broadcast_in_dim.146), calls=%async_computation.3 | async-start | bytes 4456448 | tf_op jit(solution)/shard_map/project_gather/all_to_all | solution.py:25
  123.0 1.2 copy-start.3
  123.0 1.3 copy-start.5
  124.4 4.7 %collective-permute-start.2 = (bf16[2048,128]{1,0:T(8,128)(2,1)S(1)}, bf16[2048,128]{1,0:T(8,128)(2,1)S(1)}, u32[]{:S(2)}, u32[]{:S(2)}) collective-permute-start(bf16[2048,128]{1,0:T(8,128)(2,1)S(1)} %convolution_convert_fusion), channel_id=1, source_target_pairs={{0,16},{16,0},{1,17},{17,1},{2,18},{18,2},{3,19},{19,3},{4,20},{20... | collective-permute-start | bytes 1572872 | tf_op jit(solution)/shard_map/gram_core/ppermute | solution.py:225
  146.9 24.1 %all-to-all-start.5 = ((bf16[4,136,128]{2,1,0:T(8,128)(2,1)}), bf16[4,136,128]{2,1,0:T(8,128)(2,1)S(1)}, u32[]{:S(2)}, u32[]{:S(2)}) async-start(bf16[4,136,128]{2,1,0:T(8,128)(2,1)} %pad_maximum_fusion.2), calls=%async_computation.5 | async-start | bytes 278528 | tf_op jit(solution)/shard_map/gram_reduce/all_to_all | solution.py:25
  157.5 17.8 %collective-permute-start.3 = (bf16[256,1024]{1,0:T(8,128)(2,1)S(1)}, bf16[256,1024]{1,0:T(8,128)(2,1)}, u32[]{:S(2)}, u32[]{:S(2)}) collective-permute-start(bf16[256,1024]{1,0:T(8,128)(2,1)S(1)} %get-tuple-element.58.one_low), channel_id=1, source_target_pairs={{0,1},{1,0},{2,3},{3,2},{4,5},{5,4},{6,7},{7,6},{8,9},{9,8},{10,11... | collective-permute-start | bytes 1572872 | tf_op jit(solution)/shard_map/gram_reduce/ppermute | solution.py:312
  171.0 52.0 %copy-start.6 = (bf16[2048,256]{1,0:T(8,128)(2,1)S(1)}, bf16[2048,256]{1,0:T(8,128)(2,1)}, u32[]{:S(2)}) copy-start(bf16[2048,256]{1,0:T(8,128)(2,1)} %copy-done.5) | copy-start | bytes 3145732
  175.3 27.1 %collective-permute-start.4 = (bf16[256,1024]{1,0:T(8,128)(2,1)S(1)}, bf16[256,1024]{1,0:T(8,128)(2,1)S(1)}, u32[]{:S(2)}, u32[]{:S(2)}) collective-permute-start(bf16[256,1024]{1,0:T(8,128)(2,1)S(1)} %get-tuple-element.62.one_high), channel_id=1, source_target_pairs={{0,1},{1,0},{2,3},{3,2},{4,5},{5,4},{6,7},{7,6},{8,9},{9,8},{10,11... | collective-permute-start | bytes 1572872 | tf_op jit(solution)/shard_map/gram_gather/ppermute | solution.py:321
  218.0 6.8 %copy-start.4 = (bf16[2048,256]{1,0:T(8,128)(2,1)S(1)}, bf16[2048,256]{1,0:T(8,128)(2,1)}, u32[]{:S(2)}) copy-start(bf16[2048,256]{1,0:T(8,128)(2,1)} %copy-done.3) | copy-start | bytes 3145732
  218.0 6.5 %collective-permute-start.5 = (bf16[2048,128]{1,0:T(8,128)(2,1)S(1)}, bf16[2048,128]{1,0:T(8,128)(2,1)S(1)}, u32[]{:S(2)}, u32[]{:S(2)}) collective-permute-start(bf16[2048,128]{1,0:T(8,128)(2,1)S(1)} %bitcast.51), channel_id=1, source_target_pairs={{0,16},{16,0},{1,17},{17,1},{2,18},{18,2},{3,19},{19,3},{4,20},{20... | collective-permute-start | bytes 1572872 | tf_op jit(solution)/shard_map/gram_gather/ppermute | solution.py:225
  260.9 7.2 %collective-permute-start.6 = (bf16[2064,512]{1,0:T(8,128)(2,1)S(1)}, bf16[2064,512]{1,0:T(8,128)(2,1)S(1)}, u32[]{:S(2)}, u32[]{:S(2)}) collective-permute-start(bf16[2064,512]{1,0:T(8,128)(2,1)S(1)} %grad.1.grad_ref), channel_id=1, source_target_pairs={{0,16},{16,0},{1,17},{17,1},{2,18},{18,2},{3,19},{19,3},{4,20},{20... | collective-permute-start | bytes 6340616 | tf_op jit(solution)/shard_map/grad_swap/ppermute | solution.py:225

commit v13 on v11

--- a/solution.py
+++ b/solution.py
@@ -290,12 +290,11 @@
         kept = partial(jnp.where(first, view_a, view_b))
         weight_diag = 2.0 * ((1.0 - off_weight) * diagonal - 1.0)
         factor = loss_scale / n_rows * jnp.concatenate([weight_diag, weight_diag])
-        sent, kept, diag_local, factor, inverse, one_t, other_t = lax.optimization_barrier(
-            (sent, kept, diag_local, factor, inverse, one_t, other_t)
-        )
+        sent, one_t, other_t = lax.optimization_barrier((sent, one_t, other_t))
     with jax.named_scope("gram_core"):
         extra = pad_rows(pieces(diag_local), chip_rows)
         parts = kept + swap_core(sent).astype(F32)
+        parts, extra, factor, inverse = lax.optimization_barrier((parts.astype(BF16), extra, factor, inverse))
     with jax.named_scope("gram_reduce"):
         parts = parts.astype(BF16).reshape(n_near, n_rows // n_near, chip_rows)
         extra = jnp.broadcast_to(extra[None], (n_near, PAD, chip_rows))

time: 255 us -> 254 us (level)
  no operation moved by 1% of the time
where the time goes in v13:
time: 254 us; the launch traced here: 253 us
  blocking collectives  131 us (52%)
  waiting for transfers between devices  49.9 us (20%)
  starting transfers between devices  41.7 us (16%)
  local copies, waits for them, and re-layouts  13 us (5%)
  Pallas kernels  10.9 us (4%)
  other arithmetic  3.13 us (1%)
    all_to_all x5, blocking collectives, exchange(): return lax.all_to_all(blocks, axes, split_axis=0, concat_axis=0, tiled=True)  100 us
    all_to_all x2, waiting for transfers between devices, exchange(): return lax.all_to_all(blocks, axes, split_axis=0, concat_axis=0, tiled=True)  40.9 us
    all_to_all x1, blocking collectives, ring_gather(): lax.all_to_all(blocks, BATCH, split_axis=0, concat_axis=0, tiled=True, ax...  31 us
    ppermute x5, starting transfers between devices, swap_core(): return lax.ppermute(a, 'core', [(0, 1), (1, 0)])  26.6 us
    all_to_all x2, starting transfers between devices, exchange(): return lax.all_to_all(blocks, axes, split_axis=0, concat_axis=0, tiled=True)  8.19 us
  transfers between devices with their start and end apart: 9, of which 7 were waited for; matrix products, arithmetic and copies ran while one was open for 3% of the time, Pallas kernels for 2%

profile of v13, /device:TPU:1, one launch (start us, length us, event | category | flops | bytes accessed | tf_op | source)
XLA Modules:
  0.0 253.3 jit_solution(3121206512325254165)
XLA Ops:
  0.6 2.1 broadcast_in_dim.139
  2.7 5.0 %all-to-all-start = ((bf16[4,256,512]{2,1,0:T(8,128)(2,1)}), bf16[4,256,512]{2,1,0:T(8,128)(2,1)}, u32[]{:S(2)}, u32[]{:S(2)}) async-start(bf16[4,256,512]{2,1,0:T(8,128)(2,1)} %broadcast_in_dim.139), calls=%async_computation | async-start | bytes 2097152 | tf_op jit(solution)/shard_map/weight_gather/all_to_all | solution.py:74
  7.7 2.7 %copy.8 = bf16[2,64,8192]{2,1,0:T(8,128)(2,1)S(1)} copy(bf16[2,64,8192]{2,0,1:T(2,128)(2,1)} %bitcast.54) | data formatting | bytes 4194304 | tf_op jit(solution)/shard_map/embeds_exchange/transpose | solution.py:229
  10.5 1.8 order.1
  12.4 1.0 copy-done.1
  13.4 4.2 %all-to-all-done = bf16[4,256,512]{2,1,0:T(8,128)(2,1)} async-done(((bf16[4,256,512]{2,1,0:T(8,128)(2,1)}), bf16[4,256,512]{2,1,0:T(8,128)(2,1)}, u32[]{:S(2)}, u32[]{:S(2)}) %all-to-all-start) | async-done | bytes 1048608 | tf_op jit(solution)/shard_map/weight_gather/all_to_all | solution.py:74
  17.6 1.6 broadcast_in_dim.140
  19.2 31.0 %all_to_all.45 = bf16[4,4,256,512]{3,2,1,0:T(8,128)(2,1)} all-to-all(bf16[4,4,256,512]{3,2,1,0:T(8,128)(2,1)S(1)} %broadcast_in_dim.140), channel_id=1, replica_groups={{0,128,256,384},{32,160,288,416},{64,192,320,448},{96,224,352,480},{16,..., dimensions={0} | all-to-all | bytes 8388608 | tf_op jit(solution)/shard_map/weight_gather/all_to_all | solution.py:74
  50.2 9.5 %collective-permute-start = (bf16[128,4096]{1,0:T(8,128)(2,1)S(1)}, bf16[128,4096]{1,0:T(8,128)(2,1)S(1)}, u32[]{:S(2)}, u32[]{:S(2)}) collective-permute-start(bf16[128,4096]{1,0:T(8,128)(2,1)S(1)} %copy-done.2), channel_id=1, source_target_pairs={{0,16},{16,0},{1,17},{17,1},{2,18},{18,2},{3,19},{19,3},{4,20},{20... | collective-permute-start | bytes 3145736 | tf_op jit(solution)/shard_map/weight_gather/ppermute | solution.py:220
  59.6 4.5 %all-to-all-start.2 = ((bf16[32,64,256]{2,1,0:T(8,128)(2,1)}), bf16[32,64,256]{2,1,0:T(8,128)(2,1)}, u32[]{:S(2)}, u32[]{:S(2)}) async-start(bf16[32,64,256]{2,1,0:T(8,128)(2,1)} %get-tuple-element.41), calls=%async_computation.2 | async-start | bytes 2097152 | tf_op jit(solution)/shard_map/weight_gather/all_to_all | solution.py:25
  64.1 2.2 copy-done
  66.3 1.8 project.1
  68.1 2.1 collective-permute-start.1
  70.3 1.3 collective-permute-done.1
  71.6 9.6 %all-to-all-done.2 = bf16[32,64,256]{2,1,0:T(8,128)(2,1)} async-done(((bf16[32,64,256]{2,1,0:T(8,128)(2,1)}), bf16[32,64,256]{2,1,0:T(8,128)(2,1)}, u32[]{:S(2)}, u32[]{:S(2)}) %all-to-all-start.2) | async-done | bytes 1048608 | tf_op jit(solution)/shard_map/weight_gather/all_to_all | solution.py:25
  81.3 0.1 select_select_fusion
  81.4 1.5 broadcast_in_dim.146
  82.9 3.7 %all-to-all-start.3 = ((bf16[16,136,512]{2,1,0:T(8,128)(2,1)}), bf16[16,136,512]{2,1,0:T(8,128)(2,1)S(1)}, u32[]{:S(2)}, u32[]{:S(2)}) async-start(bf16[16,136,512]{2,1,0:T(8,128)(2,1)} %broadcast_in_dim.146), calls=%async_computation.3 | async-start | bytes 4456448 | tf_op jit(solution)/shard_map/project_gather/all_to_all | solution.py:25
  86.7 1.5 copy.9
  88.2 1.9 collective-permute-start.2
  90.2 31.3 %all-to-all-done.3.got_ref = bf16[16,136,512]{2,1,0:T(8,128)(2,1)S(1)} async-done(((bf16[16,136,512]{2,1,0:T(8,128)(2,1)}), bf16[16,136,512]{2,1,0:T(8,128)(2,1)S(1)}, u32[]{:S(2)}, u32[]{:S(2)}) %all-to-all-start.3) | async-done | bytes 2228256 | tf_op jit(solution)/shard_map/project_gather/all_to_all | solution.py:25
  121.6 0.7 multiply_reduce_fusion
  122.3 0.6 fusion
  122.9 0.3 multiply_reduce_fusion.1
  123.2 0.1 broadcast_select_fusion
  123.4 0.4 convolution_convert_fusion
  123.8 3.1 %collective-permute-start.3 = (bf16[2048,128]{1,0:T(8,128)(2,1)S(1)}, bf16[2048,128]{1,0:T(8,128)(2,1)S(1)}, u32[]{:S(2)}, u32[]{:S(2)}) collective-permute-start(bf16[2048,128]{1,0:T(8,128)(2,1)S(1)} %convolution_convert_fusion), channel_id=1, source_target_pairs={{0,16},{16,0},{1,17},{17,1},{2,18},{18,2},{3,19},{19,3},{4,20},{20... | collective-permute-start | bytes 1572872 | tf_op jit(solution)/shard_map/gram_core/ppermute | solution.py:220
  127.1 0.4 fusion.13
  127.5 1.0 collective-permute-done.3
  128.7 16.8 %all_to_all.46 = bf16[4,520,128]{2,1,0:T(8,128)(2,1)S(1)} all-to-all(bf16[4,520,128]{2,1,0:T(8,128)(2,1)S(1)} %pad_maximum_fusion), channel_id=1, replica_groups=mesh['y'=4,'x'=4,'core'=2,'z1'=4,'z0'=4] {'z0'}, dimensions={0} | all-to-all | bytes 1064960 | tf_op jit(solution)/shard_map/gram_reduce/all_to_all | solution.py:25
  145.7 23.8 %all_to_all.47 = bf16[4,136,128]{2,1,0:T(8,128)(2,1)S(1)} all-to-all(bf16[4,136,128]{2,1,0:T(8,128)(2,1)S(1)} %pad_maximum_fusion.2), channel_id=1, replica_groups=mesh['y'=4,'x'=4,'core'=2,'z1'=4,'z0'=4] {'z1'}, dimensions={0} | all-to-all | bytes 278528 | tf_op jit(solution)/shard_map/gram_reduce/all_to_all | solution.py:25
  169.6 15.4 %all_to_all.48 = bf16[4,128,128]{2,1,0:T(8,128)(2,1)S(1)} all-to-all(bf16[4,128,128]{2,1,0:T(8,128)(2,1)S(1)} %broadcast_in_dim.149), channel_id=1, replica_groups=mesh['y'=4,'x'=4,'core'=2,'z1'=4,'z0'=4] {'z1'}, dimensions={0} | all-to-all | bytes 262144 | tf_op jit(solution)/shard_map/gram_gather/all_to_all | solution.py:25
  185.1 11.8 %all_to_all.49 = bf16[4,4,128,128]{3,2,1,0:T(8,128)(2,1)S(1)} all-to-all(bf16[4,4,128,128]{3,2,1,0:T(8,128)(2,1)S(1)} %broadcast_in_dim.150), channel_id=1, replica_groups=mesh['y'=4,'x'=4,'core'=2,'z1'=4,'z0'=4] {'z0'}, dimensions={0} | all-to-all | bytes 1048576 | tf_op jit(solution)/shard_map/gram_gather/all_to_all | solution.py:25
  196.9 8.5 %collective-permute-start.4 = (bf16[2048,128]{1,0:T(8,128)(2,1)S(1)}, bf16[2048,128]{1,0:T(8,128)(2,1)S(1)}, u32[]{:S(2)}, u32[]{:S(2)}) collective-permute-start(bf16[2048,128]{1,0:T(8,128)(2,1)S(1)} %bitcast.51), channel_id=1, source_target_pairs={{0,16},{16,0},{1,17},{17,1},{2,18},{18,2},{3,19},{19,3},{4,20},{20... | collective-permute-start | bytes 1572872 | tf_op jit(solution)/shard_map/gram_gather/ppermute | solution.py:220
  205.4 0.3 fusion.27
  205.8 0.4 convolution_add_fusion
  206.1 0.8 collective-permute-done.4
  206.9 0.3 fusion.2
  207.3 0.3 fusion.4
  207.6 0.4 select_convert_fusion.1
  208.0 0.1 fusion.12
  208.1 0.1 broadcast_in_dim.154
  208.3 32.6 %all_to_all.50.back_ref = bf16[16,136,512]{2,1,0:T(8,128)(2,1)S(1)} all-to-all(bf16[16,136,512]{2,1,0:T(8,128)(2,1)S(1)} %broadcast_in_dim.154), channel_id=1, replica_groups=mesh['y'=4,'x'=4,'core'=2,'z1'=4,'z0'=4] {'y','x'}, dimensions={0} | all-to-all | bytes 4456448 | tf_op jit(solution)/shard_map/back_gather/all_to_all | solution.py:25
  240.9 2.4 grad.1.grad_ref
  243.3 3.4 %collective-permute-start.5 = (bf16[2064,512]{1,0:T(8,128)(2,1)S(1)}, bf16[2064,512]{1,0:T(8,128)(2,1)S(1)}, u32[]{:S(2)}, u32[]{:S(2)}) collective-permute-start(bf16[2064,512]{1,0:T(8,128)(2,1)S(1)} %grad.1.grad_ref), channel_id=1, source_target_pairs={{0,16},{16,0},{1,17},{17,1},{2,18},{18,2},{3,19},{19,3},{4,20},{20... | collective-permute-start | bytes 6340616 | tf_op jit(solution)/shard_map/grad_swap/ppermute | solution.py:220
  246.7 2.0 own_half.1.mine_ref
  248.7 1.8 collective-permute-done.5.grad_ref
  250.5 2.9 %other_half.1 = (f32[256,512]{1,0:T(8,128)}, f32[1]{0:T(128)}) custom-call(s32[2]{0:T(128)S(1)} %pad_add_fusion.place_ref, bf16[256,2048]{1,0:T(8,128)(2,1)S(1)} %bitcast.44, bf16[256,2048]{1,0:T(8,128)(2,1)} %collective-permute-done.2.other_ref, bf16[2064,512]{1,0:T(8,128)(2,1)S(1)} %collective-permute-done.5.grad_ref, f32[256,256]{1,0:T(8,128)S(1)} %own_half.1.mine_ref, ...), custom_call_target="tpu_custom_call" | custom-call | tf_op jit(solution)/shard_map/weight_grad/other_half/pallas_call | solution.py:348
  (42 shorter events, 1.1 us)
Async XLA Ops:
  2.7 14.9 %all-to-all-start = ((bf16[4,256,512]{2,1,0:T(8,128)(2,1)}), bf16[4,256,512]{2,1,0:T(8,128)(2,1)}, u32[]{:S(2)}, u32[]{:S(2)}) async-start(bf16[4,256,512]{2,1,0:T(8,128)(2,1)} %broadcast_in_dim.139), calls=%async_computation | async-start | bytes 2097152 | tf_op jit(solution)/shard_map/weight_gather/all_to_all | solution.py:74
  12.4 1.0 copy-start.1
  19.2 31.0 %copy-start.2 = (bf16[128,4096]{1,0:T(8,128)(2,1)S(1)}, bf16[128,4096]{1,0:T(8,128)(2,1)}, u32[]{:S(2)}) copy-start(bf16[128,4096]{1,0:T(8,128)(2,1)} %copy-done.1) | copy-start | bytes 3145732
  50.2 13.9 %collective-permute-start = (bf16[128,4096]{1,0:T(8,128)(2,1)S(1)}, bf16[128,4096]{1,0:T(8,128)(2,1)S(1)}, u32[]{:S(2)}, u32[]{:S(2)}) collective-permute-start(bf16[128,4096]{1,0:T(8,128)(2,1)S(1)} %copy-done.2), channel_id=1, source_target_pairs={{0,16},{16,0},{1,17},{17,1},{2,18},{18,2},{3,19},{19,3},{4,20},{20... | collective-permute-start | bytes 3145736 | tf_op jit(solution)/shard_map/weight_gather/ppermute | solution.py:220
  59.6 21.6 %all-to-all-start.2 = ((bf16[32,64,256]{2,1,0:T(8,128)(2,1)}), bf16[32,64,256]{2,1,0:T(8,128)(2,1)}, u32[]{:S(2)}, u32[]{:S(2)}) async-start(bf16[32,64,256]{2,1,0:T(8,128)(2,1)} %get-tuple-element.41), calls=%async_computation.2 | async-start | bytes 2097152 | tf_op jit(solution)/shard_map/weight_gather/all_to_all | solution.py:25
  64.1 2.2 copy-start
  68.1 3.4 %collective-permute-start.1 = (f32[128,512]{1,0:T(8,128)S(1)}, f32[128,512]{1,0:T(8,128)S(1)}, u32[]{:S(2)}, u32[]{:S(2)}) collective-permute-start(f32[128,512]{1,0:T(8,128)S(1)} %get-tuple-element.40), channel_id=1, source_target_pairs={{0,16},{16,0},{1,17},{17,1},{2,18},{18,2},{3,19},{19,3},{4,20},{20... | collective-permute-start | bytes 786440 | tf_op jit(solution)/shard_map/project/ppermute | solution.py:220
  82.9 38.6 %all-to-all-start.3 = ((bf16[16,136,512]{2,1,0:T(8,128)(2,1)}), bf16[16,136,512]{2,1,0:T(8,128)(2,1)S(1)}, u32[]{:S(2)}, u32[]{:S(2)}) async-start(bf16[16,136,512]{2,1,0:T(8,128)(2,1)} %broadcast_in_dim.146), calls=%async_computation.3 | async-start | bytes 4456448 | tf_op jit(solution)/shard_map/project_gather/all_to_all | solution.py:25
  88.2 35.6 %collective-permute-start.2 = (bf16[256,2048]{1,0:T(8,128)(2,1)S(1)}, bf16[256,2048]{1,0:T(8,128)(2,1)}, u32[]{:S(2)}, u32[]{:S(2)}) collective-permute-start(bf16[256,2048]{1,0:T(8,128)(2,1)S(1)} %bitcast.42), channel_id=1, source_target_pairs={{0,1},{1,0},{2,3},{3,2},{4,5},{5,4},{6,7},{7,6},{8,9},{9,8},{10,11... | collective-permute-start | bytes 3145736 | tf_op jit(solution)/shard_map/project_gather/ppermute | solution.py:266
  123.8 4.7 %collective-permute-start.3 = (bf16[2048,128]{1,0:T(8,128)(2,1)S(1)}, bf16[2048,128]{1,0:T(8,128)(2,1)S(1)}, u32[]{:S(2)}, u32[]{:S(2)}) collective-permute-start(bf16[2048,128]{1,0:T(8,128)(2,1)S(1)} %convolution_convert_fusion), channel_id=1, source_target_pairs={{0,16},{16,0},{1,17},{17,1},{2,18},{18,2},{3,19},{19,3},{4,20},{20... | collective-permute-start | bytes 1572872 | tf_op jit(solution)/shard_map/gram_core/ppermute | solution.py:220
  196.9 10.0 %collective-permute-start.4 = (bf16[2048,128]{1,0:T(8,128)(2,1)S(1)}, bf16[2048,128]{1,0:T(8,128)(2,1)S(1)}, u32[]{:S(2)}, u32[]{:S(2)}) collective-permute-start(bf16[2048,128]{1,0:T(8,128)(2,1)S(1)} %bitcast.51), channel_id=1, source_target_pairs={{0,16},{16,0},{1,17},{17,1},{2,18},{18,2},{3,19},{19,3},{4,20},{20... | collective-permute-start | bytes 1572872 | tf_op jit(solution)/shard_map/gram_gather/ppermute | solution.py:220
  243.3 7.2 %collective-permute-start.5 = (bf16[2064,512]{1,0:T(8,128)(2,1)S(1)}, bf16[2064,512]{1,0:T(8,128)(2,1)S(1)}, u32[]{:S(2)}, u32[]{:S(2)}) collective-permute-start(bf16[2064,512]{1,0:T(8,128)(2,1)S(1)} %grad.1.grad_ref), channel_id=1, source_target_pairs={{0,16},{16,0},{1,17},{17,1},{2,18},{18,2},{3,19},{19,3},{4,20},{20... | collective-permute-start | bytes 6340616 | tf_op jit(solution)/shard_map/grad_swap/ppermute | solution.py:220

commit v14 on v13

--- a/solution.py
+++ b/solution.py
@@ -117,17 +117,12 @@
     n, width = rows_ref.shape
     depth = width // 32
 
-    def blocks(view):
-        for j in range(32):
-            view_ref[j] = rows_ref[view * n // 2 : (view + 1) * n // 2, j * depth : (j + 1) * depth]
-
-    @pl.when(place_ref[1] == 0)
-    def _():
-        blocks(0)
-
-    @pl.when(place_ref[1] != 0)
-    def _():
-        blocks(1)
+    for q in range(4):
+
+        @pl.when(place_ref[2] == q)
+        def _(q=q):
+            for j in range(32):
+                view_ref[j] = rows_ref[q * n // 4 : (q + 1) * n // 4, j * depth : (j + 1) * depth]
 
     def pick(core, out_ref):
         for j in range(16):
@@ -219,8 +214,9 @@
     def swap_core(a):
         return lax.ppermute(a, "core", [(0, 1), (1, 0)])
 
-    odd = lax.axis_index("z0") % 2
-    place = jnp.stack([core, odd]).astype(jnp.int32)
+    near = lax.axis_index("z0")
+    odd = near // 2
+    place = jnp.stack([core, odd, near]).astype(jnp.int32)
     vmem = pl.BlockSpec(memory_space=pltpu.VMEM)
     smem = pl.BlockSpec(memory_space=pltpu.SMEM)
     params = pltpu.CompilerParams(vmem_limit_bytes=32 * 1024 * 1024)
@@ -231,7 +227,7 @@
         own_rows, sent_rows, one_view = pl.pallas_call(
             order_kernel,
             out_shape=[jax.ShapeDtypeStruct((2 * local_rows, n_chip * depth), BF16)] * 2
-            + [jax.ShapeDtypeStruct((n_batch, local_rows, depth), BF16)],
+            + [jax.ShapeDtypeStruct((n_batch, local_rows // 2, depth), BF16)],
             in_specs=[smem, vmem],
             out_specs=[vmem] * 3,
             compiler_params=params,
@@ -243,7 +239,7 @@
         row_weight, one_view, own_rows, sent_rows = lax.optimization_barrier((row_weight, one_view, own_rows, sent_rows))
         core_weight = ring_gather(row_weight, second_groups).reshape(n_chip * depth, width_out)
         core_weight, one_view, sent_rows = lax.optimization_barrier((core_weight, one_view, sent_rows))
-        one_view = exchange(one_view, BATCH).reshape(n_rows, depth)
+        one_view = exchange(one_view, BATCH)
         other_rows = swap_core(sent_rows)
     with jax.named_scope("project"):
         kept, sent = pl.pallas_call(
@@ -262,8 +258,12 @@
         projected, chip_mean, one_view = lax.optimization_barrier((projected, chip_mean, one_view))
         block = with_rows((projected - chip_mean).astype(BF16), pieces(chip_mean))
         block, one_view = lax.optimization_barrier((block, one_view))
-        one_t = one_view.T
-        other_t = lax.ppermute(one_t, "z0", [(0, 1), (1, 0), (2, 3), (3, 2)])
+        half_got = lax.ppermute(one_view, "z0", [(0, 1), (1, 0), (2, 3), (3, 2)])
+        even = near % 2 == 0
+        low, high = jnp.where(even, one_view, half_got), jnp.where(even, half_got, one_view)
+        one_t = jnp.concatenate([low, high], axis=1).reshape(n_rows, depth).T
+        pairs = [(z, (z + 1) % n_feat) for z in range(1, n_feat, 2)]
+        other_t = lax.ppermute(one_t, FEAT, pairs + [(b, a) for a, b in pairs])
         got = gather(block, PLANE)
     with jax.named_scope("standardize"):
         chip_means = jnp.sum(got[:, chip_rows : chip_rows + 3].astype(F32), axis=1)

time: 254 us -> 266 us (1.047)
  starting transfers between devices: 41.7 us -> 48.6 us
  waiting for transfers between devices: 49.9 us -> 54.7 us
    ppermute x1 -> x2, waiting for transfers between devices: 0.01 us -> 24.6 us  [the longest x1 13 us: body(): half_got = lax.ppermute(one_view, 'z0', [(0, 1), (1, 0), (2, 3), (3, 2)])]
    all_to_all x2, waiting for transfers between devices: 40.9 us -> 19.9 us  [exchange(): return lax.all_to_all(blocks, axes, split_axis=0, concat_axis=0, tiled=True)]
    ppermute x1 -> x2, starting transfers between devices: 1.92 us -> 9.48 us  [the longest x1 7.55 us: body(): other_t = lax.ppermute(one_t, FEAT, pairs + [(b, a) for a, b in pairs])]
  transfers between devices with their start and end apart: 9 -> 10, of which waited for: 7 -> 9; matrix products, arithmetic and copies ran while one was open for 3% -> 4% of each run, Pallas kernels for 2% -> 1%
where the time goes in v14:
time: 266 us; the launch traced here: 265 us
  blocking collectives  132 us (50%)
  waiting for transfers between devices  54.7 us (21%)
  starting transfers between devices  48.6 us (18%)
  local copies, waits for them, and re-layouts  10.8 us (4%)
  Pallas kernels  10.7 us (4%)
  other arithmetic  5.33 us (2%)
    all_to_all x5, blocking collectives, exchange(): return lax.all_to_all(blocks, axes, split_axis=0, concat_axis=0, tiled=True)  101 us
    all_to_all x1, blocking collectives, ring_gather(): lax.all_to_all(blocks, BATCH, split_axis=0, concat_axis=0, tiled=True, ax...  30.8 us
    ppermute x5, starting transfers between devices, swap_core(): return lax.ppermute(a, 'core', [(0, 1), (1, 0)])  26.7 us
    all_to_all x2, waiting for transfers between devices, exchange(): return lax.all_to_all(blocks, axes, split_axis=0, concat_axis=0, tiled=True)  19.9 us
    ppermute x1, waiting for transfers between devices, body(): half_got = lax.ppermute(one_view, 'z0', [(0, 1), (1, 0), (2, 3), (3, 2)])  13 us
    ppermute x1, waiting for transfers between devices, body(): other_t = lax.ppermute(one_t, FEAT, pairs + [(b, a) for a, b in pairs])  11.6 us
    ppermute x1, starting transfers between devices, body(): other_t = lax.ppermute(one_t, FEAT, pairs + [(b, a) for a, b in pairs])  7.55 us
    all_to_all x2, starting transfers between devices, exchange(): return lax.all_to_all(blocks, axes, split_axis=0, concat_axis=0, tiled=True)  7.42 us
  transfers between devices with their start and end apart: 10, of which 9 were waited for; matrix products, arithmetic and copies ran while one was open for 4% of the time, Pallas kernels for 1%

profile of v14, /device:TPU:1, one launch (start us, length us, event | category | flops | bytes accessed | tf_op | source)
XLA Modules:
  0.0 265.2 jit_solution(13178570243170326344)
XLA Ops:
  0.6 2.1 broadcast_in_dim.139
  2.7 5.0 %all-to-all-start = ((bf16[4,256,512]{2,1,0:T(8,128)(2,1)}), bf16[4,256,512]{2,1,0:T(8,128)(2,1)}, u32[]{:S(2)}, u32[]{:S(2)}) async-start(bf16[4,256,512]{2,1,0:T(8,128)(2,1)} %broadcast_in_dim.139), calls=%async_computation | async-start | bytes 2097152 | tf_op jit(solution)/shard_map/weight_gather/all_to_all | solution.py:74
  7.7 2.7 %copy.8 = bf16[2,64,8192]{2,1,0:T(8,128)(2,1)S(1)} copy(bf16[2,64,8192]{2,0,1:T(2,128)(2,1)} %bitcast.56) | data formatting | bytes 4194304 | tf_op jit(solution)/shard_map/embeds_exchange/transpose | solution.py:225
  10.6 1.6 order.1
  12.2 1.0 copy-done
  13.2 4.4 %all-to-all-done = bf16[4,256,512]{2,1,0:T(8,128)(2,1)} async-done(((bf16[4,256,512]{2,1,0:T(8,128)(2,1)}), bf16[4,256,512]{2,1,0:T(8,128)(2,1)}, u32[]{:S(2)}, u32[]{:S(2)}) %all-to-all-start) | async-done | bytes 1048608 | tf_op jit(solution)/shard_map/weight_gather/all_to_all | solution.py:74
  17.6 1.6 broadcast_in_dim.140
  19.2 30.8 %all_to_all.45 = bf16[4,4,256,512]{3,2,1,0:T(8,128)(2,1)S(1)} all-to-all(bf16[4,4,256,512]{3,2,1,0:T(8,128)(2,1)S(1)} %broadcast_in_dim.140), channel_id=1, replica_groups={{0,128,256,384},{32,160,288,416},{64,192,320,448},{96,224,352,480},{16,..., dimensions={0} | all-to-all | bytes 8388608 | tf_op jit(solution)/shard_map/weight_gather/all_to_all | solution.py:74
  50.1 8.7 %collective-permute-start = (bf16[128,4096]{1,0:T(8,128)(2,1)S(1)}, bf16[128,4096]{1,0:T(8,128)(2,1)S(1)}, u32[]{:S(2)}, u32[]{:S(2)}) collective-permute-start(bf16[128,4096]{1,0:T(8,128)(2,1)S(1)} %copy-done.1), channel_id=1, source_target_pairs={{0,16},{16,0},{1,17},{17,1},{2,18},{18,2},{3,19},{19,3},{4,20},{20... | collective-permute-start | bytes 3145736 | tf_op jit(solution)/shard_map/weight_gather/ppermute | solution.py:215
  58.8 2.3 collective-permute-done.other_ref
  61.0 1.8 project.1
  62.8 2.3 collective-permute-start.1
  65.2 3.7 %all-to-all-start.2 = ((bf16[32,32,256]{2,1,0:T(8,128)(2,1)}), bf16[32,32,256]{2,1,0:T(8,128)(2,1)S(1)}, u32[]{:S(2)}, u32[]{:S(2)}) async-start(bf16[32,32,256]{2,1,0:T(8,128)(2,1)} %get-tuple-element.41), calls=%async_computation.2 | async-start | bytes 1048576 | tf_op jit(solution)/shard_map/weight_gather/all_to_all | solution.py:25
  69.0 11.5 %all-to-all-done.2 = bf16[32,32,256]{2,1,0:T(8,128)(2,1)S(1)} async-done(((bf16[32,32,256]{2,1,0:T(8,128)(2,1)}), bf16[32,32,256]{2,1,0:T(8,128)(2,1)S(1)}, u32[]{:S(2)}, u32[]{:S(2)}) %all-to-all-start.2) | async-done | bytes 524320 | tf_op jit(solution)/shard_map/weight_gather/all_to_all | solution.py:25
  80.7 1.5 broadcast_in_dim.146
  82.2 3.7 %all-to-all-start.3 = ((bf16[16,136,512]{2,1,0:T(8,128)(2,1)}), bf16[16,136,512]{2,1,0:T(8,128)(2,1)S(1)}, u32[]{:S(2)}, u32[]{:S(2)}) async-start(bf16[16,136,512]{2,1,0:T(8,128)(2,1)} %broadcast_in_dim.146), calls=%async_computation.3 | async-start | bytes 4456448 | tf_op jit(solution)/shard_map/project_gather/all_to_all | solution.py:25
  85.9 1.9 collective-permute-start.2
  88.0 13.0 %collective-permute-done.2 = bf16[32,32,256]{2,1,0:T(8,128)(2,1)} collective-permute-done((bf16[32,32,256]{2,1,0:T(8,128)(2,1)S(1)}, bf16[32,32,256]{2,1,0:T(8,128)(2,1)}, u32[]{:S(2)}, u32[]{:S(2)}) %collective-permute-start.2) | collective-permute-done | bytes 524320 | tf_op jit(solution)/shard_map/project_gather/ppermute | solution.py:261
  101.0 1.1 broadcast_select_fusion.3
  102.1 1.1 pad_maximum_fusion
  103.2 1.5 copy.9
  104.7 7.6 %collective-permute-start.3 = (bf16[256,2048]{1,0:T(8,128)(2,1)S(1)}, bf16[256,2048]{1,0:T(8,128)(2,1)}, u32[]{:S(2)}, u32[]{:S(2)}) collective-permute-start(bf16[256,2048]{1,0:T(8,128)(2,1)S(1)} %bitcast.43), channel_id=1, source_target_pairs={{1,2},{3,4},{5,6},{7,8},{9,10},{11,12},{13,14},{15,0},{2,1},{4,3},... | collective-permute-start | bytes 3145736 | tf_op jit(solution)/shard_map/project_gather/ppermute | solution.py:266
  112.2 8.4 %all-to-all-done.3.got_ref = bf16[16,136,512]{2,1,0:T(8,128)(2,1)S(1)} async-done(((bf16[16,136,512]{2,1,0:T(8,128)(2,1)}), bf16[16,136,512]{2,1,0:T(8,128)(2,1)S(1)}, u32[]{:S(2)}, u32[]{:S(2)}) %all-to-all-start.3) | async-done | bytes 2228256 | tf_op jit(solution)/shard_map/project_gather/all_to_all | solution.py:25
  120.7 0.7 multiply_reduce_fusion
  121.4 0.6 fusion
  122.0 0.3 multiply_reduce_fusion.1
  122.5 0.4 convolution_convert_fusion
  123.0 11.6 %collective-permute-done.3.other_ref = bf16[256,2048]{1,0:T(8,128)(2,1)} collective-permute-done((bf16[256,2048]{1,0:T(8,128)(2,1)S(1)}, bf16[256,2048]{1,0:T(8,128)(2,1)}, u32[]{:S(2)}, u32[]{:S(2)}) %collective-permute-start.3) | collective-permute-done | bytes 1048608 | tf_op jit(solution)/shard_map/project_gather/ppermute | solution.py:266
  134.5 3.8 %collective-permute-start.4 = (bf16[2048,128]{1,0:T(8,128)(2,1)S(1)}, bf16[2048,128]{1,0:T(8,128)(2,1)S(1)}, u32[]{:S(2)}, u32[]{:S(2)}) collective-permute-start(bf16[2048,128]{1,0:T(8,128)(2,1)S(1)} %convolution_convert_fusion), channel_id=1, source_target_pairs={{0,16},{16,0},{1,17},{17,1},{2,18},{18,2},{3,19},{19,3},{4,20},{20... | collective-permute-start | bytes 1572872 | tf_op jit(solution)/shard_map/gram_core/ppermute | solution.py:215
  138.4 0.4 fusion.13
  138.9 1.0 collective-permute-done.4
  140.0 16.8 %all_to_all.46 = bf16[4,520,128]{2,1,0:T(8,128)(2,1)S(1)} all-to-all(bf16[4,520,128]{2,1,0:T(8,128)(2,1)S(1)} %pad_maximum_fusion.1), channel_id=1, replica_groups=mesh['y'=4,'x'=4,'core'=2,'z1'=4,'z0'=4] {'z0'}, dimensions={0} | all-to-all | bytes 1064960 | tf_op jit(solution)/shard_map/gram_reduce/all_to_all | solution.py:25
  157.1 21.6 %all_to_all.47 = bf16[4,136,128]{2,1,0:T(8,128)(2,1)S(1)} all-to-all(bf16[4,136,128]{2,1,0:T(8,128)(2,1)S(1)} %pad_maximum_fusion.3), channel_id=1, replica_groups=mesh['y'=4,'x'=4,'core'=2,'z1'=4,'z0'=4] {'z1'}, dimensions={0} | all-to-all | bytes 278528 | tf_op jit(solution)/shard_map/gram_reduce/all_to_all | solution.py:25
  178.8 15.4 %all_to_all.48 = bf16[4,128,128]{2,1,0:T(8,128)(2,1)S(1)} all-to-all(bf16[4,128,128]{2,1,0:T(8,128)(2,1)S(1)} %broadcast_in_dim.149), channel_id=1, replica_groups=mesh['y'=4,'x'=4,'core'=2,'z1'=4,'z0'=4] {'z1'}, dimensions={0} | all-to-all | bytes 262144 | tf_op jit(solution)/shard_map/gram_gather/all_to_all | solution.py:25
  194.2 11.8 %all_to_all.49 = bf16[4,4,128,128]{3,2,1,0:T(8,128)(2,1)S(1)} all-to-all(bf16[4,4,128,128]{3,2,1,0:T(8,128)(2,1)S(1)} %broadcast_in_dim.150), channel_id=1, replica_groups=mesh['y'=4,'x'=4,'core'=2,'z1'=4,'z0'=4] {'z0'}, dimensions={0} | all-to-all | bytes 1048576 | tf_op jit(solution)/shard_map/gram_gather/all_to_all | solution.py:25
  206.1 8.5 %collective-permute-start.5 = (bf16[2048,128]{1,0:T(8,128)(2,1)S(1)}, bf16[2048,128]{1,0:T(8,128)(2,1)S(1)}, u32[]{:S(2)}, u32[]{:S(2)}) collective-permute-start(bf16[2048,128]{1,0:T(8,128)(2,1)S(1)} %bitcast.52), channel_id=1, source_target_pairs={{0,16},{16,0},{1,17},{17,1},{2,18},{18,2},{3,19},{19,3},{4,20},{20... | collective-permute-start | bytes 1572872 | tf_op jit(solution)/shard_map/gram_gather/ppermute | solution.py:215
  214.6 0.3 fusion.27
  214.9 0.4 convolution_add_fusion
  215.3 0.8 collective-permute-done.5
  216.1 0.3 fusion.2
  216.4 0.3 fusion.4
  216.8 0.4 select_convert_fusion.1
  217.4 35.3 %all_to_all.50.back_ref = bf16[16,136,512]{2,1,0:T(8,128)(2,1)S(1)} all-to-all(bf16[16,136,512]{2,1,0:T(8,128)(2,1)S(1)} %broadcast_in_dim.154), channel_id=1, replica_groups=mesh['y'=4,'x'=4,'core'=2,'z1'=4,'z0'=4] {'y','x'}, dimensions={0} | all-to-all | bytes 4456448 | tf_op jit(solution)/shard_map/back_gather/all_to_all | solution.py:25
  252.8 2.4 grad.1.grad_ref
  255.2 3.4 %collective-permute-start.6 = (bf16[2064,512]{1,0:T(8,128)(2,1)S(1)}, bf16[2064,512]{1,0:T(8,128)(2,1)S(1)}, u32[]{:S(2)}, u32[]{:S(2)}) collective-permute-start(bf16[2064,512]{1,0:T(8,128)(2,1)S(1)} %grad.1.grad_ref), channel_id=1, source_target_pairs={{0,16},{16,0},{1,17},{17,1},{2,18},{18,2},{3,19},{19,3},{4,20},{20... | collective-permute-start | bytes 6340616 | tf_op jit(solution)/shard_map/grad_swap/ppermute | solution.py:215
  258.6 2.0 own_half.1.mine_ref
  260.6 1.8 collective-permute-done.6.grad_ref
  262.4 2.9 %other_half.1 = (f32[256,512]{1,0:T(8,128)}, f32[1]{0:T(128)}) custom-call(s32[3]{0:T(128)S(1)} %pad_add_fusion.place_ref, bf16[256,2048]{1,0:T(8,128)(2,1)S(1)} %bitcast.45, bf16[256,2048]{1,0:T(8,128)(2,1)} %collective-permute-done.3.other_ref, bf16[2064,512]{1,0:T(8,128)(2,1)S(1)} %collective-permute-done.6.grad_ref, f32[256,256]{1,0:T(8,128)S(1)} %own_half.1.mine_ref, ...), custom_call_target="tpu_custom_call" | custom-call | tf_op jit(solution)/shard_map/weight_grad/other_half/pallas_call | solution.py:348
  (44 shorter events, 1.6 us)
Async XLA Ops:
  2.7 14.9 %all-to-all-start = ((bf16[4,256,512]{2,1,0:T(8,128)(2,1)}), bf16[4,256,512]{2,1,0:T(8,128)(2,1)}, u32[]{:S(2)}, u32[]{:S(2)}) async-start(bf16[4,256,512]{2,1,0:T(8,128)(2,1)} %broadcast_in_dim.139), calls=%async_computation | async-start | bytes 2097152 | tf_op jit(solution)/shard_map/weight_gather/all_to_all | solution.py:74
  12.2 1.0 copy-start
  19.2 30.9 %copy-start.1 = (bf16[128,4096]{1,0:T(8,128)(2,1)S(1)}, bf16[128,4096]{1,0:T(8,128)(2,1)}, u32[]{:S(2)}) copy-start(bf16[128,4096]{1,0:T(8,128)(2,1)} %copy-done) | copy-start | bytes 3145732
  50.1 11.0 %collective-permute-start = (bf16[128,4096]{1,0:T(8,128)(2,1)S(1)}, bf16[128,4096]{1,0:T(8,128)(2,1)S(1)}, u32[]{:S(2)}, u32[]{:S(2)}) collective-permute-start(bf16[128,4096]{1,0:T(8,128)(2,1)S(1)} %copy-done.1), channel_id=1, source_target_pairs={{0,16},{16,0},{1,17},{17,1},{2,18},{18,2},{3,19},{19,3},{4,20},{20... | collective-permute-start | bytes 3145736 | tf_op jit(solution)/shard_map/weight_gather/ppermute | solution.py:215
  62.8 6.0 %collective-permute-start.1 = (f32[128,512]{1,0:T(8,128)S(1)}, f32[128,512]{1,0:T(8,128)S(1)}, u32[]{:S(2)}, u32[]{:S(2)}) collective-permute-start(f32[128,512]{1,0:T(8,128)S(1)} %get-tuple-element.40), channel_id=1, source_target_pairs={{0,16},{16,0},{1,17},{17,1},{2,18},{18,2},{3,19},{19,3},{4,20},{20... | collective-permute-start | bytes 786440 | tf_op jit(solution)/shard_map/project/ppermute | solution.py:215
  65.2 15.4 %all-to-all-start.2 = ((bf16[32,32,256]{2,1,0:T(8,128)(2,1)}), bf16[32,32,256]{2,1,0:T(8,128)(2,1)S(1)}, u32[]{:S(2)}, u32[]{:S(2)}) async-start(bf16[32,32,256]{2,1,0:T(8,128)(2,1)} %get-tuple-element.41), calls=%async_computation.2 | async-start | bytes 1048576 | tf_op jit(solution)/shard_map/weight_gather/all_to_all | solution.py:25
  82.2 38.4 %all-to-all-start.3 = ((bf16[16,136,512]{2,1,0:T(8,128)(2,1)}), bf16[16,136,512]{2,1,0:T(8,128)(2,1)S(1)}, u32[]{:S(2)}, u32[]{:S(2)}) async-start(bf16[16,136,512]{2,1,0:T(8,128)(2,1)} %broadcast_in_dim.146), calls=%async_computation.3 | async-start | bytes 4456448 | tf_op jit(solution)/shard_map/project_gather/all_to_all | solution.py:25
  85.9 15.1 %collective-permute-start.2 = (bf16[32,32,256]{2,1,0:T(8,128)(2,1)S(1)}, bf16[32,32,256]{2,1,0:T(8,128)(2,1)}, u32[]{:S(2)}, u32[]{:S(2)}) collective-permute-start(bf16[32,32,256]{2,1,0:T(8,128)(2,1)S(1)} %all-to-all-done.2), channel_id=1, source_target_pairs={{0,1},{1,0},{2,3},{3,2},{4,5},{5,4},{6,7},{7,6},{8,9},{9,8},{10,11... | collective-permute-start | bytes 1572872 | tf_op jit(solution)/shard_map/project_gather/ppermute | solution.py:261
  104.7 29.8 %collective-permute-start.3 = (bf16[256,2048]{1,0:T(8,128)(2,1)S(1)}, bf16[256,2048]{1,0:T(8,128)(2,1)}, u32[]{:S(2)}, u32[]{:S(2)}) collective-permute-start(bf16[256,2048]{1,0:T(8,128)(2,1)S(1)} %bitcast.43), channel_id=1, source_target_pairs={{1,2},{3,4},{5,6},{7,8},{9,10},{11,12},{13,14},{15,0},{2,1},{4,3},... | collective-permute-start | bytes 3145736 | tf_op jit(solution)/shard_map/project_gather/ppermute | solution.py:266
  134.5 5.4 %collective-permute-start.4 = (bf16[2048,128]{1,0:T(8,128)(2,1)S(1)}, bf16[2048,128]{1,0:T(8,128)(2,1)S(1)}, u32[]{:S(2)}, u32[]{:S(2)}) collective-permute-start(bf16[2048,128]{1,0:T(8,128)(2,1)S(1)} %convolution_convert_fusion), channel_id=1, source_target_pairs={{0,16},{16,0},{1,17},{17,1},{2,18},{18,2},{3,19},{19,3},{4,20},{20... | collective-permute-start | bytes 1572872 | tf_op jit(solution)/shard_map/gram_core/ppermute | solution.py:215
  206.1 10.0 %collective-permute-start.5 = (bf16[2048,128]{1,0:T(8,128)(2,1)S(1)}, bf16[2048,128]{1,0:T(8,128)(2,1)S(1)}, u32[]{:S(2)}, u32[]{:S(2)}) collective-permute-start(bf16[2048,128]{1,0:T(8,128)(2,1)S(1)} %bitcast.52), channel_id=1, source_target_pairs={{0,16},{16,0},{1,17},{17,1},{2,18},{18,2},{3,19},{19,3},{4,20},{20... | collective-permute-start | bytes 1572872 | tf_op jit(solution)/shard_map/gram_gather/ppermute | solution.py:215
  255.2 7.2 %collective-permute-start.6 = (bf16[2064,512]{1,0:T(8,128)(2,1)S(1)}, bf16[2064,512]{1,0:T(8,128)(2,1)S(1)}, u32[]{:S(2)}, u32[]{:S(2)}) collective-permute-start(bf16[2064,512]{1,0:T(8,128)(2,1)S(1)} %grad.1.grad_ref), channel_id=1, source_target_pairs={{0,16},{16,0},{1,17},{17,1},{2,18},{18,2},{3,19},{19,3},{4,20},{20... | collective-permute-start | bytes 6340616 | tf_op jit(solution)/shard_map/grad_swap/ppermute | solution.py:215
